TPU v7x, 256 devices: a whole 4x4x8 slice. The times are simulated.
256 devices in a mesh: inst: 16 (over y_lo, z), blk: 16 (over y_hi, x, core).
Axes of the slice: x: 4, y: 4 (y_hi: 2, y_lo: 2; y = y_hi * 2 + y_lo), z: 8, core: 2. Of those that a mesh axis runs over, the one named last changes fastest.
Arguments:
- state: float32 [16, 5, 32, 128, 128], P('inst', None, 'blk'), may hold values from -6 to 6
- row_jacobian: float32 [5, 5], replicated, may hold values from -2.5 to 2.5
- cell_jacobian: float32 [5, 5], replicated, may hold values from -2.5 to 2.5
- viscosity: float32 [32, 128, 128], P('blk'), may hold values from 0.05 to 1
- local_step: float32 [32, 128, 128], P('blk'), may hold values from 0.02 to 0.1
- live_rows: int32 [32], replicated, may hold values from 1 to 128, 3072 in all
- partner: int32 [64], replicated, may hold values from 0 to 63, as said below
Outputs:
- new_state: float32 [16, 5, 32, 128, 128], P('inst', None, 'blk')
- final_residual: float32 [16, 5, 32, 128, 128], P('inst', None, 'blk')
Inputs may be any that keep to these rules, and one draw needn't show every extreme that they name: partner pairs the faces: partner[partner[f]] = f and partner[f] differs from f.
All inputs are finite; a program needn't handle non-finite values.
Results may differ from a plain program's by a relative error of at most 0.000058.
Values sent between devices are 32-bit elements; how exact they have to be, the bound alone decides.
No kernel may reach another device: no remote copies, remote signals or barrier semaphores. Data moves between devices by JAX's collectives and lax.ppermute only.
A program may use at most 64 MiB of HBM per device.

v0:
```python
import jax
import jax.numpy as jnp
from jax import lax
from jax.sharding import PartitionSpec as P

precise = lax.Precision.HIGHEST


def passed_along(value, axis, steps):
    count = lax.axis_size(axis)
    pairs = [(source, (source + steps) % count) for source in range(count)]
    return lax.ppermute(value, axis, pairs)


def spectral_matrix(count):
    numbers = jnp.arange(count, dtype=jnp.int32)
    offset = (numbers[:, None] - numbers[None, :]) % count
    angle = jnp.pi * offset.astype(jnp.float32) / count
    parity = 1.0 - 2.0 * (offset % 2).astype(jnp.float32)
    sine = jnp.where(offset == 0, 1.0, jnp.sin(angle))
    return jnp.where(offset == 0, 0.0, 0.5 * parity * jnp.cos(angle) / sine)


def time_term(state):
    count = lax.axis_size("inst")
    matrix = spectral_matrix(count)
    weights = matrix[:, 0]

    def advance(turn, paired):
        running, moving = paired
        moving = passed_along(moving, "inst", 1)
        return (running + weights[turn] * moving, moving)

    return lax.fori_loop(1, count, advance, (jnp.zeros_like(state), state))[0]


def evaluate(state, row_jacobian, cell_jacobian, viscosity, local_live, local_partner):
    instances, variables, blocks, height, width = state.shape
    row_index = jnp.arange(height, dtype=jnp.int32)
    last_mask = (row_index[None, :] == (local_live - 1)[:, None])[:, :, None]
    upper = jnp.sum(jnp.where(last_mask, state, 0.0), axis=3)
    lower = state[:, :, :, 0, :]
    face_rows = jnp.stack([lower, upper], axis=3).reshape(instances, variables, 2 * blocks, width)
    gathered = lax.all_gather(face_rows, "blk", axis=2, tiled=True)
    ghosts = gathered[:, :, local_partner, :].reshape(instances, variables, blocks, 2, width)
    previous = jnp.concatenate([ghosts[:, :, :, 0:1, :], state[:, :, :, :-1, :]], axis=3)
    shifted = jnp.concatenate(
        [state[:, :, :, 1:, :], jnp.zeros_like(state[:, :, :, :1, :])], axis=3
    )
    edge_mask = (row_index[None, :] + 1 == local_live[:, None])[:, :, None]
    following = jnp.where(edge_mask, ghosts[:, :, :, 1:2, :], shifted)
    east = jnp.roll(state, -1, axis=4)
    west = jnp.roll(state, 1, axis=4)
    spectral = time_term(state)
    convect = 0.5 * jnp.einsum(
        "uv,tvbrc->tubrc", row_jacobian, following - previous, precision=precise
    )
    convect = convect + 0.5 * jnp.einsum(
        "uv,tvbrc->tubrc", cell_jacobian, east - west, precision=precise
    )
    damping = (0.25 + viscosity) * (
        following - 2.0 * state + previous + (east - 2.0 * state + west)
    )
    live_mask = (row_index[None, :] < local_live[:, None])[:, :, None]
    return jnp.where(live_mask, spectral + convect - damping, 0.0)


def per_device(state, row_jacobian, cell_jacobian, viscosity, local_step, live_rows, partner):
    blocks = state.shape[2]
    first_block = lax.axis_index("blk") * blocks
    local_live = lax.dynamic_slice_in_dim(live_rows, first_block, blocks)
    local_partner = lax.dynamic_slice_in_dim(partner, 2 * first_block, 2 * blocks)
    first = evaluate(state, row_jacobian, cell_jacobian, viscosity, local_live, local_partner)
    half_state = state - 0.5 * local_step * first
    final_residual = evaluate(
        half_state, row_jacobian, cell_jacobian, viscosity, local_live, local_partner
    )
    return (state - local_step * final_residual, final_residual)


def solution(mesh):
    return jax.shard_map(
        per_device,
        mesh=mesh,
        in_specs=(
            P("inst", None, "blk", None, None),
            P(),
            P(),
            P("blk", None, None),
            P("blk", None, None),
            P(),
            P(),
        ),
        out_specs=(P("inst", None, "blk", None, None), P("inst", None, "blk", None, None)),
        check_vma=False,
    )
```

profile of v0, /device:TPU:6, one launch (start us, length us, event | category | flops | bytes accessed | tf_op | source)
XLA Modules:
  0.0 627.5 jit_solution(11439536145640802910)
XLA Ops:
  5.5 263.7 %while.36 = (s32[]{:T(128)}, f32[1,5,2,128,128]{4,3,2,1,0:T(8,128)S(1)}, f32[1,5,2,128,128]{4,3,2,1,0:T(8,128)S(1)}, f32[16]{0:T(128)S(1)}, s32[]{:T(128)}, /*index=5*/s32[]{:T(128)}, s32[]{:T(128)}) while((s32[]{:T(128)}, f32[1,5,2,128,128]{4,3,2,1,0:T(8,128)S(1)}, f32[1,5,2,128,128]{4,3,2,1,0:T(8,128)S(1)}, f32[16]{0:T(128)S(1)}, ...), condition=%wide.region_1.2_spmd.clone, body=%wide.region_0.1_spmd.clone.sunk | while | flops 491526 | bytes 5898425 | solution.py:34
  8.0 19.1 %collective-permute-done = f32[1,5,2,128,128]{4,3,2,1,0:T(8,128)S(1)} collective-permute-done((f32[1,5,2,128,128]{4,3,2,1,0:T(8,128)S(1)}, f32[1,5,2,128,128]{4,3,2,1,0:T(8,128)S(1)}, u32[]{:S(2)}, u32[]{:S(2)}) %collective-permute-start) | collective-permute-done | bytes 655392 | tf_op jit(solution)/shard_map/while/body/eval_jaxpr/ppermute | solution.py:12
  28.6 17.4 %collective-permute-done = f32[1,5,2,128,128]{4,3,2,1,0:T(8,128)S(1)} collective-permute-done((f32[1,5,2,128,128]{4,3,2,1,0:T(8,128)S(1)}, f32[1,5,2,128,128]{4,3,2,1,0:T(8,128)S(1)}, u32[]{:S(2)}, u32[]{:S(2)}) %collective-permute-start) | collective-permute-done | bytes 655392 | tf_op jit(solution)/shard_map/while/body/eval_jaxpr/ppermute | solution.py:12
  47.6 16.5 %collective-permute-done = f32[1,5,2,128,128]{4,3,2,1,0:T(8,128)S(1)} collective-permute-done((f32[1,5,2,128,128]{4,3,2,1,0:T(8,128)S(1)}, f32[1,5,2,128,128]{4,3,2,1,0:T(8,128)S(1)}, u32[]{:S(2)}, u32[]{:S(2)}) %collective-permute-start) | collective-permute-done | bytes 655392 | tf_op jit(solution)/shard_map/while/body/eval_jaxpr/ppermute | solution.py:12
  65.6 15.6 %collective-permute-done = f32[1,5,2,128,128]{4,3,2,1,0:T(8,128)S(1)} collective-permute-done((f32[1,5,2,128,128]{4,3,2,1,0:T(8,128)S(1)}, f32[1,5,2,128,128]{4,3,2,1,0:T(8,128)S(1)}, u32[]{:S(2)}, u32[]{:S(2)}) %collective-permute-start) | collective-permute-done | bytes 655392 | tf_op jit(solution)/shard_map/while/body/eval_jaxpr/ppermute | solution.py:12
  144.3 14.8 %collective-permute-done = f32[1,5,2,128,128]{4,3,2,1,0:T(8,128)S(1)} collective-permute-done((f32[1,5,2,128,128]{4,3,2,1,0:T(8,128)S(1)}, f32[1,5,2,128,128]{4,3,2,1,0:T(8,128)S(1)}, u32[]{:S(2)}, u32[]{:S(2)}) %collective-permute-start) | collective-permute-done | bytes 655392 | tf_op jit(solution)/shard_map/while/body/eval_jaxpr/ppermute | solution.py:12
  160.6 15.9 %collective-permute-done = f32[1,5,2,128,128]{4,3,2,1,0:T(8,128)S(1)} collective-permute-done((f32[1,5,2,128,128]{4,3,2,1,0:T(8,128)S(1)}, f32[1,5,2,128,128]{4,3,2,1,0:T(8,128)S(1)}, u32[]{:S(2)}, u32[]{:S(2)}) %collective-permute-start) | collective-permute-done | bytes 655392 | tf_op jit(solution)/shard_map/while/body/eval_jaxpr/ppermute | solution.py:12
  178.0 17.0 %collective-permute-done = f32[1,5,2,128,128]{4,3,2,1,0:T(8,128)S(1)} collective-permute-done((f32[1,5,2,128,128]{4,3,2,1,0:T(8,128)S(1)}, f32[1,5,2,128,128]{4,3,2,1,0:T(8,128)S(1)}, u32[]{:S(2)}, u32[]{:S(2)}) %collective-permute-start) | collective-permute-done | bytes 655392 | tf_op jit(solution)/shard_map/while/body/eval_jaxpr/ppermute | solution.py:12
  196.5 18.2 %collective-permute-done = f32[1,5,2,128,128]{4,3,2,1,0:T(8,128)S(1)} collective-permute-done((f32[1,5,2,128,128]{4,3,2,1,0:T(8,128)S(1)}, f32[1,5,2,128,128]{4,3,2,1,0:T(8,128)S(1)}, u32[]{:S(2)}, u32[]{:S(2)}) %collective-permute-start) | collective-permute-done | bytes 655392 | tf_op jit(solution)/shard_map/while/body/eval_jaxpr/ppermute | solution.py:12
  216.2 19.0 %collective-permute-done = f32[1,5,2,128,128]{4,3,2,1,0:T(8,128)S(1)} collective-permute-done((f32[1,5,2,128,128]{4,3,2,1,0:T(8,128)S(1)}, f32[1,5,2,128,128]{4,3,2,1,0:T(8,128)S(1)}, u32[]{:S(2)}, u32[]{:S(2)}) %collective-permute-start) | collective-permute-done | bytes 655392 | tf_op jit(solution)/shard_map/while/body/eval_jaxpr/ppermute | solution.py:12
  236.6 18.1 %collective-permute-done = f32[1,5,2,128,128]{4,3,2,1,0:T(8,128)S(1)} collective-permute-done((f32[1,5,2,128,128]{4,3,2,1,0:T(8,128)S(1)}, f32[1,5,2,128,128]{4,3,2,1,0:T(8,128)S(1)}, u32[]{:S(2)}, u32[]{:S(2)}) %collective-permute-start) | collective-permute-done | bytes 655392 | tf_op jit(solution)/shard_map/while/body/eval_jaxpr/ppermute | solution.py:12
  271.3 18.7 %all_gather.6 = f32[1,5,64,128]{3,0,1,2:T(1,128)S(1)} all-gather(f32[1,5,4,128]{3,0,1,2:T(1,128)S(1)} %reshape.100), channel_id=1, replica_groups=mesh['inst'=16,'blk'=16] {'blk'}, dimensions={2}, use_global_device_ids=true | all-gather | bytes 174080 | tf_op jit(solution)/shard_map/all_gather | solution.py:44
  310.5 22.2 %all_gather.7 = f32[1,5,64,128]{3,0,1,2:T(1,128)S(1)} all-gather(f32[1,5,4,128]{3,0,1,2:T(1,128)S(1)} %copy.129), channel_id=1, replica_groups=mesh['inst'=16,'blk'=16] {'blk'}, dimensions={2}, use_global_device_ids=true | all-gather | bytes 174080 | tf_op jit(solution)/shard_map/all_gather | solution.py:44
  334.4 272.5 %while.37 = (s32[]{:T(128)}, f32[1,5,2,128,128]{4,3,2,1,0:T(8,128)S(1)}, f32[1,5,2,128,128]{4,3,2,1,0:T(8,128)}, f32[16]{0:T(128)S(1)}, s32[]{:T(128)}, /*index=5*/s32[]{:T(128)}, s32[]{:T(128)}) while((s32[]{:T(128)}, f32[1,5,2,128,128]{4,3,2,1,0:T(8,128)S(1)}, f32[1,5,2,128,128]{4,3,2,1,0:T(8,128)}, f32[16]{0:T(128)S(1)}, ...), condition=%wide.region_4.5_spmd.clone, body=%wide.region_3.4_spmd.clone.sunk | while | flops 491526 | bytes 5898425 | solution.py:34
  335.0 18.7 %collective-permute-done.1 = f32[1,5,2,128,128]{4,3,2,1,0:T(8,128)S(1)} collective-permute-done((f32[1,5,2,128,128]{4,3,2,1,0:T(8,128)}, f32[1,5,2,128,128]{4,3,2,1,0:T(8,128)S(1)}, u32[]{:S(2)}, u32[]{:S(2)}) %collective-permute-start.1) | collective-permute-done | bytes 655392 | tf_op jit(solution)/shard_map/while/body/eval_jaxpr/ppermute | solution.py:12
  356.1 17.9 %collective-permute-done.1 = f32[1,5,2,128,128]{4,3,2,1,0:T(8,128)S(1)} collective-permute-done((f32[1,5,2,128,128]{4,3,2,1,0:T(8,128)}, f32[1,5,2,128,128]{4,3,2,1,0:T(8,128)S(1)}, u32[]{:S(2)}, u32[]{:S(2)}) %collective-permute-start.1) | collective-permute-done | bytes 655392 | tf_op jit(solution)/shard_map/while/body/eval_jaxpr/ppermute | solution.py:12
  376.4 17.0 %collective-permute-done.1 = f32[1,5,2,128,128]{4,3,2,1,0:T(8,128)S(1)} collective-permute-done((f32[1,5,2,128,128]{4,3,2,1,0:T(8,128)}, f32[1,5,2,128,128]{4,3,2,1,0:T(8,128)S(1)}, u32[]{:S(2)}, u32[]{:S(2)}) %collective-permute-start.1) | collective-permute-done | bytes 655392 | tf_op jit(solution)/shard_map/while/body/eval_jaxpr/ppermute | solution.py:12
  395.8 16.1 %collective-permute-done.1 = f32[1,5,2,128,128]{4,3,2,1,0:T(8,128)S(1)} collective-permute-done((f32[1,5,2,128,128]{4,3,2,1,0:T(8,128)}, f32[1,5,2,128,128]{4,3,2,1,0:T(8,128)S(1)}, u32[]{:S(2)}, u32[]{:S(2)}) %collective-permute-start.1) | collective-permute-done | bytes 655392 | tf_op jit(solution)/shard_map/while/body/eval_jaxpr/ppermute | solution.py:12
  414.2 15.1 %collective-permute-done.1 = f32[1,5,2,128,128]{4,3,2,1,0:T(8,128)S(1)} collective-permute-done((f32[1,5,2,128,128]{4,3,2,1,0:T(8,128)}, f32[1,5,2,128,128]{4,3,2,1,0:T(8,128)S(1)}, u32[]{:S(2)}, u32[]{:S(2)}) %collective-permute-start.1) | collective-permute-done | bytes 655392 | tf_op jit(solution)/shard_map/while/body/eval_jaxpr/ppermute | solution.py:12
  495.5 14.9 %collective-permute-done.1 = f32[1,5,2,128,128]{4,3,2,1,0:T(8,128)S(1)} collective-permute-done((f32[1,5,2,128,128]{4,3,2,1,0:T(8,128)}, f32[1,5,2,128,128]{4,3,2,1,0:T(8,128)S(1)}, u32[]{:S(2)}, u32[]{:S(2)}) %collective-permute-start.1) | collective-permute-done | bytes 655392 | tf_op jit(solution)/shard_map/while/body/eval_jaxpr/ppermute | solution.py:12
  512.8 16.0 %collective-permute-done.1 = f32[1,5,2,128,128]{4,3,2,1,0:T(8,128)S(1)} collective-permute-done((f32[1,5,2,128,128]{4,3,2,1,0:T(8,128)}, f32[1,5,2,128,128]{4,3,2,1,0:T(8,128)S(1)}, u32[]{:S(2)}, u32[]{:S(2)}) %collective-permute-start.1) | collective-permute-done | bytes 655392 | tf_op jit(solution)/shard_map/while/body/eval_jaxpr/ppermute | solution.py:12
  531.1 17.0 %collective-permute-done.1 = f32[1,5,2,128,128]{4,3,2,1,0:T(8,128)S(1)} collective-permute-done((f32[1,5,2,128,128]{4,3,2,1,0:T(8,128)}, f32[1,5,2,128,128]{4,3,2,1,0:T(8,128)S(1)}, u32[]{:S(2)}, u32[]{:S(2)}) %collective-permute-start.1) | collective-permute-done | bytes 655392 | tf_op jit(solution)/shard_map/while/body/eval_jaxpr/ppermute | solution.py:12
  550.6 18.2 %collective-permute-done.1 = f32[1,5,2,128,128]{4,3,2,1,0:T(8,128)S(1)} collective-permute-done((f32[1,5,2,128,128]{4,3,2,1,0:T(8,128)}, f32[1,5,2,128,128]{4,3,2,1,0:T(8,128)S(1)}, u32[]{:S(2)}, u32[]{:S(2)}) %collective-permute-start.1) | collective-permute-done | bytes 655392 | tf_op jit(solution)/shard_map/while/body/eval_jaxpr/ppermute | solution.py:12
  571.2 19.3 %collective-permute-done.1 = f32[1,5,2,128,128]{4,3,2,1,0:T(8,128)S(1)} collective-permute-done((f32[1,5,2,128,128]{4,3,2,1,0:T(8,128)}, f32[1,5,2,128,128]{4,3,2,1,0:T(8,128)S(1)}, u32[]{:S(2)}, u32[]{:S(2)}) %collective-permute-start.1) | collective-permute-done | bytes 655392 | tf_op jit(solution)/shard_map/while/body/eval_jaxpr/ppermute | solution.py:12
  (244 shorter events, 242.5 us)
Async XLA Ops:
  5.5 21.6 %collective-permute-start = (f32[1,5,2,128,128]{4,3,2,1,0:T(8,128)S(1)}, f32[1,5,2,128,128]{4,3,2,1,0:T(8,128)S(1)}, u32[]{:S(2)}, u32[]{:S(2)}) collective-permute-start(f32[1,5,2,128,128]{4,3,2,1,0:T(8,128)S(1)} %get-tuple-element.394), channel_id=1, source_target_pairs={{0,16},{16,32},{32,48},{48,64},{64,80},{80,96},{96,112},{112,128},... | collective-permute-start | bytes 1966088 | tf_op jit(solution)/shard_map/while/body/eval_jaxpr/ppermute | solution.py:12
  28.0 18.1 %collective-permute-start = (f32[1,5,2,128,128]{4,3,2,1,0:T(8,128)S(1)}, f32[1,5,2,128,128]{4,3,2,1,0:T(8,128)S(1)}, u32[]{:S(2)}, u32[]{:S(2)}) collective-permute-start(f32[1,5,2,128,128]{4,3,2,1,0:T(8,128)S(1)} %get-tuple-element.394), channel_id=1, source_target_pairs={{0,16},{16,32},{32,48},{48,64},{64,80},{80,96},{96,112},{112,128},... | collective-permute-start | bytes 1966088 | tf_op jit(solution)/shard_map/while/body/eval_jaxpr/ppermute | solution.py:12
  46.9 17.2 %collective-permute-start = (f32[1,5,2,128,128]{4,3,2,1,0:T(8,128)S(1)}, f32[1,5,2,128,128]{4,3,2,1,0:T(8,128)S(1)}, u32[]{:S(2)}, u32[]{:S(2)}) collective-permute-start(f32[1,5,2,128,128]{4,3,2,1,0:T(8,128)S(1)} %get-tuple-element.394), channel_id=1, source_target_pairs={{0,16},{16,32},{32,48},{48,64},{64,80},{80,96},{96,112},{112,128},... | collective-permute-start | bytes 1966088 | tf_op jit(solution)/shard_map/while/body/eval_jaxpr/ppermute | solution.py:12
  64.9 16.3 %collective-permute-start = (f32[1,5,2,128,128]{4,3,2,1,0:T(8,128)S(1)}, f32[1,5,2,128,128]{4,3,2,1,0:T(8,128)S(1)}, u32[]{:S(2)}, u32[]{:S(2)}) collective-permute-start(f32[1,5,2,128,128]{4,3,2,1,0:T(8,128)S(1)} %get-tuple-element.394), channel_id=1, source_target_pairs={{0,16},{16,32},{32,48},{48,64},{64,80},{80,96},{96,112},{112,128},... | collective-permute-start | bytes 1966088 | tf_op jit(solution)/shard_map/while/body/eval_jaxpr/ppermute | solution.py:12
  82.0 15.3 %collective-permute-start = (f32[1,5,2,128,128]{4,3,2,1,0:T(8,128)S(1)}, f32[1,5,2,128,128]{4,3,2,1,0:T(8,128)S(1)}, u32[]{:S(2)}, u32[]{:S(2)}) collective-permute-start(f32[1,5,2,128,128]{4,3,2,1,0:T(8,128)S(1)} %get-tuple-element.394), channel_id=1, source_target_pairs={{0,16},{16,32},{32,48},{48,64},{64,80},{80,96},{96,112},{112,128},... | collective-permute-start | bytes 1966088 | tf_op jit(solution)/shard_map/while/body/eval_jaxpr/ppermute | solution.py:12
  98.2 14.4 %collective-permute-start = (f32[1,5,2,128,128]{4,3,2,1,0:T(8,128)S(1)}, f32[1,5,2,128,128]{4,3,2,1,0:T(8,128)S(1)}, u32[]{:S(2)}, u32[]{:S(2)}) collective-permute-start(f32[1,5,2,128,128]{4,3,2,1,0:T(8,128)S(1)} %get-tuple-element.394), channel_id=1, source_target_pairs={{0,16},{16,32},{32,48},{48,64},{64,80},{80,96},{96,112},{112,128},... | collective-permute-start | bytes 1966088 | tf_op jit(solution)/shard_map/while/body/eval_jaxpr/ppermute | solution.py:12
  143.6 15.5 %collective-permute-start = (f32[1,5,2,128,128]{4,3,2,1,0:T(8,128)S(1)}, f32[1,5,2,128,128]{4,3,2,1,0:T(8,128)S(1)}, u32[]{:S(2)}, u32[]{:S(2)}) collective-permute-start(f32[1,5,2,128,128]{4,3,2,1,0:T(8,128)S(1)} %get-tuple-element.394), channel_id=1, source_target_pairs={{0,16},{16,32},{32,48},{48,64},{64,80},{80,96},{96,112},{112,128},... | collective-permute-start | bytes 1966088 | tf_op jit(solution)/shard_map/while/body/eval_jaxpr/ppermute | solution.py:12
  159.9 16.6 %collective-permute-start = (f32[1,5,2,128,128]{4,3,2,1,0:T(8,128)S(1)}, f32[1,5,2,128,128]{4,3,2,1,0:T(8,128)S(1)}, u32[]{:S(2)}, u32[]{:S(2)}) collective-permute-start(f32[1,5,2,128,128]{4,3,2,1,0:T(8,128)S(1)} %get-tuple-element.394), channel_id=1, source_target_pairs={{0,16},{16,32},{32,48},{48,64},{64,80},{80,96},{96,112},{112,128},... | collective-permute-start | bytes 1966088 | tf_op jit(solution)/shard_map/while/body/eval_jaxpr/ppermute | solution.py:12
  177.4 17.7 %collective-permute-start = (f32[1,5,2,128,128]{4,3,2,1,0:T(8,128)S(1)}, f32[1,5,2,128,128]{4,3,2,1,0:T(8,128)S(1)}, u32[]{:S(2)}, u32[]{:S(2)}) collective-permute-start(f32[1,5,2,128,128]{4,3,2,1,0:T(8,128)S(1)} %get-tuple-element.394), channel_id=1, source_target_pairs={{0,16},{16,32},{32,48},{48,64},{64,80},{80,96},{96,112},{112,128},... | collective-permute-start | bytes 1966088 | tf_op jit(solution)/shard_map/while/body/eval_jaxpr/ppermute | solution.py:12
  195.9 18.8 %collective-permute-start = (f32[1,5,2,128,128]{4,3,2,1,0:T(8,128)S(1)}, f32[1,5,2,128,128]{4,3,2,1,0:T(8,128)S(1)}, u32[]{:S(2)}, u32[]{:S(2)}) collective-permute-start(f32[1,5,2,128,128]{4,3,2,1,0:T(8,128)S(1)} %get-tuple-element.394), channel_id=1, source_target_pairs={{0,16},{16,32},{32,48},{48,64},{64,80},{80,96},{96,112},{112,128},... | collective-permute-start | bytes 1966088 | tf_op jit(solution)/shard_map/while/body/eval_jaxpr/ppermute | solution.py:12
  215.5 19.6 %collective-permute-start = (f32[1,5,2,128,128]{4,3,2,1,0:T(8,128)S(1)}, f32[1,5,2,128,128]{4,3,2,1,0:T(8,128)S(1)}, u32[]{:S(2)}, u32[]{:S(2)}) collective-permute-start(f32[1,5,2,128,128]{4,3,2,1,0:T(8,128)S(1)} %get-tuple-element.394), channel_id=1, source_target_pairs={{0,16},{16,32},{32,48},{48,64},{64,80},{80,96},{96,112},{112,128},... | collective-permute-start | bytes 1966088 | tf_op jit(solution)/shard_map/while/body/eval_jaxpr/ppermute | solution.py:12
  236.0 18.8 %collective-permute-start = (f32[1,5,2,128,128]{4,3,2,1,0:T(8,128)S(1)}, f32[1,5,2,128,128]{4,3,2,1,0:T(8,128)S(1)}, u32[]{:S(2)}, u32[]{:S(2)}) collective-permute-start(f32[1,5,2,128,128]{4,3,2,1,0:T(8,128)S(1)} %get-tuple-element.394), channel_id=1, source_target_pairs={{0,16},{16,32},{32,48},{48,64},{64,80},{80,96},{96,112},{112,128},... | collective-permute-start | bytes 1966088 | tf_op jit(solution)/shard_map/while/body/eval_jaxpr/ppermute | solution.py:12
  334.4 19.3 %collective-permute-start.1 = (f32[1,5,2,128,128]{4,3,2,1,0:T(8,128)}, f32[1,5,2,128,128]{4,3,2,1,0:T(8,128)S(1)}, u32[]{:S(2)}, u32[]{:S(2)}) collective-permute-start(f32[1,5,2,128,128]{4,3,2,1,0:T(8,128)} %get-tuple-element.415), channel_id=1, source_target_pairs={{0,16},{16,32},{32,48},{48,64},{64,80},{80,96},{96,112},{112,128},... | collective-permute-start | bytes 1966088 | tf_op jit(solution)/shard_map/while/body/eval_jaxpr/ppermute | solution.py:12
  355.4 18.6 %collective-permute-start.1 = (f32[1,5,2,128,128]{4,3,2,1,0:T(8,128)}, f32[1,5,2,128,128]{4,3,2,1,0:T(8,128)S(1)}, u32[]{:S(2)}, u32[]{:S(2)}) collective-permute-start(f32[1,5,2,128,128]{4,3,2,1,0:T(8,128)} %get-tuple-element.415), channel_id=1, source_target_pairs={{0,16},{16,32},{32,48},{48,64},{64,80},{80,96},{96,112},{112,128},... | collective-permute-start | bytes 1966088 | tf_op jit(solution)/shard_map/while/body/eval_jaxpr/ppermute | solution.py:12
  375.7 17.7 %collective-permute-start.1 = (f32[1,5,2,128,128]{4,3,2,1,0:T(8,128)}, f32[1,5,2,128,128]{4,3,2,1,0:T(8,128)S(1)}, u32[]{:S(2)}, u32[]{:S(2)}) collective-permute-start(f32[1,5,2,128,128]{4,3,2,1,0:T(8,128)} %get-tuple-element.415), channel_id=1, source_target_pairs={{0,16},{16,32},{32,48},{48,64},{64,80},{80,96},{96,112},{112,128},... | collective-permute-start | bytes 1966088 | tf_op jit(solution)/shard_map/while/body/eval_jaxpr/ppermute | solution.py:12
  395.1 16.7 %collective-permute-start.1 = (f32[1,5,2,128,128]{4,3,2,1,0:T(8,128)}, f32[1,5,2,128,128]{4,3,2,1,0:T(8,128)S(1)}, u32[]{:S(2)}, u32[]{:S(2)}) collective-permute-start(f32[1,5,2,128,128]{4,3,2,1,0:T(8,128)} %get-tuple-element.415), channel_id=1, source_target_pairs={{0,16},{16,32},{32,48},{48,64},{64,80},{80,96},{96,112},{112,128},... | collective-permute-start | bytes 1966088 | tf_op jit(solution)/shard_map/while/body/eval_jaxpr/ppermute | solution.py:12
  413.6 15.8 %collective-permute-start.1 = (f32[1,5,2,128,128]{4,3,2,1,0:T(8,128)}, f32[1,5,2,128,128]{4,3,2,1,0:T(8,128)S(1)}, u32[]{:S(2)}, u32[]{:S(2)}) collective-permute-start(f32[1,5,2,128,128]{4,3,2,1,0:T(8,128)} %get-tuple-element.415), channel_id=1, source_target_pairs={{0,16},{16,32},{32,48},{48,64},{64,80},{80,96},{96,112},{112,128},... | collective-permute-start | bytes 1966088 | tf_op jit(solution)/shard_map/while/body/eval_jaxpr/ppermute | solution.py:12
  431.1 14.9 %collective-permute-start.1 = (f32[1,5,2,128,128]{4,3,2,1,0:T(8,128)}, f32[1,5,2,128,128]{4,3,2,1,0:T(8,128)S(1)}, u32[]{:S(2)}, u32[]{:S(2)}) collective-permute-start(f32[1,5,2,128,128]{4,3,2,1,0:T(8,128)} %get-tuple-element.415), channel_id=1, source_target_pairs={{0,16},{16,32},{32,48},{48,64},{64,80},{80,96},{96,112},{112,128},... | collective-permute-start | bytes 1966088 | tf_op jit(solution)/shard_map/while/body/eval_jaxpr/ppermute | solution.py:12
  478.6 14.5 %collective-permute-start.1 = (f32[1,5,2,128,128]{4,3,2,1,0:T(8,128)}, f32[1,5,2,128,128]{4,3,2,1,0:T(8,128)S(1)}, u32[]{:S(2)}, u32[]{:S(2)}) collective-permute-start(f32[1,5,2,128,128]{4,3,2,1,0:T(8,128)} %get-tuple-element.415), channel_id=1, source_target_pairs={{0,16},{16,32},{32,48},{48,64},{64,80},{80,96},{96,112},{112,128},... | collective-permute-start | bytes 1966088 | tf_op jit(solution)/shard_map/while/body/eval_jaxpr/ppermute | solution.py:12
  494.8 15.6 %collective-permute-start.1 = (f32[1,5,2,128,128]{4,3,2,1,0:T(8,128)}, f32[1,5,2,128,128]{4,3,2,1,0:T(8,128)S(1)}, u32[]{:S(2)}, u32[]{:S(2)}) collective-permute-start(f32[1,5,2,128,128]{4,3,2,1,0:T(8,128)} %get-tuple-element.415), channel_id=1, source_target_pairs={{0,16},{16,32},{32,48},{48,64},{64,80},{80,96},{96,112},{112,128},... | collective-permute-start | bytes 1966088 | tf_op jit(solution)/shard_map/while/body/eval_jaxpr/ppermute | solution.py:12
  512.1 16.6 %collective-permute-start.1 = (f32[1,5,2,128,128]{4,3,2,1,0:T(8,128)}, f32[1,5,2,128,128]{4,3,2,1,0:T(8,128)S(1)}, u32[]{:S(2)}, u32[]{:S(2)}) collective-permute-start(f32[1,5,2,128,128]{4,3,2,1,0:T(8,128)} %get-tuple-element.415), channel_id=1, source_target_pairs={{0,16},{16,32},{32,48},{48,64},{64,80},{80,96},{96,112},{112,128},... | collective-permute-start | bytes 1966088 | tf_op jit(solution)/shard_map/while/body/eval_jaxpr/ppermute | solution.py:12
  530.5 17.7 %collective-permute-start.1 = (f32[1,5,2,128,128]{4,3,2,1,0:T(8,128)}, f32[1,5,2,128,128]{4,3,2,1,0:T(8,128)S(1)}, u32[]{:S(2)}, u32[]{:S(2)}) collective-permute-start(f32[1,5,2,128,128]{4,3,2,1,0:T(8,128)} %get-tuple-element.415), channel_id=1, source_target_pairs={{0,16},{16,32},{32,48},{48,64},{64,80},{80,96},{96,112},{112,128},... | collective-permute-start | bytes 1966088 | tf_op jit(solution)/shard_map/while/body/eval_jaxpr/ppermute | solution.py:12
  549.9 18.9 %collective-permute-start.1 = (f32[1,5,2,128,128]{4,3,2,1,0:T(8,128)}, f32[1,5,2,128,128]{4,3,2,1,0:T(8,128)S(1)}, u32[]{:S(2)}, u32[]{:S(2)}) collective-permute-start(f32[1,5,2,128,128]{4,3,2,1,0:T(8,128)} %get-tuple-element.415), channel_id=1, source_target_pairs={{0,16},{16,32},{32,48},{48,64},{64,80},{80,96},{96,112},{112,128},... | collective-permute-start | bytes 1966088 | tf_op jit(solution)/shard_map/while/body/eval_jaxpr/ppermute | solution.py:12
  570.5 20.0 %collective-permute-start.1 = (f32[1,5,2,128,128]{4,3,2,1,0:T(8,128)}, f32[1,5,2,128,128]{4,3,2,1,0:T(8,128)S(1)}, u32[]{:S(2)}, u32[]{:S(2)}) collective-permute-start(f32[1,5,2,128,128]{4,3,2,1,0:T(8,128)} %get-tuple-element.415), channel_id=1, source_target_pairs={{0,16},{16,32},{32,48},{48,64},{64,80},{80,96},{96,112},{112,128},... | collective-permute-start | bytes 1966088 | tf_op jit(solution)/shard_map/while/body/eval_jaxpr/ppermute | solution.py:12
  (41 other events, 1282.3 us)
where the time goes:
time: 632 us; the launch traced here: 627 us
  waiting for transfers between devices  476 us (75%)
  local copies, waits for them, and re-layouts  58.6 us (9%)
  blocking collectives  40.9 us (6%)
  other arithmetic  28.5 us (5%)
  matrix products  17.1 us (3%)
    ppermute x30, waiting for transfers between devices, passed_along(): return lax.ppermute(value, axis, pairs)  476 us
    all_gather x2, blocking collectives, evaluate(): gathered = lax.all_gather(face_rows, 'blk', axis=2, tiled=True)  40.9 us
    add x30, other arithmetic, advance(): return (running + weights[turn] * moving, moving)  24.5 us
    dynamic_slice x30, local copies, waits for them, and re-layouts, advance(): return (running + weights[turn] * moving, moving)  17.2 us
    while x30, local copies, waits for them, and re-layouts  13.2 us
  transfers between devices with their start and end apart: 30, of which 30 were waited for; matrix products, arithmetic and copies ran while one was open for 3% of the time, Pallas kernels for 0%

commit v1 on v0

v1 whole, which is shorter than its diff:
```python
import functools
import math

import jax
import jax.numpy as jnp
from jax import lax
from jax.experimental import pallas as pl
from jax.experimental.pallas import tpu as pltpu
from jax.sharding import PartitionSpec as P

VARS, BLOCKS, ROWS, CELLS, INST = 5, 2, 128, 128, 16
SLAB = 16
PER_BLOCK = ROWS // SLAB
MAIN = VARS * SLAB
PREV, NEXT, FACE = MAIN, MAIN + VARS, MAIN + 2 * VARS
SENT = 112
FACES = 2 * BLOCKS
VMEM = pl.BlockSpec(memory_space=pltpu.VMEM)
SMEM = pl.BlockSpec(memory_space=pltpu.SMEM)
PARAMS = pltpu.CompilerParams(vmem_limit_bytes=32 * 1024 * 1024)


def spectral(m):
    m = m % INST
    if m in (0, INST // 2):
        return 0.0
    return 0.5 * (-1.0) ** m * math.cos(math.pi * m / INST) / math.sin(math.pi * m / INST)


HALF = INST // 2
EVEN = [0.5 * (spectral(m) + spectral(m + HALF)) for m in range(HALF)]
ODD = [0.5 * (spectral(m) - spectral(m + HALF)) for m in range(HALF)]


def weighted(terms):
    total = None
    for weight, value in terms:
        term = weight * value
        total = term if total is None else total + term
    return total


def apply_even(p):
    return [
        weighted([(EVEN[m], p[(t - m) % HALF] - p[(t + m) % HALF]) for m in range(1, HALF // 2)])
        for t in range(HALF)
    ]


def apply_odd(q):
    def at(index):
        index %= INST
        return q[index] if index < HALF else -q[index - HALF]

    def pair(t, m):
        low, high = (t - m) % INST, (t + m) % INST
        first = q[low % HALF] if low < HALF else None
        second = q[high % HALF] if high < HALF else None
        a, b = q[low % HALF], q[high % HALF]
        if first is not None and second is not None:
            return a - b, 1.0
        if first is None and second is not None:
            return a + b, -1.0
        if first is not None:
            return a + b, 1.0
        return a - b, -1.0

    result = []
    for t in range(HALF):
        terms = []
        for m in range(1, HALF // 2):
            value, sign = pair(t, m)
            terms.append((sign * ODD[m], value))
        last = (t - HALF // 2) % INST
        terms.append((ODD[HALF // 2] if last < HALF else -ODD[HALF // 2], q[last % HALF]))
        result.append(weighted(terms))
    return result


def row_shifts(tile, before, after):
    rows = tile.shape[0]
    row = lax.broadcasted_iota(jnp.int32, tile.shape, 0)
    following = jnp.where(row == rows - 1, after, pltpu.roll(tile, rows - 1, 0))
    previous = jnp.where(row == 0, before, pltpu.roll(tile, 1, 0))
    return following, previous


def east_west(tile):
    return pltpu.roll(tile, CELLS - 1, 1), pltpu.roll(tile, 1, 1)


def pack_kernel(live_ref, state_ref, chunks_ref, faces_ref):
    first = lax.axis_index("blk") * BLOCKS
    for b in range(BLOCKS):
        last = live_ref[first + b] - 1
        for v in range(VARS):
            faces_ref[pl.ds((2 * b) * VARS + v, 1), :] = state_ref[0, v, b, 0:1, :]
            faces_ref[pl.ds((2 * b + 1) * VARS + v, 1), :] = state_ref[0, v, b, pl.ds(last, 1), :]
    faces = faces_ref[...]
    for b in range(BLOCKS):
        for j in range(PER_BLOCK):
            i = b * PER_BLOCK + j
            low = j * SLAB
            for v in range(VARS):
                chunks_ref[i, v * SLAB : (v + 1) * SLAB, :] = state_ref[0, v, b, low : low + SLAB, :]
                before, after = max(low - 1, 0), min(low + SLAB, ROWS - 1)
                chunks_ref[i, PREV + v : PREV + v + 1, :] = state_ref[0, v, b, before : before + 1, :]
                chunks_ref[i, NEXT + v : NEXT + v + 1, :] = state_ref[0, v, b, after : after + 1, :]
            chunks_ref[i, FACE : FACE + FACES * VARS, :] = faces
            chunks_ref[i, FACE + FACES * VARS : SENT, :] = jnp.zeros((SENT - FACE - FACES * VARS, CELLS), jnp.float32)


def ghost_place(partner_ref, face):
    me = lax.axis_index("blk")
    other = partner_ref[me * FACES + face]
    device, local = other // FACES, other % FACES
    core = (device % 2 + me % 2) % 2
    x = ((device // 2) % 4 - (me // 2) % 4 + 4) % 4
    y = (device // 8 + me // 8) % 2
    return (core * 4 + x) * 2 + y, local


def spatial_kernel(live_ref, partner_ref, row_ref, cell_ref, state_ref, visc_ref, step_ref, gathered_ref,
                   spatial_ref, faces_ref, half_ref):
    first = lax.axis_index("blk") * BLOCKS

    def stencil(tiles, befores, afters, mask_n, mask_p, damp):
        across, along, smooth = [], [], []
        for v in range(VARS):
            n, p = row_shifts(tiles[v], befores[v], afters[v])
            n, p = n * mask_n, p * mask_p
            e, w = east_west(tiles[v])
            across.append(n - p)
            along.append(e - w)
            smooth.append((n + p) + (e + w) - 4.0 * tiles[v])
        result = []
        for u in range(VARS):
            total = -damp * smooth[u]
            for v in range(VARS):
                total = total + (0.5 * row_ref[u, v]) * across[v] + (0.5 * cell_ref[u, v]) * along[v]
            result.append(total)
        return result

    def sweep(read, write, b, live):
        def step(j, carry):
            low = pl.multiple_of(j * SLAB, SLAB)
            before, after = jnp.maximum(low - 1, 0), jnp.minimum(low + SLAB, ROWS - 1)
            row = low + lax.broadcasted_iota(jnp.int32, (SLAB, CELLS), 0)
            mask_n = jnp.where(row + 1 < live, 1.0, 0.0)
            mask_p = jnp.where(row > 0, 1.0, 0.0)
            damp = 0.25 + visc_ref[b, pl.ds(low, SLAB), :]
            tiles = [read(v, b, pl.ds(low, SLAB)) for v in range(VARS)]
            befores = [read(v, b, pl.ds(before, 1)) for v in range(VARS)]
            afters = [read(v, b, pl.ds(after, 1)) for v in range(VARS)]
            result = stencil(tiles, befores, afters, mask_n, mask_p, damp)
            write(b, low, tiles, result)
            return carry

        lax.fori_loop(0, PER_BLOCK, step, 0)

    def read_state(v, b, rows):
        return state_ref[0, v, b, rows, :]

    def read_half(v, b, rows):
        return half_ref[v, b, rows, :]

    def write_half(b, low, tiles, result):
        scale = 0.5 * step_ref[b, pl.ds(low, SLAB), :]
        for v in range(VARS):
            half_ref[v, b, pl.ds(low, SLAB), :] = tiles[v] - scale * result[v]

    def write_spatial(b, low, tiles, result):
        for v in range(VARS):
            spatial_ref[v, b, pl.ds(low, SLAB), :] = result[v]

    for b in range(BLOCKS):
        live = live_ref[first + b]
        sweep(read_state, write_half, b, live)
        for side in range(2):
            place, local = ghost_place(partner_ref, 2 * b + side)
            row = (live - 1) if side else 0
            sign = 0.5 if side else -0.5
            rows = pl.ds(row, 1)
            ghost = [gathered_ref[place, pl.ds(local * VARS + v, 1), :] for v in range(VARS)]
            damp = 0.25 + visc_ref[b, rows, :]
            scale = 0.5 * step_ref[b, rows, :]
            for u in range(VARS):
                total = -damp * ghost[u]
                for v in range(VARS):
                    total = total + (sign * row_ref[u, v]) * ghost[v]
                half_ref[u, b, rows, :] = half_ref[u, b, rows, :] - scale * total
        for side in range(2):
            row = (live - 1) if side else 0
            for v in range(VARS):
                faces_ref[pl.ds((2 * b + side) * VARS + v, 1), :] = half_ref[v, b, pl.ds(row, 1), :]
        sweep(read_half, write_spatial, b, live)


def slab_kernel(live_ref, row_ref, cell_ref, got_ref, visc_ref, step_ref, sent_ref, rate_ref):
    i = lax.axis_index("inst")
    b, j = i // PER_BLOCK, i % PER_BLOCK
    live = live_ref[lax.axis_index("blk") * BLOCKS + b]
    low = pl.multiple_of(j * SLAB, SLAB)
    step = step_ref[b, pl.ds(low, SLAB), :]
    step_before = step_ref[b, pl.ds(jnp.maximum(low - 1, 0), 1), :]
    step_after = step_ref[b, pl.ds(jnp.minimum(low + SLAB, ROWS - 1), 1), :]
    row = low + lax.broadcasted_iota(jnp.int32, (SLAB, CELLS), 0)
    step_n, step_p = row_shifts(step, step_before, step_after)
    step_e, step_w = east_west(step)
    scale_n = jnp.where(row + 1 < live, step + step_n, 0.0)
    scale_p = jnp.where(row > 0, step + step_p, 0.0)
    scale_e, scale_w = step + step_e, step + step_w
    damp = 0.5 * (0.25 + visc_ref[b, pl.ds(low, SLAB), :])
    centre = 8.0 * step

    def times(rows, with_second):
        values = [got_ref[t, rows, :] for t in range(INST)]
        p = [values[t] + values[t + HALF] for t in range(HALF)]
        q = [values[t] - values[t + HALF] for t in range(HALF)]
        p, q = apply_even(p), apply_odd(q)
        for t in range(HALF):
            rate_ref[t, rows, :] = p[t] + q[t]
            rate_ref[t + HALF, rows, :] = p[t] - q[t]
        if with_second is not None:
            p, q = apply_even(p), apply_odd(q)
            for t in range(HALF):
                sent_ref[t, rows, :] = with_second * (p[t] + q[t])
                sent_ref[t + HALF, rows, :] = with_second * (p[t] - q[t])

    half_step = [-step[0:8, :], -step[8:16, :]]
    for v in range(VARS):
        for k in range(2):
            at = v * SLAB + 8 * k
            times(slice(at, at + 8), half_step[k])
    times(slice(MAIN, MAIN + 8), None)
    times(slice(MAIN + 8, MAIN + 16), None)

    def instance(t, carry):
        across, along, smooth, rates = [], [], [], []
        for v in range(VARS):
            rate = rate_ref[t, pl.ds(v * SLAB, SLAB), :]
            n, p = row_shifts(rate, rate_ref[t, PREV + v : PREV + v + 1, :], rate_ref[t, NEXT + v : NEXT + v + 1, :])
            e, w = east_west(rate)
            n, p, e, w = scale_n * n, scale_p * p, scale_e * e, scale_w * w
            across.append(n - p)
            along.append(e - w)
            smooth.append((n + p) + (e + w) - centre * rate)
            rates.append(rate)
        for u in range(VARS):
            rows = pl.ds(u * SLAB, SLAB)
            total = sent_ref[t, rows, :] + rates[u] + damp * smooth[u]
            for v in range(VARS):
                total = total - (0.25 * row_ref[u, v]) * across[v] - (0.25 * cell_ref[u, v]) * along[v]
            sent_ref[t, rows, :] = total
        return carry

    lax.fori_loop(0, INST, instance, 0)


def face_kernel(live_ref, weights_ref, got_ref, half_ref, step_ref, out_ref):
    first = lax.axis_index("blk") * BLOCKS
    me = lax.axis_index("inst")
    total = jnp.zeros((FACES * VARS, CELLS), jnp.float32)
    for s in range(INST):
        total = total + weights_ref[me, s] * got_ref[s, FACE : FACE + FACES * VARS, :]
    out_ref[FACES * VARS :, :] = total
    for b in range(BLOCKS):
        for side in range(2):
            row = (live_ref[first + b] - 1) if side else 0
            scale = 0.5 * step_ref[b, pl.ds(row, 1), :]
            at = (2 * b + side) * VARS
            out_ref[at : at + VARS, :] = half_ref[at : at + VARS, :] - scale * total[at : at + VARS, :]


def final_kernel(live_ref, partner_ref, row_ref, state_ref, visc_ref, step_ref, spatial_ref, got_ref, gathered_ref,
                 new_ref, residual_ref):
    first = lax.axis_index("blk") * BLOCKS
    for b in range(BLOCKS):
        live = live_ref[first + b]
        for j in range(PER_BLOCK):
            low = j * SLAB
            rows = slice(low, low + SLAB)
            row = low + lax.broadcasted_iota(jnp.int32, (SLAB, CELLS), 0)
            step = step_ref[b, rows, :]
            for v in range(VARS):
                total = got_ref[b * PER_BLOCK + j, v * SLAB : (v + 1) * SLAB, :] + spatial_ref[v, b, rows, :]
                total = jnp.where(row < live, total, 0.0)
                residual_ref[0, v, b, rows, :] = total
                new_ref[0, v, b, rows, :] = state_ref[0, v, b, rows, :] - step * total
        for side in range(2):
            place, local = ghost_place(partner_ref, 2 * b + side)
            row = (live - 1) if side else 0
            sign = 0.5 if side else -0.5
            rows = pl.ds(row, 1)
            step = step_ref[b, rows, :]
            damp = 0.25 + visc_ref[b, rows, :]
            ghost = [
                gathered_ref[place, pl.ds(local * VARS + v, 1), :]
                - 0.5 * step * gathered_ref[place, pl.ds((FACES + local) * VARS + v, 1), :]
                for v in range(VARS)
            ]
            for u in range(VARS):
                total = -damp * ghost[u]
                for v in range(VARS):
                    total = total + (sign * row_ref[u, v]) * ghost[v]
                residual_ref[0, u, b, rows, :] = residual_ref[0, u, b, rows, :] + total
                new_ref[0, u, b, rows, :] = new_ref[0, u, b, rows, :] - step * total


def call(body, outs, in_specs, scratch=(), name=None):
    return pl.pallas_call(
        body,
        out_shape=[jax.ShapeDtypeStruct(shape, jnp.float32) for shape in outs],
        in_specs=in_specs,
        out_specs=[VMEM] * len(outs),
        scratch_shapes=[pltpu.VMEM(shape, jnp.float32) for shape in scratch],
        compiler_params=PARAMS,
        name=name,
    )


def gathered_over_blocks(value):
    def moved(array, y, x, core):
        pairs = []
        for to in range(16):
            source = ((to // 8 + y) % 2) * 8 + (((to // 2) % 4 + x) % 4) * 2 + (to + core) % 2
            pairs.append((source, to))
        return lax.ppermute(array, "blk", pairs)

    value = value[None]
    value = jnp.concatenate([value, moved(value, 1, 0, 0)])
    value = jnp.concatenate([value] + [moved(value, 0, x, 0) for x in (1, 2, 3)])
    return jnp.concatenate([value, moved(value, 0, 0, 1)])


def per_device(state, row_jacobian, cell_jacobian, viscosity, local_step, live_rows, partner):
    whole = state.shape
    chunks, faces = call(
        pack_kernel, [(INST, SENT, CELLS), (FACES * VARS, CELLS)], [SMEM, VMEM], name="pack"
    )(live_rows, state)
    slabs = lax.all_to_all(chunks, "inst", 0, 0, tiled=True)
    ghosts = gathered_over_blocks(faces)
    spatial, half_faces = call(
        spatial_kernel,
        [(VARS, BLOCKS, ROWS, CELLS), (FACES * VARS, CELLS)],
        [SMEM, SMEM, SMEM, SMEM, VMEM, VMEM, VMEM, VMEM],
        [(VARS, BLOCKS, ROWS, CELLS)],
        name="spatial",
    )(live_rows, partner, row_jacobian, cell_jacobian, state, viscosity, local_step, ghosts)
    slabs, spatial = lax.optimization_barrier((slabs, spatial))
    (sent,) = call(
        slab_kernel, [(INST, MAIN, CELLS)], [SMEM, SMEM, SMEM, VMEM, VMEM, VMEM], [(INST, 96, CELLS)], name="slab"
    )(live_rows, row_jacobian, cell_jacobian, slabs, viscosity, local_step)
    back = lax.all_to_all(sent, "inst", 0, 0, tiled=True)
    weights = jnp.array([[spectral(t - s) for s in range(INST)] for t in range(INST)], jnp.float32)
    (faces2,) = call(
        face_kernel, [(2 * FACES * VARS, CELLS)], [SMEM, SMEM, VMEM, VMEM, VMEM], name="faces"
    )(live_rows, weights, slabs, half_faces, local_step)
    ghosts2 = gathered_over_blocks(faces2)
    new_state, residual = call(
        final_kernel, [whole, whole], [SMEM, SMEM, SMEM] + [VMEM] * 6, name="final"
    )(live_rows, partner, row_jacobian, state, viscosity, local_step, spatial, back, ghosts2)
    return new_state, residual


def solution(mesh):
    return jax.shard_map(
        per_device,
        mesh=mesh,
        in_specs=(
            P("inst", None, "blk", None, None),
            P(),
            P(),
            P("blk", None, None),
            P("blk", None, None),
            P(),
            P(),
        ),
        out_specs=(P("inst", None, "blk", None, None), P("inst", None, "blk", None, None)),
        check_vma=False,
    )
```

time: 632 us -> 67.8 us (0.11)
  waiting for transfers between devices: 476 us -> 23.1 us
  local copies, waits for them, and re-layouts: 58.6 us -> 2.49 us
  blocking collectives: 40.9 us -> 0 us
  other arithmetic: 28.5 us -> 0.01 us
  starting transfers between devices: 4.26 us -> 27.4 us
  matrix products: 17.1 us -> 0 us
  Pallas kernels: 0 us -> 12.6 us
    ppermute x30 -> x10, waiting for transfers between devices: 476 us -> 17.2 us  [moved(): return lax.ppermute(array, 'blk', pairs)]
    all_gather x2 -> x0, blocking collectives: 40.9 us -> none  [evaluate(): gathered = lax.all_gather(face_rows, 'blk', axis=2, tiled=True)]
    add x32 -> x0, other arithmetic: 26.1 us -> none  [the longest x30 24.5 us: advance(): return (running + weights[turn] * moving, moving)]
    dynamic_slice x30 -> x0, local copies, waits for them, and re-layouts: 17.2 us -> none  [advance(): return (running + weights[turn] * moving, moving)]
    dot_general x4 -> x0, matrix products: 17.1 us -> none  [the longest x2 12.6 us: evaluate(): jnp.einsum('uv,tvbrc->tubrc', cell_jacobian, east - west, precision=precise)]
    all_to_all x0 -> x2, starting transfers between devices: none -> 14.5 us  [the longest x1 9.71 us: per_device(): slabs = lax.all_to_all(chunks, 'inst', 0, 0, tiled=True)]
    while x30 -> x0, local copies, waits for them, and re-layouts: 13.2 us -> none
    pallas_call x0 -> x5, Pallas kernels: none -> 12.6 us  [the longest x1 4.52 us: per_device(): call(spatial_kernel, [(VARS, BLOCKS, ROWS, CELLS), (FACES * VARS, CELLS)]...]
  transfers between devices with their start and end apart: 30 -> 12, of which waited for: 30 -> 8; matrix products, arithmetic and copies ran while one was open for 3% -> 0% of each run, Pallas kernels for 0% -> 8%
where the time goes in v1:
time: 67.8 us; the launch traced here: 66.5 us
  starting transfers between devices  27.4 us (40%)
  waiting for transfers between devices  23.1 us (34%)
  Pallas kernels  12.6 us (19%)
  local copies, waits for them, and re-layouts  2.49 us (4%)
  between operations  0.81 us (1%)
    ppermute x10, waiting for transfers between devices, moved(): return lax.ppermute(array, 'blk', pairs)  17.2 us
    ppermute x10, starting transfers between devices, moved(): return lax.ppermute(array, 'blk', pairs)  13 us
    all_to_all x1, starting transfers between devices, per_device(): slabs = lax.all_to_all(chunks, 'inst', 0, 0, tiled=True)  9.71 us
    all_to_all x1, starting transfers between devices, per_device(): back = lax.all_to_all(sent, 'inst', 0, 0, tiled=True)  4.74 us
    pallas_call x1, Pallas kernels, per_device(): call(spatial_kernel, [(VARS, BLOCKS, ROWS, CELLS), (FACES * VARS, CELLS)]...  4.52 us
    all_to_all x1, waiting for transfers between devices, per_device(): slabs = lax.all_to_all(chunks, 'inst', 0, 0, tiled=True)  4.12 us
    pallas_call x1, Pallas kernels, per_device(): call(slab_kernel, [(INST, MAIN, CELLS)], [SMEM, SMEM, SMEM, VMEM, VMEM, V...  3.88 us
    unnamed x28, local copies, waits for them, and re-layouts  2.45 us
  transfers between devices with their start and end apart: 12, of which 8 were waited for; matrix products, arithmetic and copies ran while one was open for 0% of the time, Pallas kernels for 8%

profile of v1, /device:TPU:6, one launch (start us, length us, event | category | flops | bytes accessed | tf_op | source)
XLA Modules:
  0.0 66.5 jit_solution(3815834469844153024)
XLA Ops:
  0.6 1.1 %copy-done = f32[1,5,2,128,128]{4,3,2,1,0:T(8,128)S(1)} copy-done((f32[1,5,2,128,128]{4,3,2,1,0:T(8,128)S(1)}, f32[1,5,2,128,128]{4,3,2,1,0:T(8,128)}, u32[]{:S(2)}) %copy-start) | copy-done | bytes 655384
  1.7 0.7 copy-done.6
  2.4 1.6 %pack.1 = (f32[16,112,128]{2,1,0:T(8,128)}, f32[20,128]{1,0:T(8,128)S(1)}) custom-call(s32[32]{0:T(128)S(1)} %copy-done.6, f32[1,5,2,128,128]{4,3,2,1,0:T(8,128)S(1)} %copy-done), custom_call_target="tpu_custom_call" | custom-call | tf_op jit(solution)/shard_map/pack/pallas_call | solution.py:338
  4.0 9.7 %all-to-all-start = ((f32[16,112,128]{2,1,0:T(8,128)}), f32[16,112,128]{2,1,0:T(8,128)S(1)}, u32[]{:S(2)}, u32[]{:S(2)}) async-start(f32[16,112,128]{2,1,0:T(8,128)} %get-tuple-element.8), calls=%async_computation | async-start | bytes 1835008 | tf_op jit(solution)/shard_map/all_to_all | solution.py:341
  13.7 3.0 %collective-permute-start = (f32[1,20,128]{2,1,0:T(8,128)S(1)}, f32[1,20,128]{2,1,0:T(8,128)S(1)}, u32[]{:S(2)}, u32[]{:S(2)}) collective-permute-start(f32[1,20,128]{2,1,0:T(8,128)S(1)} %bitcast.8), channel_id=1, source_target_pairs={{8,0},{9,1},{10,2},{11,3},{12,4},{13,5},{14,6},{15,7},{0,8},{1,9},... | collective-permute-start | bytes 30728 | tf_op jit(solution)/shard_map/ppermute | solution.py:328
  16.7 2.3 %collective-permute-done = f32[1,20,128]{2,1,0:T(8,128)S(1)} collective-permute-done((f32[1,20,128]{2,1,0:T(8,128)S(1)}, f32[1,20,128]{2,1,0:T(8,128)S(1)}, u32[]{:S(2)}, u32[]{:S(2)}) %collective-permute-start) | collective-permute-done | bytes 10272 | tf_op jit(solution)/shard_map/ppermute | solution.py:328
  19.0 0.5 collective-permute-start.3
  19.5 2.4 %collective-permute-start.2 = (f32[2,20,128]{2,1,0:T(8,128)S(1)}, f32[2,20,128]{2,1,0:T(8,128)S(1)}, u32[]{:S(2)}, u32[]{:S(2)}) collective-permute-start(f32[2,20,128]{2,1,0:T(8,128)S(1)} %pad_maximum_fusion.1), channel_id=1, source_target_pairs={{4,0},{5,1},{6,2},{7,3},{0,4},{1,5},{2,6},{3,7},{12,8},{13,9},{14,... | collective-permute-start | bytes 61448 | tf_op jit(solution)/shard_map/ppermute | solution.py:328
  21.9 5.0 %collective-permute-done.1 = f32[2,20,128]{2,1,0:T(8,128)S(1)} collective-permute-done((f32[2,20,128]{2,1,0:T(8,128)S(1)}, f32[2,20,128]{2,1,0:T(8,128)S(1)}, u32[]{:S(2)}, u32[]{:S(2)}) %collective-permute-start.1) | collective-permute-done | bytes 20512 | tf_op jit(solution)/shard_map/ppermute | solution.py:328
  27.1 1.3 %collective-permute-done.4 = f32[8,20,128]{2,1,0:T(8,128)S(1)} collective-permute-done((f32[8,20,128]{2,1,0:T(8,128)S(1)}, f32[8,20,128]{2,1,0:T(8,128)S(1)}, u32[]{:S(2)}, u32[]{:S(2)}) %collective-permute-start.4) | collective-permute-done | bytes 81952 | tf_op jit(solution)/shard_map/ppermute | solution.py:328
  28.4 0.6 copy-done.4
  29.1 4.5 %spatial.1 = (f32[5,2,128,128]{3,2,1,0:T(8,128)S(1)}, f32[20,128]{1,0:T(8,128)S(1)}) custom-call(s32[32]{0:T(128)S(1)} %copy-done.7, s32[64]{0:T(128)S(1)} %copy-done.9, f32[5,5]{1,0:T(8,128)S(1)} %copy-done.4, f32[5,5]{1,0:T(8,128)S(1)} %copy-done.5, f32[1,5,2,128,128]{4,3,2,1,0:T(8,128)S(1)} %copy-done.1, f32[2,128,128]{2,1,0:T(8,128)S(1)} %copy-done.3, ...), custom_call_target="tpu_custom_call" | custom-call | tf_op jit(solution)/shard_map/spatial/pallas_call | solution.py:343
  33.6 4.1 %all-to-all-done.got_ref = f32[16,112,128]{2,1,0:T(8,128)S(1)} async-done(((f32[16,112,128]{2,1,0:T(8,128)}), f32[16,112,128]{2,1,0:T(8,128)S(1)}, u32[]{:S(2)}, u32[]{:S(2)}) %all-to-all-start) | async-done | bytes 917536 | tf_op jit(solution)/shard_map/all_to_all | solution.py:341
  37.7 3.9 %slab.1 = f32[16,80,128]{2,1,0:T(8,128)} custom-call(s32[32]{0:T(128)S(1)} %copy-done.7, f32[5,5]{1,0:T(8,128)S(1)} %copy-done.4, f32[5,5]{1,0:T(8,128)S(1)} %copy-done.5, f32[16,112,128]{2,1,0:T(8,128)S(1)} %all-to-all-done.got_ref, f32[2,128,128]{2,1,0:T(8,128)S(1)} %copy-done.3, f32[2,128,128]{2,1,0:T(8,128)S(1)} %copy-done.2), custom_call_target="tpu_custom_call" | custom-call | tf_op jit(solution)/shard_map/slab/pallas_call | solution.py:351
  41.6 4.7 %all-to-all-start.1 = ((f32[16,80,128]{2,1,0:T(8,128)}), f32[16,80,128]{2,1,0:T(8,128)S(1)}, u32[]{:S(2)}, u32[]{:S(2)}) async-start(f32[16,80,128]{2,1,0:T(8,128)} %slab.1), calls=%async_computation.1 | async-start | bytes 1310720 | tf_op jit(solution)/shard_map/all_to_all | solution.py:354
  46.4 0.7 %faces.1 = f32[40,128]{1,0:T(8,128)S(1)} custom-call(s32[32]{0:T(128)S(1)} %copy-done.7, f32[16,16]{1,0:T(8,128)S(1)} %copy-done.8, f32[16,112,128]{2,1,0:T(8,128)S(1)} %all-to-all-done.got_ref, f32[20,128]{1,0:T(8,128)S(1)} %get-tuple-element.13.half_ref, f32[2,128,128]{2,1,0:T(8,128)S(1)} %copy-done.2), custom_call_target="tpu_custom_call" | custom-call | tf_op jit(solution)/shard_map/faces/pallas_call | solution.py:356
  47.1 3.4 %collective-permute-start.5 = (f32[1,40,128]{2,1,0:T(8,128)S(1)}, f32[1,40,128]{2,1,0:T(8,128)S(1)}, u32[]{:S(2)}, u32[]{:S(2)}) collective-permute-start(f32[1,40,128]{2,1,0:T(8,128)S(1)} %bitcast.6), channel_id=1, source_target_pairs={{8,0},{9,1},{10,2},{11,3},{12,4},{13,5},{14,6},{15,7},{0,8},{1,9},... | collective-permute-start | bytes 61448 | tf_op jit(solution)/shard_map/ppermute | solution.py:328
  50.5 2.0 %collective-permute-done.5 = f32[1,40,128]{2,1,0:T(8,128)S(1)} collective-permute-done((f32[1,40,128]{2,1,0:T(8,128)S(1)}, f32[1,40,128]{2,1,0:T(8,128)S(1)}, u32[]{:S(2)}, u32[]{:S(2)}) %collective-permute-start.5) | collective-permute-done | bytes 20512 | tf_op jit(solution)/shard_map/ppermute | solution.py:328
  52.5 0.5 collective-permute-start.8
  53.0 3.1 %collective-permute-start.7 = (f32[2,40,128]{2,1,0:T(8,128)S(1)}, f32[2,40,128]{2,1,0:T(8,128)S(1)}, u32[]{:S(2)}, u32[]{:S(2)}) collective-permute-start(f32[2,40,128]{2,1,0:T(8,128)S(1)} %pad_maximum_fusion), channel_id=1, source_target_pairs={{4,0},{5,1},{6,2},{7,3},{0,4},{1,5},{2,6},{3,7},{12,8},{13,9},{14,... | collective-permute-start | bytes 122888 | tf_op jit(solution)/shard_map/ppermute | solution.py:328
  56.1 5.2 %collective-permute-done.6 = f32[2,40,128]{2,1,0:T(8,128)S(1)} collective-permute-done((f32[2,40,128]{2,1,0:T(8,128)S(1)}, f32[2,40,128]{2,1,0:T(8,128)S(1)}, u32[]{:S(2)}, u32[]{:S(2)}) %collective-permute-start.6) | collective-permute-done | bytes 40992 | tf_op jit(solution)/shard_map/ppermute | solution.py:328
  61.4 1.4 %collective-permute-done.9 = f32[8,40,128]{2,1,0:T(8,128)S(1)} collective-permute-done((f32[8,40,128]{2,1,0:T(8,128)S(1)}, f32[8,40,128]{2,1,0:T(8,128)S(1)}, u32[]{:S(2)}, u32[]{:S(2)}) %collective-permute-start.9) | collective-permute-done | bytes 163872 | tf_op jit(solution)/shard_map/ppermute | solution.py:328
  62.8 1.8 %all-to-all-done.1.got_ref = f32[16,80,128]{2,1,0:T(8,128)S(1)} async-done(((f32[16,80,128]{2,1,0:T(8,128)}), f32[16,80,128]{2,1,0:T(8,128)S(1)}, u32[]{:S(2)}, u32[]{:S(2)}) %all-to-all-start.1) | async-done | bytes 655392 | tf_op jit(solution)/shard_map/all_to_all | solution.py:354
  64.6 1.9 %final.1 = (f32[1,5,2,128,128]{4,3,2,1,0:T(8,128)}, f32[1,5,2,128,128]{4,3,2,1,0:T(8,128)}) custom-call(s32[32]{0:T(128)S(1)} %copy-done.7, s32[64]{0:T(128)S(1)} %copy-done.9, f32[5,5]{1,0:T(8,128)S(1)} %copy-done.4, f32[1,5,2,128,128]{4,3,2,1,0:T(8,128)S(1)} %copy-done.1, f32[2,128,128]{2,1,0:T(8,128)S(1)} %copy-done.3, f32[2,128,128]{2,1,0:T(8,128)S(1)} %copy-done.2, ...), custom_call_target="tpu_custom_call" | custom-call | tf_op jit(solution)/shard_map/final/pallas_call | solution.py:360
  (39 shorter events, 0.3 us)
Async XLA Ops:
  0.6 1.1 %copy-start = (f32[1,5,2,128,128]{4,3,2,1,0:T(8,128)S(1)}, f32[1,5,2,128,128]{4,3,2,1,0:T(8,128)}, u32[]{:S(2)}) copy-start(f32[1,5,2,128,128]{4,3,2,1,0:T(8,128)} %state_ref.5) | copy-start | bytes 1966084
  1.7 0.7 copy-start.6
  4.0 24.5 %copy-start.1 = (f32[1,5,2,128,128]{4,3,2,1,0:T(8,128)S(1)}, f32[1,5,2,128,128]{4,3,2,1,0:T(8,128)}, u32[]{:S(2)}) copy-start(f32[1,5,2,128,128]{4,3,2,1,0:T(8,128)} %state_ref.5) | copy-start | bytes 1966084
  4.0 33.8 %all-to-all-start = ((f32[16,112,128]{2,1,0:T(8,128)}), f32[16,112,128]{2,1,0:T(8,128)S(1)}, u32[]{:S(2)}, u32[]{:S(2)}) async-start(f32[16,112,128]{2,1,0:T(8,128)} %get-tuple-element.8), calls=%async_computation | async-start | bytes 1835008 | tf_op jit(solution)/shard_map/all_to_all | solution.py:341
  13.7 5.3 %collective-permute-start = (f32[1,20,128]{2,1,0:T(8,128)S(1)}, f32[1,20,128]{2,1,0:T(8,128)S(1)}, u32[]{:S(2)}, u32[]{:S(2)}) collective-permute-start(f32[1,20,128]{2,1,0:T(8,128)S(1)} %bitcast.8), channel_id=1, source_target_pairs={{8,0},{9,1},{10,2},{11,3},{12,4},{13,5},{14,6},{15,7},{0,8},{1,9},... | collective-permute-start | bytes 30728 | tf_op jit(solution)/shard_map/ppermute | solution.py:328
  19.0 8.0 %collective-permute-start.3 = (f32[2,20,128]{2,1,0:T(8,128)S(1)}, f32[2,20,128]{2,1,0:T(8,128)S(1)}, u32[]{:S(2)}, u32[]{:S(2)}) collective-permute-start(f32[2,20,128]{2,1,0:T(8,128)S(1)} %pad_maximum_fusion.1), channel_id=1, source_target_pairs={{6,0},{7,1},{0,2},{1,3},{2,4},{3,5},{4,6},{5,7},{14,8},{15,9},{8,1... | collective-permute-start | bytes 61448 | tf_op jit(solution)/shard_map/ppermute | solution.py:328
  19.5 7.5 %collective-permute-start.2 = (f32[2,20,128]{2,1,0:T(8,128)S(1)}, f32[2,20,128]{2,1,0:T(8,128)S(1)}, u32[]{:S(2)}, u32[]{:S(2)}) collective-permute-start(f32[2,20,128]{2,1,0:T(8,128)S(1)} %pad_maximum_fusion.1), channel_id=1, source_target_pairs={{4,0},{5,1},{6,2},{7,3},{0,4},{1,5},{2,6},{3,7},{12,8},{13,9},{14,... | collective-permute-start | bytes 61448 | tf_op jit(solution)/shard_map/ppermute | solution.py:328
  21.9 5.0 %collective-permute-start.1 = (f32[2,20,128]{2,1,0:T(8,128)S(1)}, f32[2,20,128]{2,1,0:T(8,128)S(1)}, u32[]{:S(2)}, u32[]{:S(2)}) collective-permute-start(f32[2,20,128]{2,1,0:T(8,128)S(1)} %pad_maximum_fusion.1), channel_id=1, source_target_pairs={{2,0},{3,1},{4,2},{5,3},{6,4},{7,5},{0,6},{1,7},{10,8},{11,9},{12,... | collective-permute-start | bytes 61448 | tf_op jit(solution)/shard_map/ppermute | solution.py:328
  27.0 1.5 %copy-start.2 = (f32[2,128,128]{2,1,0:T(8,128)S(1)}, f32[2,128,128]{2,1,0:T(8,128)}, u32[]{:S(2)}) copy-start(f32[2,128,128]{2,1,0:T(8,128)} %step_ref.7) | copy-start | bytes 393220
  27.0 1.5 %copy-start.3 = (f32[2,128,128]{2,1,0:T(8,128)S(1)}, f32[2,128,128]{2,1,0:T(8,128)}, u32[]{:S(2)}) copy-start(f32[2,128,128]{2,1,0:T(8,128)} %visc_ref.5) | copy-start | bytes 393220
  27.0 1.4 %collective-permute-start.4 = (f32[8,20,128]{2,1,0:T(8,128)S(1)}, f32[8,20,128]{2,1,0:T(8,128)S(1)}, u32[]{:S(2)}, u32[]{:S(2)}) collective-permute-start(f32[8,20,128]{2,1,0:T(8,128)S(1)} %get-tuple-element.20), channel_id=1, source_target_pairs={{1,0},{0,1},{3,2},{2,3},{5,4},{4,5},{7,6},{6,7},{9,8},{8,9},{11,10... | collective-permute-start | bytes 245768 | tf_op jit(solution)/shard_map/ppermute | solution.py:328
  28.4 0.7 %copy-start.4 = (f32[5,5]{1,0:T(8,128)S(1)}, f32[5,5]{1,0:T(8,128)}, u32[]{:S(2)}) copy-start(f32[5,5]{1,0:T(8,128)} %row_ref.5) | copy-start | bytes 304
  28.4 0.7 %copy-start.5 = (f32[5,5]{1,0:T(8,128)S(1)}, f32[5,5]{1,0:T(8,128)}, u32[]{:S(2)}) copy-start(f32[5,5]{1,0:T(8,128)} %cell_ref.3) | copy-start | bytes 304
  28.4 0.7 %copy-start.7 = (s32[32]{0:T(128)S(1)}, s32[32]{0:T(128)}, u32[]{:S(2)}) copy-start(s32[32]{0:T(128)} %live_ref.9) | copy-start | bytes 388
  28.4 0.7 %copy-start.9 = (s32[64]{0:T(128)S(1)}, s32[64]{0:T(128)}, u32[]{:S(2)}) copy-start(s32[64]{0:T(128)} %partner_ref.3) | copy-start | bytes 772
  41.6 4.8 %copy-start.8 = (f32[16,16]{1,0:T(8,128)S(1)}, f32[16,16]{1,0:T(8,128)}, u32[]{:S(2)}) copy-start(f32[16,16]{1,0:T(8,128)} %constant.2.clone.weights_ref) | copy-start | bytes 3076
  41.6 23.0 %all-to-all-start.1 = ((f32[16,80,128]{2,1,0:T(8,128)}), f32[16,80,128]{2,1,0:T(8,128)S(1)}, u32[]{:S(2)}, u32[]{:S(2)}) async-start(f32[16,80,128]{2,1,0:T(8,128)} %slab.1), calls=%async_computation.1 | async-start | bytes 1310720 | tf_op jit(solution)/shard_map/all_to_all | solution.py:354
  47.1 5.4 %collective-permute-start.5 = (f32[1,40,128]{2,1,0:T(8,128)S(1)}, f32[1,40,128]{2,1,0:T(8,128)S(1)}, u32[]{:S(2)}, u32[]{:S(2)}) collective-permute-start(f32[1,40,128]{2,1,0:T(8,128)S(1)} %bitcast.6), channel_id=1, source_target_pairs={{8,0},{9,1},{10,2},{11,3},{12,4},{13,5},{14,6},{15,7},{0,8},{1,9},... | collective-permute-start | bytes 61448 | tf_op jit(solution)/shard_map/ppermute | solution.py:328
  52.5 8.8 %collective-permute-start.8 = (f32[2,40,128]{2,1,0:T(8,128)S(1)}, f32[2,40,128]{2,1,0:T(8,128)S(1)}, u32[]{:S(2)}, u32[]{:S(2)}) collective-permute-start(f32[2,40,128]{2,1,0:T(8,128)S(1)} %pad_maximum_fusion), channel_id=1, source_target_pairs={{6,0},{7,1},{0,2},{1,3},{2,4},{3,5},{4,6},{5,7},{14,8},{15,9},{8,1... | collective-permute-start | bytes 122888 | tf_op jit(solution)/shard_map/ppermute | solution.py:328
  53.0 8.3 %collective-permute-start.7 = (f32[2,40,128]{2,1,0:T(8,128)S(1)}, f32[2,40,128]{2,1,0:T(8,128)S(1)}, u32[]{:S(2)}, u32[]{:S(2)}) collective-permute-start(f32[2,40,128]{2,1,0:T(8,128)S(1)} %pad_maximum_fusion), channel_id=1, source_target_pairs={{4,0},{5,1},{6,2},{7,3},{0,4},{1,5},{2,6},{3,7},{12,8},{13,9},{14,... | collective-permute-start | bytes 122888 | tf_op jit(solution)/shard_map/ppermute | solution.py:328
  56.1 5.2 %collective-permute-start.6 = (f32[2,40,128]{2,1,0:T(8,128)S(1)}, f32[2,40,128]{2,1,0:T(8,128)S(1)}, u32[]{:S(2)}, u32[]{:S(2)}) collective-permute-start(f32[2,40,128]{2,1,0:T(8,128)S(1)} %pad_maximum_fusion), channel_id=1, source_target_pairs={{2,0},{3,1},{4,2},{5,3},{6,4},{7,5},{0,6},{1,7},{10,8},{11,9},{12,... | collective-permute-start | bytes 122888 | tf_op jit(solution)/shard_map/ppermute | solution.py:328
  61.3 1.5 %collective-permute-start.9 = (f32[8,40,128]{2,1,0:T(8,128)S(1)}, f32[8,40,128]{2,1,0:T(8,128)S(1)}, u32[]{:S(2)}, u32[]{:S(2)}) collective-permute-start(f32[8,40,128]{2,1,0:T(8,128)S(1)} %get-tuple-element.14), channel_id=1, source_target_pairs={{1,0},{0,1},{3,2},{2,3},{5,4},{4,5},{7,6},{6,7},{9,8},{8,9},{11,10... | collective-permute-start | bytes 491528 | tf_op jit(solution)/shard_map/ppermute | solution.py:328

commit v2 on v1

--- a/solution.py
+++ b/solution.py
@@ -17,7 +17,11 @@
 FACES = 2 * BLOCKS
 VMEM = pl.BlockSpec(memory_space=pltpu.VMEM)
 SMEM = pl.BlockSpec(memory_space=pltpu.SMEM)
-PARAMS = pltpu.CompilerParams(vmem_limit_bytes=32 * 1024 * 1024)
+HBM = pl.BlockSpec(memory_space=pltpu.HBM)
+
+LIVE = pltpu.SMEM((32,), jnp.int32)
+PARTNER = pltpu.SMEM((64,), jnp.int32)
+JACOBIAN = pltpu.SMEM((VARS, VARS), jnp.float32)
 
 
 def spectral(m):
@@ -89,25 +93,51 @@
     return pltpu.roll(tile, CELLS - 1, 1), pltpu.roll(tile, 1, 1)
 
 
-def pack_kernel(live_ref, state_ref, chunks_ref, faces_ref):
+def fetched(sources, held, ready):
+    copies = [pltpu.make_async_copy(a, b, ready.at[k]) for k, (a, b) in enumerate(zip(sources, held))]
+    for copy in copies:
+        copy.start()
+    return copies
+
+
+def pack_kernel(live_in, state_ref, chunks_ref, faces_ref, live_ref, arrived, ready):
     first = lax.axis_index("blk") * BLOCKS
+    scalars = fetched([live_in], [live_ref], ready)
+    copies = []
+    for i in range(INST):
+        b, low = i // PER_BLOCK, (i % PER_BLOCK) * SLAB
+        copy = pltpu.make_async_copy(
+            state_ref.at[0, :, b, low : low + SLAB, :], chunks_ref.at[i, 0:VARS], arrived.at[i]
+        )
+        copy.start()
+        copies.append(copy)
+    for copy in copies + scalars:
+        copy.wait()
+
+    def row_of(v, b, row):
+        return chunks_ref[b * PER_BLOCK + row // SLAB, v, pl.ds(row % SLAB, 1), :]
+
     for b in range(BLOCKS):
         last = live_ref[first + b] - 1
         for v in range(VARS):
-            faces_ref[pl.ds((2 * b) * VARS + v, 1), :] = state_ref[0, v, b, 0:1, :]
-            faces_ref[pl.ds((2 * b + 1) * VARS + v, 1), :] = state_ref[0, v, b, pl.ds(last, 1), :]
+            low, high = (2 * b) * VARS + v, (2 * b + 1) * VARS + v
+            faces_ref[low : low + 1, :] = row_of(v, b, 0)
+            faces_ref[high : high + 1, :] = row_of(v, b, last)
     faces = faces_ref[...]
-    for b in range(BLOCKS):
-        for j in range(PER_BLOCK):
-            i = b * PER_BLOCK + j
-            low = j * SLAB
-            for v in range(VARS):
-                chunks_ref[i, v * SLAB : (v + 1) * SLAB, :] = state_ref[0, v, b, low : low + SLAB, :]
-                before, after = max(low - 1, 0), min(low + SLAB, ROWS - 1)
-                chunks_ref[i, PREV + v : PREV + v + 1, :] = state_ref[0, v, b, before : before + 1, :]
-                chunks_ref[i, NEXT + v : NEXT + v + 1, :] = state_ref[0, v, b, after : after + 1, :]
-            chunks_ref[i, FACE : FACE + FACES * VARS, :] = faces
-            chunks_ref[i, FACE + FACES * VARS : SENT, :] = jnp.zeros((SENT - FACE - FACES * VARS, CELLS), jnp.float32)
+    chunks_ref[0, VARS, 2 * VARS :, :] = faces[: SLAB - 2 * VARS, :]
+    chunks_ref[0, VARS + 1, : FACES * VARS + 2 * VARS - SLAB, :] = faces[SLAB - 2 * VARS :, :]
+    chunks_ref[0, VARS + 1, FACES * VARS + 2 * VARS - SLAB :, :] = jnp.zeros((SENT - FACE - FACES * VARS, CELLS), jnp.float32)
+    chunks_ref[0, VARS, 0 : 2 * VARS, :] = jnp.zeros((2 * VARS, CELLS), jnp.float32)
+    extra = chunks_ref[0, VARS : VARS + 2, :, :]
+    for i in range(1, INST):
+        chunks_ref[i, VARS : VARS + 2, :, :] = extra
+    for i in range(INST):
+        b, j = i // PER_BLOCK, i % PER_BLOCK
+        for v in range(VARS):
+            if j > 0:
+                chunks_ref[i, VARS, v : v + 1, :] = row_of(v, b, j * SLAB - 1)
+            if j < PER_BLOCK - 1:
+                chunks_ref[i, VARS, VARS + v : VARS + v + 1, :] = row_of(v, b, (j + 1) * SLAB)
 
 
 def ghost_place(partner_ref, face):
@@ -196,22 +226,12 @@
         sweep(read_half, write_spatial, b, live)
 
 
-def slab_kernel(live_ref, row_ref, cell_ref, got_ref, visc_ref, step_ref, sent_ref, rate_ref):
+def slab_kernel(live_in, row_in, cell_in, got_ref, visc_ref, step_ref, sent_ref, rate_ref, live_ref, row_ref, cell_ref, ready):
+    scalars = fetched([live_in, row_in, cell_in], [live_ref, row_ref, cell_ref], ready)
     i = lax.axis_index("inst")
     b, j = i // PER_BLOCK, i % PER_BLOCK
-    live = live_ref[lax.axis_index("blk") * BLOCKS + b]
     low = pl.multiple_of(j * SLAB, SLAB)
     step = step_ref[b, pl.ds(low, SLAB), :]
-    step_before = step_ref[b, pl.ds(jnp.maximum(low - 1, 0), 1), :]
-    step_after = step_ref[b, pl.ds(jnp.minimum(low + SLAB, ROWS - 1), 1), :]
-    row = low + lax.broadcasted_iota(jnp.int32, (SLAB, CELLS), 0)
-    step_n, step_p = row_shifts(step, step_before, step_after)
-    step_e, step_w = east_west(step)
-    scale_n = jnp.where(row + 1 < live, step + step_n, 0.0)
-    scale_p = jnp.where(row > 0, step + step_p, 0.0)
-    scale_e, scale_w = step + step_e, step + step_w
-    damp = 0.5 * (0.25 + visc_ref[b, pl.ds(low, SLAB), :])
-    centre = 8.0 * step
 
     def times(rows, with_second):
         values = [got_ref[t, rows, :] for t in range(INST)]
@@ -234,6 +254,19 @@
             times(slice(at, at + 8), half_step[k])
     times(slice(MAIN, MAIN + 8), None)
     times(slice(MAIN + 8, MAIN + 16), None)
+    for copy in scalars:
+        copy.wait()
+    live = live_ref[lax.axis_index("blk") * BLOCKS + b]
+    step_before = step_ref[b, pl.ds(jnp.maximum(low - 1, 0), 1), :]
+    step_after = step_ref[b, pl.ds(jnp.minimum(low + SLAB, ROWS - 1), 1), :]
+    row = low + lax.broadcasted_iota(jnp.int32, (SLAB, CELLS), 0)
+    step_n, step_p = row_shifts(step, step_before, step_after)
+    step_e, step_w = east_west(step)
+    scale_n = jnp.where(row + 1 < live, step + step_n, 0.0)
+    scale_p = jnp.where(row > 0, step + step_p, 0.0)
+    scale_e, scale_w = step + step_e, step + step_w
+    damp = 0.5 * (0.25 + visc_ref[b, pl.ds(low, SLAB), :])
+    centre = 8.0 * step
 
     def instance(t, carry):
         across, along, smooth, rates = [], [], [], []
@@ -254,7 +287,7 @@
             sent_ref[t, rows, :] = total
         return carry
 
-    lax.fori_loop(0, INST, instance, 0)
+    lax.fori_loop(0, INST, instance, 0, unroll=4)
 
 
 def face_kernel(live_ref, weights_ref, got_ref, half_ref, step_ref, out_ref):
@@ -272,9 +305,12 @@
             out_ref[at : at + VARS, :] = half_ref[at : at + VARS, :] - scale * total[at : at + VARS, :]
 
 
-def final_kernel(live_ref, partner_ref, row_ref, state_ref, visc_ref, step_ref, spatial_ref, got_ref, gathered_ref,
-                 new_ref, residual_ref):
+def final_kernel(live_in, partner_in, row_in, state_ref, visc_ref, step_ref, spatial_ref, got_ref, gathered_ref,
+                 new_out, residual_out, new_ref, residual_ref, written, live_ref, partner_ref, row_ref, ready):
+    for copy in fetched([live_in, partner_in, row_in], [live_ref, partner_ref, row_ref], ready):
+        copy.wait()
     first = lax.axis_index("blk") * BLOCKS
+    copies = []
     for b in range(BLOCKS):
         live = live_ref[first + b]
         for j in range(PER_BLOCK):
@@ -285,8 +321,8 @@
             for v in range(VARS):
                 total = got_ref[b * PER_BLOCK + j, v * SLAB : (v + 1) * SLAB, :] + spatial_ref[v, b, rows, :]
                 total = jnp.where(row < live, total, 0.0)
-                residual_ref[0, v, b, rows, :] = total
-                new_ref[0, v, b, rows, :] = state_ref[0, v, b, rows, :] - step * total
+                residual_ref[v, b, rows, :] = total
+                new_ref[v, b, rows, :] = state_ref[0, v, b, rows, :] - step * total
         for side in range(2):
             place, local = ghost_place(partner_ref, 2 * b + side)
             row = (live - 1) if side else 0
@@ -303,18 +339,24 @@
                 total = -damp * ghost[u]
                 for v in range(VARS):
                     total = total + (sign * row_ref[u, v]) * ghost[v]
-                residual_ref[0, u, b, rows, :] = residual_ref[0, u, b, rows, :] + total
-                new_ref[0, u, b, rows, :] = new_ref[0, u, b, rows, :] - step * total
-
-
-def call(body, outs, in_specs, scratch=(), name=None):
+                residual_ref[u, b, rows, :] = residual_ref[u, b, rows, :] + total
+                new_ref[u, b, rows, :] = new_ref[u, b, rows, :] - step * total
+        for k, (held, out) in enumerate(((new_ref, new_out), (residual_ref, residual_out))):
+            copy = pltpu.make_async_copy(held.at[:, b], out.at[0, :, b], written.at[2 * b + k])
+            copy.start()
+            copies.append(copy)
+    for copy in copies:
+        copy.wait()
+
+
+def call(body, outs, in_specs, scratch=(), name=None, out_specs=None, limit=32):
     return pl.pallas_call(
         body,
         out_shape=[jax.ShapeDtypeStruct(shape, jnp.float32) for shape in outs],
         in_specs=in_specs,
-        out_specs=[VMEM] * len(outs),
-        scratch_shapes=[pltpu.VMEM(shape, jnp.float32) for shape in scratch],
-        compiler_params=PARAMS,
+        out_specs=out_specs or [VMEM] * len(outs),
+        scratch_shapes=list(scratch),
+        compiler_params=pltpu.CompilerParams(vmem_limit_bytes=limit * 1024 * 1024),
         name=name,
     )
 
@@ -336,20 +378,22 @@
 def per_device(state, row_jacobian, cell_jacobian, viscosity, local_step, live_rows, partner):
     whole = state.shape
     chunks, faces = call(
-        pack_kernel, [(INST, SENT, CELLS), (FACES * VARS, CELLS)], [SMEM, VMEM], name="pack"
+        pack_kernel, [(INST, SENT // SLAB, SLAB, CELLS), (FACES * VARS, CELLS)], [HBM, HBM],
+        [LIVE, pltpu.SemaphoreType.DMA((INST,)), pltpu.SemaphoreType.DMA((1,))], name="pack", limit=60
     )(live_rows, state)
-    slabs = lax.all_to_all(chunks, "inst", 0, 0, tiled=True)
+    slabs = lax.all_to_all(chunks, "inst", 0, 0, tiled=True).reshape(INST, SENT, CELLS)
     ghosts = gathered_over_blocks(faces)
     spatial, half_faces = call(
         spatial_kernel,
         [(VARS, BLOCKS, ROWS, CELLS), (FACES * VARS, CELLS)],
         [SMEM, SMEM, SMEM, SMEM, VMEM, VMEM, VMEM, VMEM],
-        [(VARS, BLOCKS, ROWS, CELLS)],
+        [pltpu.VMEM((VARS, BLOCKS, ROWS, CELLS), jnp.float32)],
         name="spatial",
     )(live_rows, partner, row_jacobian, cell_jacobian, state, viscosity, local_step, ghosts)
     slabs, spatial = lax.optimization_barrier((slabs, spatial))
     (sent,) = call(
-        slab_kernel, [(INST, MAIN, CELLS)], [SMEM, SMEM, SMEM, VMEM, VMEM, VMEM], [(INST, 96, CELLS)], name="slab"
+        slab_kernel, [(INST, MAIN, CELLS)], [HBM, HBM, HBM, VMEM, VMEM, VMEM],
+        [pltpu.VMEM((INST, 96, CELLS), jnp.float32), LIVE, JACOBIAN, JACOBIAN, pltpu.SemaphoreType.DMA((3,))], name="slab"
     )(live_rows, row_jacobian, cell_jacobian, slabs, viscosity, local_step)
     back = lax.all_to_all(sent, "inst", 0, 0, tiled=True)
     weights = jnp.array([[spectral(t - s) for s in range(INST)] for t in range(INST)], jnp.float32)
@@ -358,7 +402,10 @@
     )(live_rows, weights, slabs, half_faces, local_step)
     ghosts2 = gathered_over_blocks(faces2)
     new_state, residual = call(
-        final_kernel, [whole, whole], [SMEM, SMEM, SMEM] + [VMEM] * 6, name="final"
+        final_kernel, [whole, whole], [HBM, HBM, HBM] + [VMEM] * 6,
+        [pltpu.VMEM((VARS, BLOCKS, ROWS, CELLS), jnp.float32)] * 2
+        + [pltpu.SemaphoreType.DMA((2 * BLOCKS,)), LIVE, PARTNER, JACOBIAN, pltpu.SemaphoreType.DMA((3,))],
+        name="final", out_specs=[HBM] * 2
     )(live_rows, partner, row_jacobian, state, viscosity, local_step, spatial, back, ghosts2)
     return new_state, residual
 

time: 67.8 us -> 65.4 us (0.965)
  local copies, waits for them, and re-layouts: 2.49 us -> 0.76 us
    unnamed x28 -> x26, local copies, waits for them, and re-layouts: 2.45 us -> 0.73 us
where the time goes in v2:
time: 65.4 us; the launch traced here: 64.2 us
  starting transfers between devices  27.3 us (42%)
  waiting for transfers between devices  23.1 us (35%)
  Pallas kernels  12.1 us (19%)
  between operations  0.85 us (1%)
  local copies, waits for them, and re-layouts  0.76 us (1%)
    ppermute x10, waiting for transfers between devices, moved(): return lax.ppermute(array, 'blk', pairs)  17.2 us
    ppermute x10, starting transfers between devices, moved(): return lax.ppermute(array, 'blk', pairs)  13 us
    all_to_all x1, starting transfers between devices, per_device(): lax.all_to_all(chunks, 'inst', 0, 0, tiled=True).reshape(INST, SENT, CELLS)  9.73 us
    all_to_all x1, starting transfers between devices, per_device(): back = lax.all_to_all(sent, 'inst', 0, 0, tiled=True)  4.62 us
    pallas_call x1, Pallas kernels, per_device(): call(spatial_kernel, [(VARS, BLOCKS, ROWS, CELLS), (FACES * VARS, CELLS)]...  4.52 us
    all_to_all x1, waiting for transfers between devices, per_device(): lax.all_to_all(chunks, 'inst', 0, 0, tiled=True).reshape(INST, SENT, CELLS)  4.12 us
    pallas_call x1, Pallas kernels, per_device(): call(slab_kernel, [(INST, MAIN, CELLS)], [HBM, HBM, HBM, VMEM, VMEM, VMEM...  2.74 us
    pallas_call x1, Pallas kernels, per_device(): call(pack_kernel, [(INST, SENT // SLAB, SLAB, CELLS), (FACES * VARS, CELL...  2.26 us
  transfers between devices with their start and end apart: 12, of which 8 were waited for; matrix products, arithmetic and copies ran while one was open for 0% of the time, Pallas kernels for 8%

profile of v2, /device:TPU:6, one launch (start us, length us, event | category | flops | bytes accessed | tf_op | source)
XLA Modules:
  0.0 64.2 jit_solution(12683799904555590626)
XLA Ops:
  0.6 2.3 %pack.1 = (f32[16,7,16,128]{3,2,1,0:T(8,128)}, f32[20,128]{1,0:T(8,128)}) custom-call(s32[32]{0:T(128)} %live_in.5, f32[1,5,2,128,128]{4,3,2,1,0:T(8,128)} %state_ref.5), custom_call_target="tpu_custom_call" | custom-call | tf_op jit(solution)/shard_map/pack/pallas_call | solution.py:380
  2.9 9.7 %all-to-all-start = ((f32[16,7,16,128]{3,2,1,0:T(8,128)}), f32[16,7,16,128]{3,2,1,0:T(8,128)S(1)}, u32[]{:S(2)}, u32[]{:S(2)}) async-start(f32[16,7,16,128]{3,2,1,0:T(8,128)} %get-tuple-element.8), calls=%async_computation | async-start | bytes 1835008 | tf_op jit(solution)/shard_map/all_to_all | solution.py:384
  12.7 3.0 %collective-permute-start = (f32[1,20,128]{2,1,0:T(8,128)S(1)}, f32[1,20,128]{2,1,0:T(8,128)S(1)}, u32[]{:S(2)}, u32[]{:S(2)}) collective-permute-start(f32[1,20,128]{2,1,0:T(8,128)S(1)} %bitcast.11), channel_id=1, source_target_pairs={{8,0},{9,1},{10,2},{11,3},{12,4},{13,5},{14,6},{15,7},{0,8},{1,9},... | collective-permute-start | bytes 30728 | tf_op jit(solution)/shard_map/ppermute | solution.py:370
  15.7 2.3 %collective-permute-done = f32[1,20,128]{2,1,0:T(8,128)S(1)} collective-permute-done((f32[1,20,128]{2,1,0:T(8,128)S(1)}, f32[1,20,128]{2,1,0:T(8,128)S(1)}, u32[]{:S(2)}, u32[]{:S(2)}) %collective-permute-start) | collective-permute-done | bytes 10272 | tf_op jit(solution)/shard_map/ppermute | solution.py:370
  18.0 0.5 collective-permute-start.3
  18.4 2.4 %collective-permute-start.2 = (f32[2,20,128]{2,1,0:T(8,128)S(1)}, f32[2,20,128]{2,1,0:T(8,128)S(1)}, u32[]{:S(2)}, u32[]{:S(2)}) collective-permute-start(f32[2,20,128]{2,1,0:T(8,128)S(1)} %pad_maximum_fusion.1), channel_id=1, source_target_pairs={{4,0},{5,1},{6,2},{7,3},{0,4},{1,5},{2,6},{3,7},{12,8},{13,9},{14,... | collective-permute-start | bytes 61448 | tf_op jit(solution)/shard_map/ppermute | solution.py:370
  20.9 5.0 %collective-permute-done.1 = f32[2,20,128]{2,1,0:T(8,128)S(1)} collective-permute-done((f32[2,20,128]{2,1,0:T(8,128)S(1)}, f32[2,20,128]{2,1,0:T(8,128)S(1)}, u32[]{:S(2)}, u32[]{:S(2)}) %collective-permute-start.1) | collective-permute-done | bytes 20512 | tf_op jit(solution)/shard_map/ppermute | solution.py:370
  26.0 0.1 collective-permute-start.4
  26.1 1.3 %collective-permute-done.4 = f32[8,20,128]{2,1,0:T(8,128)S(1)} collective-permute-done((f32[8,20,128]{2,1,0:T(8,128)S(1)}, f32[8,20,128]{2,1,0:T(8,128)S(1)}, u32[]{:S(2)}, u32[]{:S(2)}) %collective-permute-start.4) | collective-permute-done | bytes 81952 | tf_op jit(solution)/shard_map/ppermute | solution.py:370
  27.4 0.6 copy-done.3
  28.1 4.5 %spatial.1 = (f32[5,2,128,128]{3,2,1,0:T(8,128)S(1)}, f32[20,128]{1,0:T(8,128)S(1)}) custom-call(s32[32]{0:T(128)S(1)} %copy-done.5, s32[64]{0:T(128)S(1)} %copy-done.7, f32[5,5]{1,0:T(8,128)S(1)} %copy-done.3, f32[5,5]{1,0:T(8,128)S(1)} %copy-done.4, f32[1,5,2,128,128]{4,3,2,1,0:T(8,128)S(1)} %copy-done, f32[2,128,128]{2,1,0:T(8,128)S(1)} %copy-done.2, ...), custom_call_target="tpu_custom_call" | custom-call | tf_op jit(solution)/shard_map/spatial/pallas_call | solution.py:386
  32.6 4.1 %all-to-all-done = f32[16,7,16,128]{3,2,1,0:T(8,128)S(1)} async-done(((f32[16,7,16,128]{3,2,1,0:T(8,128)}), f32[16,7,16,128]{3,2,1,0:T(8,128)S(1)}, u32[]{:S(2)}, u32[]{:S(2)}) %all-to-all-start) | async-done | bytes 917536 | tf_op jit(solution)/shard_map/all_to_all | solution.py:384
  36.7 2.7 %slab.1 = f32[16,80,128]{2,1,0:T(8,128)} custom-call(s32[32]{0:T(128)S(1)} %copy-done.5, f32[5,5]{1,0:T(8,128)S(1)} %copy-done.3, f32[5,5]{1,0:T(8,128)S(1)} %copy-done.4, f32[16,112,128]{2,1,0:T(8,128)S(1)} %bitcast.7, f32[2,128,128]{2,1,0:T(8,128)S(1)} %copy-done.2, f32[2,128,128]{2,1,0:T(8,128)S(1)} %copy-done.1), custom_call_target="tpu_custom_call" | custom-call | tf_op jit(solution)/shard_map/slab/pallas_call | solution.py:394
  39.5 4.6 %all-to-all-start.1 = ((f32[16,80,128]{2,1,0:T(8,128)}), f32[16,80,128]{2,1,0:T(8,128)S(1)}, u32[]{:S(2)}, u32[]{:S(2)}) async-start(f32[16,80,128]{2,1,0:T(8,128)} %slab.1), calls=%async_computation.1 | async-start | bytes 1310720 | tf_op jit(solution)/shard_map/all_to_all | solution.py:398
  44.1 0.7 %faces.1 = f32[40,128]{1,0:T(8,128)S(1)} custom-call(s32[32]{0:T(128)S(1)} %copy-done.5, f32[16,16]{1,0:T(8,128)S(1)} %copy-done.6, f32[16,112,128]{2,1,0:T(8,128)S(1)} %bitcast.8, f32[20,128]{1,0:T(8,128)S(1)} %get-tuple-element.13.half_ref, f32[2,128,128]{2,1,0:T(8,128)S(1)} %copy-done.1), custom_call_target="tpu_custom_call" | custom-call | tf_op jit(solution)/shard_map/faces/pallas_call | solution.py:400
  44.8 3.4 %collective-permute-start.5 = (f32[1,40,128]{2,1,0:T(8,128)S(1)}, f32[1,40,128]{2,1,0:T(8,128)S(1)}, u32[]{:S(2)}, u32[]{:S(2)}) collective-permute-start(f32[1,40,128]{2,1,0:T(8,128)S(1)} %bitcast.9), channel_id=1, source_target_pairs={{8,0},{9,1},{10,2},{11,3},{12,4},{13,5},{14,6},{15,7},{0,8},{1,9},... | collective-permute-start | bytes 61448 | tf_op jit(solution)/shard_map/ppermute | solution.py:370
  48.2 2.0 %collective-permute-done.5 = f32[1,40,128]{2,1,0:T(8,128)S(1)} collective-permute-done((f32[1,40,128]{2,1,0:T(8,128)S(1)}, f32[1,40,128]{2,1,0:T(8,128)S(1)}, u32[]{:S(2)}, u32[]{:S(2)}) %collective-permute-start.5) | collective-permute-done | bytes 20512 | tf_op jit(solution)/shard_map/ppermute | solution.py:370
  50.2 0.5 collective-permute-start.8
  50.7 3.1 %collective-permute-start.7 = (f32[2,40,128]{2,1,0:T(8,128)S(1)}, f32[2,40,128]{2,1,0:T(8,128)S(1)}, u32[]{:S(2)}, u32[]{:S(2)}) collective-permute-start(f32[2,40,128]{2,1,0:T(8,128)S(1)} %pad_maximum_fusion), channel_id=1, source_target_pairs={{4,0},{5,1},{6,2},{7,3},{0,4},{1,5},{2,6},{3,7},{12,8},{13,9},{14,... | collective-permute-start | bytes 122888 | tf_op jit(solution)/shard_map/ppermute | solution.py:370
  53.8 5.2 %collective-permute-done.6 = f32[2,40,128]{2,1,0:T(8,128)S(1)} collective-permute-done((f32[2,40,128]{2,1,0:T(8,128)S(1)}, f32[2,40,128]{2,1,0:T(8,128)S(1)}, u32[]{:S(2)}, u32[]{:S(2)}) %collective-permute-start.6) | collective-permute-done | bytes 40992 | tf_op jit(solution)/shard_map/ppermute | solution.py:370
  59.0 0.1 collective-permute-start.9
  59.1 1.4 %collective-permute-done.9 = f32[8,40,128]{2,1,0:T(8,128)S(1)} collective-permute-done((f32[8,40,128]{2,1,0:T(8,128)S(1)}, f32[8,40,128]{2,1,0:T(8,128)S(1)}, u32[]{:S(2)}, u32[]{:S(2)}) %collective-permute-start.9) | collective-permute-done | bytes 163872 | tf_op jit(solution)/shard_map/ppermute | solution.py:370
  60.5 1.8 %all-to-all-done.1.got_ref = f32[16,80,128]{2,1,0:T(8,128)S(1)} async-done(((f32[16,80,128]{2,1,0:T(8,128)}), f32[16,80,128]{2,1,0:T(8,128)S(1)}, u32[]{:S(2)}, u32[]{:S(2)}) %all-to-all-start.1) | async-done | bytes 655392 | tf_op jit(solution)/shard_map/all_to_all | solution.py:398
  62.3 1.8 %final.1 = (f32[1,5,2,128,128]{4,3,2,1,0:T(8,128)}, f32[1,5,2,128,128]{4,3,2,1,0:T(8,128)}) custom-call(s32[32]{0:T(128)S(1)} %copy-done.5, s32[64]{0:T(128)S(1)} %copy-done.7, f32[5,5]{1,0:T(8,128)S(1)} %copy-done.3, f32[1,5,2,128,128]{4,3,2,1,0:T(8,128)S(1)} %copy-done, f32[2,128,128]{2,1,0:T(8,128)S(1)} %copy-done.2, f32[2,128,128]{2,1,0:T(8,128)S(1)} %copy-done.1, ...), custom_call_target="tpu_custom_call" | custom-call | tf_op jit(solution)/shard_map/final/pallas_call | solution.py:404
  (37 shorter events, 0.2 us)
Async XLA Ops:
  2.9 9.8 %copy-start.8 = (f32[20,128]{1,0:T(8,128)S(1)}, f32[20,128]{1,0:T(8,128)}, u32[]{:S(2)}) copy-start(f32[20,128]{1,0:T(8,128)} %get-tuple-element.9) | copy-start | bytes 30724
  2.9 24.5 %copy-start = (f32[1,5,2,128,128]{4,3,2,1,0:T(8,128)S(1)}, f32[1,5,2,128,128]{4,3,2,1,0:T(8,128)}, u32[]{:S(2)}) copy-start(f32[1,5,2,128,128]{4,3,2,1,0:T(8,128)} %state_ref.5) | copy-start | bytes 1966084
  2.9 33.8 %all-to-all-start = ((f32[16,7,16,128]{3,2,1,0:T(8,128)}), f32[16,7,16,128]{3,2,1,0:T(8,128)S(1)}, u32[]{:S(2)}, u32[]{:S(2)}) async-start(f32[16,7,16,128]{3,2,1,0:T(8,128)} %get-tuple-element.8), calls=%async_computation | async-start | bytes 1835008 | tf_op jit(solution)/shard_map/all_to_all | solution.py:384
  12.7 5.3 %collective-permute-start = (f32[1,20,128]{2,1,0:T(8,128)S(1)}, f32[1,20,128]{2,1,0:T(8,128)S(1)}, u32[]{:S(2)}, u32[]{:S(2)}) collective-permute-start(f32[1,20,128]{2,1,0:T(8,128)S(1)} %bitcast.11), channel_id=1, source_target_pairs={{8,0},{9,1},{10,2},{11,3},{12,4},{13,5},{14,6},{15,7},{0,8},{1,9},... | collective-permute-start | bytes 30728 | tf_op jit(solution)/shard_map/ppermute | solution.py:370
  18.0 8.0 %collective-permute-start.3 = (f32[2,20,128]{2,1,0:T(8,128)S(1)}, f32[2,20,128]{2,1,0:T(8,128)S(1)}, u32[]{:S(2)}, u32[]{:S(2)}) collective-permute-start(f32[2,20,128]{2,1,0:T(8,128)S(1)} %pad_maximum_fusion.1), channel_id=1, source_target_pairs={{6,0},{7,1},{0,2},{1,3},{2,4},{3,5},{4,6},{5,7},{14,8},{15,9},{8,1... | collective-permute-start | bytes 61448 | tf_op jit(solution)/shard_map/ppermute | solution.py:370
  18.4 7.5 %collective-permute-start.2 = (f32[2,20,128]{2,1,0:T(8,128)S(1)}, f32[2,20,128]{2,1,0:T(8,128)S(1)}, u32[]{:S(2)}, u32[]{:S(2)}) collective-permute-start(f32[2,20,128]{2,1,0:T(8,128)S(1)} %pad_maximum_fusion.1), channel_id=1, source_target_pairs={{4,0},{5,1},{6,2},{7,3},{0,4},{1,5},{2,6},{3,7},{12,8},{13,9},{14,... | collective-permute-start | bytes 61448 | tf_op jit(solution)/shard_map/ppermute | solution.py:370
  20.9 5.0 %collective-permute-start.1 = (f32[2,20,128]{2,1,0:T(8,128)S(1)}, f32[2,20,128]{2,1,0:T(8,128)S(1)}, u32[]{:S(2)}, u32[]{:S(2)}) collective-permute-start(f32[2,20,128]{2,1,0:T(8,128)S(1)} %pad_maximum_fusion.1), channel_id=1, source_target_pairs={{2,0},{3,1},{4,2},{5,3},{6,4},{7,5},{0,6},{1,7},{10,8},{11,9},{12,... | collective-permute-start | bytes 61448 | tf_op jit(solution)/shard_map/ppermute | solution.py:370
  25.9 1.5 %copy-start.1 = (f32[2,128,128]{2,1,0:T(8,128)S(1)}, f32[2,128,128]{2,1,0:T(8,128)}, u32[]{:S(2)}) copy-start(f32[2,128,128]{2,1,0:T(8,128)} %step_ref.7) | copy-start | bytes 393220
  25.9 1.5 %copy-start.2 = (f32[2,128,128]{2,1,0:T(8,128)S(1)}, f32[2,128,128]{2,1,0:T(8,128)}, u32[]{:S(2)}) copy-start(f32[2,128,128]{2,1,0:T(8,128)} %visc_ref.5) | copy-start | bytes 393220
  26.0 1.4 %collective-permute-start.4 = (f32[8,20,128]{2,1,0:T(8,128)S(1)}, f32[8,20,128]{2,1,0:T(8,128)S(1)}, u32[]{:S(2)}, u32[]{:S(2)}) collective-permute-start(f32[8,20,128]{2,1,0:T(8,128)S(1)} %get-tuple-element.20), channel_id=1, source_target_pairs={{1,0},{0,1},{3,2},{2,3},{5,4},{4,5},{7,6},{6,7},{9,8},{8,9},{11,10... | collective-permute-start | bytes 245768 | tf_op jit(solution)/shard_map/ppermute | solution.py:370
  27.4 0.7 %copy-start.3 = (f32[5,5]{1,0:T(8,128)S(1)}, f32[5,5]{1,0:T(8,128)}, u32[]{:S(2)}) copy-start(f32[5,5]{1,0:T(8,128)} %row_in.3) | copy-start | bytes 304
  27.4 0.7 %copy-start.4 = (f32[5,5]{1,0:T(8,128)S(1)}, f32[5,5]{1,0:T(8,128)}, u32[]{:S(2)}) copy-start(f32[5,5]{1,0:T(8,128)} %cell_in.1) | copy-start | bytes 304
  27.4 0.7 %copy-start.5 = (s32[32]{0:T(128)S(1)}, s32[32]{0:T(128)}, u32[]{:S(2)}) copy-start(s32[32]{0:T(128)} %live_in.5) | copy-start | bytes 388
  27.4 0.7 %copy-start.7 = (s32[64]{0:T(128)S(1)}, s32[64]{0:T(128)}, u32[]{:S(2)}) copy-start(s32[64]{0:T(128)} %partner_in.1) | copy-start | bytes 772
  39.5 4.6 %copy-start.6 = (f32[16,16]{1,0:T(8,128)S(1)}, f32[16,16]{1,0:T(8,128)}, u32[]{:S(2)}) copy-start(f32[16,16]{1,0:T(8,128)} %constant.2.clone.weights_ref) | copy-start | bytes 3076
  39.5 22.9 %all-to-all-start.1 = ((f32[16,80,128]{2,1,0:T(8,128)}), f32[16,80,128]{2,1,0:T(8,128)S(1)}, u32[]{:S(2)}, u32[]{:S(2)}) async-start(f32[16,80,128]{2,1,0:T(8,128)} %slab.1), calls=%async_computation.1 | async-start | bytes 1310720 | tf_op jit(solution)/shard_map/all_to_all | solution.py:398
  44.8 5.4 %collective-permute-start.5 = (f32[1,40,128]{2,1,0:T(8,128)S(1)}, f32[1,40,128]{2,1,0:T(8,128)S(1)}, u32[]{:S(2)}, u32[]{:S(2)}) collective-permute-start(f32[1,40,128]{2,1,0:T(8,128)S(1)} %bitcast.9), channel_id=1, source_target_pairs={{8,0},{9,1},{10,2},{11,3},{12,4},{13,5},{14,6},{15,7},{0,8},{1,9},... | collective-permute-start | bytes 61448 | tf_op jit(solution)/shard_map/ppermute | solution.py:370
  50.2 8.8 %collective-permute-start.8 = (f32[2,40,128]{2,1,0:T(8,128)S(1)}, f32[2,40,128]{2,1,0:T(8,128)S(1)}, u32[]{:S(2)}, u32[]{:S(2)}) collective-permute-start(f32[2,40,128]{2,1,0:T(8,128)S(1)} %pad_maximum_fusion), channel_id=1, source_target_pairs={{6,0},{7,1},{0,2},{1,3},{2,4},{3,5},{4,6},{5,7},{14,8},{15,9},{8,1... | collective-permute-start | bytes 122888 | tf_op jit(solution)/shard_map/ppermute | solution.py:370
  50.7 8.3 %collective-permute-start.7 = (f32[2,40,128]{2,1,0:T(8,128)S(1)}, f32[2,40,128]{2,1,0:T(8,128)S(1)}, u32[]{:S(2)}, u32[]{:S(2)}) collective-permute-start(f32[2,40,128]{2,1,0:T(8,128)S(1)} %pad_maximum_fusion), channel_id=1, source_target_pairs={{4,0},{5,1},{6,2},{7,3},{0,4},{1,5},{2,6},{3,7},{12,8},{13,9},{14,... | collective-permute-start | bytes 122888 | tf_op jit(solution)/shard_map/ppermute | solution.py:370
  53.8 5.2 %collective-permute-start.6 = (f32[2,40,128]{2,1,0:T(8,128)S(1)}, f32[2,40,128]{2,1,0:T(8,128)S(1)}, u32[]{:S(2)}, u32[]{:S(2)}) collective-permute-start(f32[2,40,128]{2,1,0:T(8,128)S(1)} %pad_maximum_fusion), channel_id=1, source_target_pairs={{2,0},{3,1},{4,2},{5,3},{6,4},{7,5},{0,6},{1,7},{10,8},{11,9},{12,... | collective-permute-start | bytes 122888 | tf_op jit(solution)/shard_map/ppermute | solution.py:370
  59.0 1.5 %collective-permute-start.9 = (f32[8,40,128]{2,1,0:T(8,128)S(1)}, f32[8,40,128]{2,1,0:T(8,128)S(1)}, u32[]{:S(2)}, u32[]{:S(2)}) collective-permute-start(f32[8,40,128]{2,1,0:T(8,128)S(1)} %get-tuple-element.14), channel_id=1, source_target_pairs={{1,0},{0,1},{3,2},{2,3},{5,4},{4,5},{7,6},{6,7},{9,8},{8,9},{11,10... | collective-permute-start | bytes 491528 | tf_op jit(solution)/shard_map/ppermute | solution.py:370

commit v3 on v2

--- a/solution.py
+++ b/solution.py
@@ -1,4 +1,4 @@
-import functools
+import itertools
 import math
 
 import jax
@@ -19,8 +19,10 @@
 SMEM = pl.BlockSpec(memory_space=pltpu.SMEM)
 HBM = pl.BlockSpec(memory_space=pltpu.HBM)
 
+SIZES = {"y": 2, "x": 4, "core": 2}
+ORDER = (("y", "core",), ("x",),)
+ORDER2 = (("y", "core",), ("x",),)
 LIVE = pltpu.SMEM((32,), jnp.int32)
-PARTNER = pltpu.SMEM((64,), jnp.int32)
 JACOBIAN = pltpu.SMEM((VARS, VARS), jnp.float32)
 
 
@@ -140,18 +142,24 @@
                 chunks_ref[i, VARS, VARS + v : VARS + v + 1, :] = row_of(v, b, (j + 1) * SLAB)
 
 
-def ghost_place(partner_ref, face):
+def ghost_place(partner_ref, face, order):
     me = lax.axis_index("blk")
     other = partner_ref[me * FACES + face]
     device, local = other // FACES, other % FACES
-    core = (device % 2 + me % 2) % 2
-    x = ((device // 2) % 4 - (me // 2) % 4 + 4) % 4
-    y = (device // 8 + me // 8) % 2
-    return (core * 4 + x) * 2 + y, local
+    away = {
+        "core": (device % 2 + me % 2) % 2,
+        "x": ((device // 2) % 4 - (me // 2) % 4 + 4) % 4,
+        "y": (device // 8 + me // 8) % 2,
+    }
+    place = 0
+    for stage in reversed(order):
+        for axis in stage:
+            place = place * SIZES[axis] + away[axis]
+    return place, local
 
 
 def spatial_kernel(live_ref, partner_ref, row_ref, cell_ref, state_ref, visc_ref, step_ref, gathered_ref,
-                   spatial_ref, faces_ref, half_ref):
+                   spatial_ref, faces_ref, mask_ref, half_ref):
     first = lax.axis_index("blk") * BLOCKS
 
     def stencil(tiles, befores, afters, mask_n, mask_p, damp):
@@ -200,14 +208,17 @@
             half_ref[v, b, pl.ds(low, SLAB), :] = tiles[v] - scale * result[v]
 
     def write_spatial(b, low, tiles, result):
-        for v in range(VARS):
-            spatial_ref[v, b, pl.ds(low, SLAB), :] = result[v]
+        row = low + lax.broadcasted_iota(jnp.int32, (SLAB, CELLS), 0)
+        inside = row < live_ref[first + b]
+        mask_ref[b, pl.ds(low, SLAB), :] = jnp.where(inside, 1.0, 0.0)
+        for v in range(VARS):
+            spatial_ref[v, b, pl.ds(low, SLAB), :] = jnp.where(inside, result[v], 0.0)
 
     for b in range(BLOCKS):
         live = live_ref[first + b]
         sweep(read_state, write_half, b, live)
         for side in range(2):
-            place, local = ghost_place(partner_ref, 2 * b + side)
+            place, local = ghost_place(partner_ref, 2 * b + side, ORDER)
             row = (live - 1) if side else 0
             sign = 0.5 if side else -0.5
             rows = pl.ds(row, 1)
@@ -226,7 +237,7 @@
         sweep(read_half, write_spatial, b, live)
 
 
-def slab_kernel(live_in, row_in, cell_in, got_ref, visc_ref, step_ref, sent_ref, rate_ref, live_ref, row_ref, cell_ref, ready):
+def slab_kernel(live_in, row_in, cell_in, got_ref, visc_ref, step_ref, out_ref, sent_ref, rate_ref, live_ref, row_ref, cell_ref, ready, written):
     scalars = fetched([live_in, row_in, cell_in], [live_ref, row_ref, cell_ref], ready)
     i = lax.axis_index("inst")
     b, j = i // PER_BLOCK, i % PER_BLOCK
@@ -266,10 +277,15 @@
     scale_p = jnp.where(row > 0, step + step_p, 0.0)
     scale_e, scale_w = step + step_e, step + step_w
     damp = 0.5 * (0.25 + visc_ref[b, pl.ds(low, SLAB), :])
-    centre = 8.0 * step
+    centre = 1.0 - 8.0 * step * damp
+
+    def spread(coefficients):
+        return [[jnp.full((SLAB, CELLS), 0.25 * coefficients[u, v]) for v in range(VARS)] for u in range(VARS)]
+
+    scale_row, scale_cell = spread(row_ref), spread(cell_ref)
 
     def instance(t, carry):
-        across, along, smooth, rates = [], [], [], []
+        across, along, smooth = [], [], []
         for v in range(VARS):
             rate = rate_ref[t, pl.ds(v * SLAB, SLAB), :]
             n, p = row_shifts(rate, rate_ref[t, PREV + v : PREV + v + 1, :], rate_ref[t, NEXT + v : NEXT + v + 1, :])
@@ -277,17 +293,19 @@
             n, p, e, w = scale_n * n, scale_p * p, scale_e * e, scale_w * w
             across.append(n - p)
             along.append(e - w)
-            smooth.append((n + p) + (e + w) - centre * rate)
-            rates.append(rate)
+            smooth.append(centre * rate + damp * ((n + p) + (e + w)))
         for u in range(VARS):
             rows = pl.ds(u * SLAB, SLAB)
-            total = sent_ref[t, rows, :] + rates[u] + damp * smooth[u]
+            total = sent_ref[t, rows, :] + smooth[u]
             for v in range(VARS):
-                total = total - (0.25 * row_ref[u, v]) * across[v] - (0.25 * cell_ref[u, v]) * along[v]
+                total = total - scale_row[u][v] * across[v] - scale_cell[u][v] * along[v]
             sent_ref[t, rows, :] = total
         return carry
 
     lax.fori_loop(0, INST, instance, 0, unroll=4)
+    copy = pltpu.make_async_copy(sent_ref, out_ref, written.at[0])
+    copy.start()
+    copy.wait()
 
 
 def face_kernel(live_ref, weights_ref, got_ref, half_ref, step_ref, out_ref):
@@ -305,27 +323,13 @@
             out_ref[at : at + VARS, :] = half_ref[at : at + VARS, :] - scale * total[at : at + VARS, :]
 
 
-def final_kernel(live_in, partner_in, row_in, state_ref, visc_ref, step_ref, spatial_ref, got_ref, gathered_ref,
-                 new_out, residual_out, new_ref, residual_ref, written, live_ref, partner_ref, row_ref, ready):
-    for copy in fetched([live_in, partner_in, row_in], [live_ref, partner_ref, row_ref], ready):
-        copy.wait()
+def ghost_kernel(live_ref, partner_ref, row_ref, visc_ref, step_ref, gathered_ref, spatial_in, spatial_ref):
+    del spatial_in
     first = lax.axis_index("blk") * BLOCKS
-    copies = []
     for b in range(BLOCKS):
-        live = live_ref[first + b]
-        for j in range(PER_BLOCK):
-            low = j * SLAB
-            rows = slice(low, low + SLAB)
-            row = low + lax.broadcasted_iota(jnp.int32, (SLAB, CELLS), 0)
-            step = step_ref[b, rows, :]
-            for v in range(VARS):
-                total = got_ref[b * PER_BLOCK + j, v * SLAB : (v + 1) * SLAB, :] + spatial_ref[v, b, rows, :]
-                total = jnp.where(row < live, total, 0.0)
-                residual_ref[v, b, rows, :] = total
-                new_ref[v, b, rows, :] = state_ref[0, v, b, rows, :] - step * total
         for side in range(2):
-            place, local = ghost_place(partner_ref, 2 * b + side)
-            row = (live - 1) if side else 0
+            place, local = ghost_place(partner_ref, 2 * b + side, ORDER2)
+            row = (live_ref[first + b] - 1) if side else 0
             sign = 0.5 if side else -0.5
             rows = pl.ds(row, 1)
             step = step_ref[b, rows, :]
@@ -339,8 +343,23 @@
                 total = -damp * ghost[u]
                 for v in range(VARS):
                     total = total + (sign * row_ref[u, v]) * ghost[v]
-                residual_ref[u, b, rows, :] = residual_ref[u, b, rows, :] + total
-                new_ref[u, b, rows, :] = new_ref[u, b, rows, :] - step * total
+                spatial_ref[u, b, rows, :] = spatial_ref[u, b, rows, :] + total
+
+
+def final_kernel(state_ref, step_ref, mask_ref, spatial_ref, got_ref, new_out, residual_out, new_ref, residual_ref, written):
+    copies = []
+    for b in range(BLOCKS):
+
+        def tile(j, carry):
+            rows = pl.ds(pl.multiple_of(j * SLAB, SLAB), SLAB)
+            step, mask = step_ref[b, rows, :], mask_ref[b, rows, :]
+            for v in range(VARS):
+                total = mask * got_ref[b * PER_BLOCK + j, v * SLAB : (v + 1) * SLAB, :] + spatial_ref[v, b, rows, :]
+                residual_ref[v, b, rows, :] = total
+                new_ref[v, b, rows, :] = state_ref[0, v, b, rows, :] - step * total
+            return carry
+
+        lax.fori_loop(0, PER_BLOCK, tile, 0, unroll=2)
         for k, (held, out) in enumerate(((new_ref, new_out), (residual_ref, residual_out))):
             copy = pltpu.make_async_copy(held.at[:, b], out.at[0, :, b], written.at[2 * b + k])
             copy.start()
@@ -349,7 +368,7 @@
         copy.wait()
 
 
-def call(body, outs, in_specs, scratch=(), name=None, out_specs=None, limit=32):
+def call(body, outs, in_specs, scratch=(), name=None, out_specs=None, limit=32, aliases=None):
     return pl.pallas_call(
         body,
         out_shape=[jax.ShapeDtypeStruct(shape, jnp.float32) for shape in outs],
@@ -357,12 +376,13 @@
         out_specs=out_specs or [VMEM] * len(outs),
         scratch_shapes=list(scratch),
         compiler_params=pltpu.CompilerParams(vmem_limit_bytes=limit * 1024 * 1024),
+        input_output_aliases=aliases or {},
         name=name,
     )
 
 
-def gathered_over_blocks(value):
-    def moved(array, y, x, core):
+def gathered_over_blocks(value, order):
+    def moved(array, y=0, x=0, core=0):
         pairs = []
         for to in range(16):
             source = ((to // 8 + y) % 2) * 8 + (((to // 2) % 4 + x) % 4) * 2 + (to + core) % 2
@@ -370,9 +390,11 @@
         return lax.ppermute(array, "blk", pairs)
 
     value = value[None]
-    value = jnp.concatenate([value, moved(value, 1, 0, 0)])
-    value = jnp.concatenate([value] + [moved(value, 0, x, 0) for x in (1, 2, 3)])
-    return jnp.concatenate([value, moved(value, 0, 0, 1)])
+    for stage in order:
+        steps = itertools.product(*(range(SIZES[axis]) for axis in stage))
+        moves = [moved(value, **dict(zip(stage, step))) for step in list(steps)[1:]]
+        value = jnp.concatenate([value] + moves)
+    return value
 
 
 def per_device(state, row_jacobian, cell_jacobian, viscosity, local_step, live_rows, partner):
@@ -382,10 +404,10 @@
         [LIVE, pltpu.SemaphoreType.DMA((INST,)), pltpu.SemaphoreType.DMA((1,))], name="pack", limit=60
     )(live_rows, state)
     slabs = lax.all_to_all(chunks, "inst", 0, 0, tiled=True).reshape(INST, SENT, CELLS)
-    ghosts = gathered_over_blocks(faces)
-    spatial, half_faces = call(
+    ghosts = gathered_over_blocks(faces, ORDER)
+    spatial, half_faces, mask = call(
         spatial_kernel,
-        [(VARS, BLOCKS, ROWS, CELLS), (FACES * VARS, CELLS)],
+        [(VARS, BLOCKS, ROWS, CELLS), (FACES * VARS, CELLS), (BLOCKS, ROWS, CELLS)],
         [SMEM, SMEM, SMEM, SMEM, VMEM, VMEM, VMEM, VMEM],
         [pltpu.VMEM((VARS, BLOCKS, ROWS, CELLS), jnp.float32)],
         name="spatial",
@@ -393,20 +415,31 @@
     slabs, spatial = lax.optimization_barrier((slabs, spatial))
     (sent,) = call(
         slab_kernel, [(INST, MAIN, CELLS)], [HBM, HBM, HBM, VMEM, VMEM, VMEM],
-        [pltpu.VMEM((INST, 96, CELLS), jnp.float32), LIVE, JACOBIAN, JACOBIAN, pltpu.SemaphoreType.DMA((3,))], name="slab"
+        [
+            pltpu.VMEM((INST, MAIN, CELLS), jnp.float32),
+            pltpu.VMEM((INST, 96, CELLS), jnp.float32),
+            LIVE,
+            JACOBIAN,
+            JACOBIAN,
+            pltpu.SemaphoreType.DMA((3,)),
+            pltpu.SemaphoreType.DMA((1,)),
+        ],
+        name="slab", out_specs=[HBM],
     )(live_rows, row_jacobian, cell_jacobian, slabs, viscosity, local_step)
     back = lax.all_to_all(sent, "inst", 0, 0, tiled=True)
     weights = jnp.array([[spectral(t - s) for s in range(INST)] for t in range(INST)], jnp.float32)
     (faces2,) = call(
         face_kernel, [(2 * FACES * VARS, CELLS)], [SMEM, SMEM, VMEM, VMEM, VMEM], name="faces"
     )(live_rows, weights, slabs, half_faces, local_step)
-    ghosts2 = gathered_over_blocks(faces2)
+    ghosts2 = gathered_over_blocks(faces2, ORDER2)
+    (spatial,) = call(
+        ghost_kernel, [(VARS, BLOCKS, ROWS, CELLS)], [SMEM, SMEM, SMEM] + [VMEM] * 4, name="ghosts", aliases={6: 0}
+    )(live_rows, partner, row_jacobian, viscosity, local_step, ghosts2, spatial)
     new_state, residual = call(
-        final_kernel, [whole, whole], [HBM, HBM, HBM] + [VMEM] * 6,
-        [pltpu.VMEM((VARS, BLOCKS, ROWS, CELLS), jnp.float32)] * 2
-        + [pltpu.SemaphoreType.DMA((2 * BLOCKS,)), LIVE, PARTNER, JACOBIAN, pltpu.SemaphoreType.DMA((3,))],
-        name="final", out_specs=[HBM] * 2
-    )(live_rows, partner, row_jacobian, state, viscosity, local_step, spatial, back, ghosts2)
+        final_kernel, [whole, whole], [VMEM] * 5,
+        [pltpu.VMEM((VARS, BLOCKS, ROWS, CELLS), jnp.float32)] * 2 + [pltpu.SemaphoreType.DMA((2 * BLOCKS,))],
+        name="final", out_specs=[HBM] * 2,
+    )(state, local_step, mask, spatial, back)
     return new_state, residual
 
 

time: 65.4 us -> 64.1 us (0.980); the launches traced: 64.2 us -> 63.6 us
  waiting for transfers between devices: 23.1 us -> 22.2 us
    ppermute x10 -> x12, waiting for transfers between devices: 17.2 us -> 18.6 us  [moved(): return lax.ppermute(array, 'blk', pairs)]
    all_to_all x1, waiting for transfers between devices: 1.78 us -> 0.64 us  [per_device(): back = lax.all_to_all(sent, 'inst', 0, 0, tiled=True)]
    all_to_all x1, waiting for transfers between devices: 4.12 us -> 3 us  [per_device(): lax.all_to_all(chunks, 'inst', 0, 0, tiled=True).reshape(INST, SENT, CELLS)]
    pallas_call x2 -> x3, Pallas kernels: 6.35 us -> 6.54 us  [the longest x1 4.55 us: per_device(): call(spatial_kernel, [(VARS, BLOCKS, ROWS, CELLS), (FACES * VARS, CELLS),...]
    ppermute x10 -> x12, starting transfers between devices: 13 us -> 12.9 us  [moved(): return lax.ppermute(array, 'blk', pairs)]
  transfers between devices with their start and end apart: 12 -> 14, of which waited for: 8 -> 8; matrix products, arithmetic and copies ran while one was open for 0% -> 0% of each run, Pallas kernels for 8% -> 10%
where the time goes in v3:
time: 64.1 us; the launch traced here: 63.6 us
  starting transfers between devices  27.7 us (43%)
  waiting for transfers between devices  22.2 us (35%)
  Pallas kernels  12.1 us (19%)
  between operations  0.89 us (1%)
  local copies, waits for them, and re-layouts  0.72 us (1%)
    ppermute x12, waiting for transfers between devices, moved(): return lax.ppermute(array, 'blk', pairs)  18.6 us
    ppermute x12, starting transfers between devices, moved(): return lax.ppermute(array, 'blk', pairs)  12.9 us
    all_to_all x1, starting transfers between devices, per_device(): lax.all_to_all(chunks, 'inst', 0, 0, tiled=True).reshape(INST, SENT, CELLS)  9.73 us
    all_to_all x1, starting transfers between devices, per_device(): back = lax.all_to_all(sent, 'inst', 0, 0, tiled=True)  5.12 us
    pallas_call x1, Pallas kernels, per_device(): call(spatial_kernel, [(VARS, BLOCKS, ROWS, CELLS), (FACES * VARS, CELLS),...  4.55 us
    all_to_all x1, waiting for transfers between devices, per_device(): lax.all_to_all(chunks, 'inst', 0, 0, tiled=True).reshape(INST, SENT, CELLS)  3 us
    pallas_call x1, Pallas kernels, per_device(): call(slab_kernel, [(INST, MAIN, CELLS)], [HBM, HBM, HBM, VMEM, VMEM, VMEM...  2.58 us
    pallas_call x1, Pallas kernels, per_device(): call(pack_kernel, [(INST, SENT // SLAB, SLAB, CELLS), (FACES * VARS, CELL...  2.26 us
  transfers between devices with their start and end apart: 14, of which 8 were waited for; matrix products, arithmetic and copies ran while one was open for 0% of the time, Pallas kernels for 10%

profile of v3, /device:TPU:6, one launch (start us, length us, event | category | flops | bytes accessed | tf_op | source)
XLA Modules:
  0.0 63.6 jit_solution(7936598220225834839)
XLA Ops:
  0.6 2.3 %pack.1 = (f32[16,7,16,128]{3,2,1,0:T(8,128)}, f32[20,128]{1,0:T(8,128)}) custom-call(s32[32]{0:T(128)} %live_in.3, f32[1,5,2,128,128]{4,3,2,1,0:T(8,128)} %state_ref.5), custom_call_target="tpu_custom_call" | custom-call | tf_op jit(solution)/shard_map/pack/pallas_call | solution.py:402
  2.9 9.7 %all-to-all-start = ((f32[16,7,16,128]{3,2,1,0:T(8,128)}), f32[16,7,16,128]{3,2,1,0:T(8,128)S(1)}, u32[]{:S(2)}, u32[]{:S(2)}) async-start(f32[16,7,16,128]{3,2,1,0:T(8,128)} %get-tuple-element.11), calls=%async_computation | async-start | bytes 1835008 | tf_op jit(solution)/shard_map/all_to_all | solution.py:406
  12.7 2.1 %collective-permute-start.2 = (f32[1,20,128]{2,1,0:T(8,128)S(1)}, f32[1,20,128]{2,1,0:T(8,128)S(1)}, u32[]{:S(2)}, u32[]{:S(2)}) collective-permute-start(f32[1,20,128]{2,1,0:T(8,128)S(1)} %bitcast.11), channel_id=1, source_target_pairs={{9,0},{8,1},{11,2},{10,3},{13,4},{12,5},{15,6},{14,7},{1,8},{0,9},... | collective-permute-start | bytes 30728 | tf_op jit(solution)/shard_map/ppermute | solution.py:390
  14.8 0.9 %collective-permute-start.1 = (f32[1,20,128]{2,1,0:T(8,128)S(1)}, f32[1,20,128]{2,1,0:T(8,128)S(1)}, u32[]{:S(2)}, u32[]{:S(2)}) collective-permute-start(f32[1,20,128]{2,1,0:T(8,128)S(1)} %bitcast.12), channel_id=1, source_target_pairs={{8,0},{9,1},{10,2},{11,3},{12,4},{13,5},{14,6},{15,7},{0,8},{1,9},... | collective-permute-start | bytes 30728 | tf_op jit(solution)/shard_map/ppermute | solution.py:390
  16.1 1.4 %collective-permute-done.2 = f32[1,20,128]{2,1,0:T(8,128)S(1)} collective-permute-done((f32[1,20,128]{2,1,0:T(8,128)S(1)}, f32[1,20,128]{2,1,0:T(8,128)S(1)}, u32[]{:S(2)}, u32[]{:S(2)}) %collective-permute-start.2) | collective-permute-done | bytes 10272 | tf_op jit(solution)/shard_map/ppermute | solution.py:390
  17.5 2.6 %collective-permute-done.1 = f32[1,20,128]{2,1,0:T(8,128)S(1)} collective-permute-done((f32[1,20,128]{2,1,0:T(8,128)S(1)}, f32[1,20,128]{2,1,0:T(8,128)S(1)}, u32[]{:S(2)}, u32[]{:S(2)}) %collective-permute-start.1) | collective-permute-done | bytes 10272 | tf_op jit(solution)/shard_map/ppermute | solution.py:390
  20.7 2.4 %collective-permute-start.4 = (f32[4,20,128]{2,1,0:T(8,128)S(1)}, f32[4,20,128]{2,1,0:T(8,128)S(1)}, u32[]{:S(2)}, u32[]{:S(2)}) collective-permute-start(f32[4,20,128]{2,1,0:T(8,128)S(1)} %pad_maximum_fusion.1), channel_id=1, source_target_pairs={{4,0},{5,1},{6,2},{7,3},{0,4},{1,5},{2,6},{3,7},{12,8},{13,9},{14,... | collective-permute-start | bytes 122888 | tf_op jit(solution)/shard_map/ppermute | solution.py:390
  23.2 5.3 %collective-permute-done.3 = f32[4,20,128]{2,1,0:T(8,128)S(1)} collective-permute-done((f32[4,20,128]{2,1,0:T(8,128)S(1)}, f32[4,20,128]{2,1,0:T(8,128)S(1)}, u32[]{:S(2)}, u32[]{:S(2)}) %collective-permute-start.3) | collective-permute-done | bytes 40992 | tf_op jit(solution)/shard_map/ppermute | solution.py:390
  28.5 0.6 copy-done.3
  29.2 4.6 %spatial.1 = (f32[5,2,128,128]{3,2,1,0:T(8,128)S(1)}, f32[20,128]{1,0:T(8,128)S(1)}, f32[2,128,128]{2,1,0:T(8,128)S(1)}) custom-call(s32[32]{0:T(128)S(1)} %copy-done.5, s32[64]{0:T(128)S(1)} %copy-done.7, f32[5,5]{1,0:T(8,128)S(1)} %copy-done.3, f32[5,5]{1,0:T(8,128)S(1)} %copy-done.4, f32[1,5,2,128,128]{4,3,2,1,0:T(8,128)S(1)} %copy-done, ...), custom_call_target="tpu_custom_call" | custom-call | tf_op jit(solution)/shard_map/spatial/pallas_call | solution.py:408
  33.7 3.0 %all-to-all-done = f32[16,7,16,128]{3,2,1,0:T(8,128)S(1)} async-done(((f32[16,7,16,128]{3,2,1,0:T(8,128)}), f32[16,7,16,128]{3,2,1,0:T(8,128)S(1)}, u32[]{:S(2)}, u32[]{:S(2)}) %all-to-all-start) | async-done | bytes 917536 | tf_op jit(solution)/shard_map/all_to_all | solution.py:406
  36.7 2.6 %slab.1 = f32[16,80,128]{2,1,0:T(8,128)} custom-call(s32[32]{0:T(128)S(1)} %copy-done.5, f32[5,5]{1,0:T(8,128)S(1)} %copy-done.3, f32[5,5]{1,0:T(8,128)S(1)} %copy-done.4, f32[16,112,128]{2,1,0:T(8,128)S(1)} %bitcast.5, f32[2,128,128]{2,1,0:T(8,128)S(1)} %copy-done.2, f32[2,128,128]{2,1,0:T(8,128)S(1)} %copy-done.1), custom_call_target="tpu_custom_call" | custom-call | tf_op jit(solution)/shard_map/slab/pallas_call | solution.py:416
  39.3 5.1 %all-to-all-start.1 = ((f32[16,80,128]{2,1,0:T(8,128)}), f32[16,80,128]{2,1,0:T(8,128)S(1)}, u32[]{:S(2)}, u32[]{:S(2)}) async-start(f32[16,80,128]{2,1,0:T(8,128)} %slab.1), calls=%async_computation.1 | async-start | bytes 1310720 | tf_op jit(solution)/shard_map/all_to_all | solution.py:429
  44.5 0.7 %faces.1 = f32[40,128]{1,0:T(8,128)S(1)} custom-call(s32[32]{0:T(128)S(1)} %copy-done.5, f32[16,16]{1,0:T(8,128)S(1)} %copy-done.6, f32[16,112,128]{2,1,0:T(8,128)S(1)} %bitcast.6, f32[20,128]{1,0:T(8,128)S(1)} %get-tuple-element.14.half_ref, f32[2,128,128]{2,1,0:T(8,128)S(1)} %copy-done.1), custom_call_target="tpu_custom_call" | custom-call | tf_op jit(solution)/shard_map/faces/pallas_call | solution.py:431
  45.2 1.7 %collective-permute-start.8 = (f32[1,40,128]{2,1,0:T(8,128)S(1)}, f32[1,40,128]{2,1,0:T(8,128)S(1)}, u32[]{:S(2)}, u32[]{:S(2)}) collective-permute-start(f32[1,40,128]{2,1,0:T(8,128)S(1)} %bitcast.7), channel_id=1, source_target_pairs={{9,0},{8,1},{11,2},{10,3},{13,4},{12,5},{15,6},{14,7},{1,8},{0,9},... | collective-permute-start | bytes 61448 | tf_op jit(solution)/shard_map/ppermute | solution.py:390
  46.9 0.9 %collective-permute-start.7 = (f32[1,40,128]{2,1,0:T(8,128)S(1)}, f32[1,40,128]{2,1,0:T(8,128)S(1)}, u32[]{:S(2)}, u32[]{:S(2)}) collective-permute-start(f32[1,40,128]{2,1,0:T(8,128)S(1)} %bitcast.8), channel_id=1, source_target_pairs={{8,0},{9,1},{10,2},{11,3},{12,4},{13,5},{14,6},{15,7},{0,8},{1,9},... | collective-permute-start | bytes 61448 | tf_op jit(solution)/shard_map/ppermute | solution.py:390
  47.8 0.9 %collective-permute-start.6 = (f32[1,40,128]{2,1,0:T(8,128)S(1)}, f32[1,40,128]{2,1,0:T(8,128)S(1)}, u32[]{:S(2)}, u32[]{:S(2)}) collective-permute-start(f32[1,40,128]{2,1,0:T(8,128)S(1)} %bitcast.9), channel_id=1, source_target_pairs={{1,0},{0,1},{3,2},{2,3},{5,4},{4,5},{7,6},{6,7},{9,8},{8,9},{11,10... | collective-permute-start | bytes 61448 | tf_op jit(solution)/shard_map/ppermute | solution.py:390
  48.6 2.1 %collective-permute-done.8 = f32[1,40,128]{2,1,0:T(8,128)S(1)} collective-permute-done((f32[1,40,128]{2,1,0:T(8,128)S(1)}, f32[1,40,128]{2,1,0:T(8,128)S(1)}, u32[]{:S(2)}, u32[]{:S(2)}) %collective-permute-start.8) | collective-permute-done | bytes 20512 | tf_op jit(solution)/shard_map/ppermute | solution.py:390
  50.7 1.6 %collective-permute-done.7 = f32[1,40,128]{2,1,0:T(8,128)S(1)} collective-permute-done((f32[1,40,128]{2,1,0:T(8,128)S(1)}, f32[1,40,128]{2,1,0:T(8,128)S(1)}, u32[]{:S(2)}, u32[]{:S(2)}) %collective-permute-start.7) | collective-permute-done | bytes 20512 | tf_op jit(solution)/shard_map/ppermute | solution.py:390
  52.9 2.4 %collective-permute-start.10 = (f32[4,40,128]{2,1,0:T(8,128)S(1)}, f32[4,40,128]{2,1,0:T(8,128)S(1)}, u32[]{:S(2)}, u32[]{:S(2)}) collective-permute-start(f32[4,40,128]{2,1,0:T(8,128)S(1)} %pad_maximum_fusion), channel_id=1, source_target_pairs={{4,0},{5,1},{6,2},{7,3},{0,4},{1,5},{2,6},{3,7},{12,8},{13,9},{14,... | collective-permute-start | bytes 245768 | tf_op jit(solution)/shard_map/ppermute | solution.py:390
  55.3 5.6 %collective-permute-done.9 = f32[4,40,128]{2,1,0:T(8,128)S(1)} collective-permute-done((f32[4,40,128]{2,1,0:T(8,128)S(1)}, f32[4,40,128]{2,1,0:T(8,128)S(1)}, u32[]{:S(2)}, u32[]{:S(2)}) %collective-permute-start.9) | collective-permute-done | bytes 81952 | tf_op jit(solution)/shard_map/ppermute | solution.py:390
  61.0 0.8 %ghosts.1.spatial_ref = f32[5,2,128,128]{3,2,1,0:T(8,128)S(1)} custom-call(s32[32]{0:T(128)S(1)} %copy-done.5, s32[64]{0:T(128)S(1)} %copy-done.7, f32[5,5]{1,0:T(8,128)S(1)} %copy-done.3, f32[2,128,128]{2,1,0:T(8,128)S(1)} %copy-done.2, f32[2,128,128]{2,1,0:T(8,128)S(1)} %copy-done.1, ...), custom_call_target="tpu_custom_call", output_to_operand_aliasing={{}: (6, {})} | custom-call | tf_op jit(solution)/shard_map/ghosts/pallas_call | solution.py:435
  61.8 0.6 %all-to-all-done.1.got_ref = f32[16,80,128]{2,1,0:T(8,128)S(1)} async-done(((f32[16,80,128]{2,1,0:T(8,128)}), f32[16,80,128]{2,1,0:T(8,128)S(1)}, u32[]{:S(2)}, u32[]{:S(2)}) %all-to-all-start.1) | async-done | bytes 655392 | tf_op jit(solution)/shard_map/all_to_all | solution.py:429
  62.5 1.2 %final.1 = (f32[1,5,2,128,128]{4,3,2,1,0:T(8,128)}, f32[1,5,2,128,128]{4,3,2,1,0:T(8,128)}) custom-call(f32[1,5,2,128,128]{4,3,2,1,0:T(8,128)S(1)} %copy-done, f32[2,128,128]{2,1,0:T(8,128)S(1)} %copy-done.1, f32[2,128,128]{2,1,0:T(8,128)S(1)} %get-tuple-element.10.mask_ref, f32[5,2,128,128]{3,2,1,0:T(8,128)S(1)} %ghosts.1.spatial_ref, ...), custom_call_target="tpu_custom_call" | custom-call | tf_op jit(solution)/shard_map/final/pallas_call | solution.py:438
  (44 shorter events, 1.6 us)
Async XLA Ops:
  2.9 9.8 %copy-start.8 = (f32[20,128]{1,0:T(8,128)S(1)}, f32[20,128]{1,0:T(8,128)}, u32[]{:S(2)}) copy-start(f32[20,128]{1,0:T(8,128)} %get-tuple-element.9) | copy-start | bytes 30724
  2.9 25.6 %copy-start = (f32[1,5,2,128,128]{4,3,2,1,0:T(8,128)S(1)}, f32[1,5,2,128,128]{4,3,2,1,0:T(8,128)}, u32[]{:S(2)}) copy-start(f32[1,5,2,128,128]{4,3,2,1,0:T(8,128)} %state_ref.5) | copy-start | bytes 1966084
  2.9 33.8 %all-to-all-start = ((f32[16,7,16,128]{3,2,1,0:T(8,128)}), f32[16,7,16,128]{3,2,1,0:T(8,128)S(1)}, u32[]{:S(2)}, u32[]{:S(2)}) async-start(f32[16,7,16,128]{3,2,1,0:T(8,128)} %get-tuple-element.11), calls=%async_computation | async-start | bytes 1835008 | tf_op jit(solution)/shard_map/all_to_all | solution.py:406
  12.7 4.8 %collective-permute-start.2 = (f32[1,20,128]{2,1,0:T(8,128)S(1)}, f32[1,20,128]{2,1,0:T(8,128)S(1)}, u32[]{:S(2)}, u32[]{:S(2)}) collective-permute-start(f32[1,20,128]{2,1,0:T(8,128)S(1)} %bitcast.11), channel_id=1, source_target_pairs={{9,0},{8,1},{11,2},{10,3},{13,4},{12,5},{15,6},{14,7},{1,8},{0,9},... | collective-permute-start | bytes 30728 | tf_op jit(solution)/shard_map/ppermute | solution.py:390
  14.8 5.3 %collective-permute-start.1 = (f32[1,20,128]{2,1,0:T(8,128)S(1)}, f32[1,20,128]{2,1,0:T(8,128)S(1)}, u32[]{:S(2)}, u32[]{:S(2)}) collective-permute-start(f32[1,20,128]{2,1,0:T(8,128)S(1)} %bitcast.12), channel_id=1, source_target_pairs={{8,0},{9,1},{10,2},{11,3},{12,4},{13,5},{14,6},{15,7},{0,8},{1,9},... | collective-permute-start | bytes 30728 | tf_op jit(solution)/shard_map/ppermute | solution.py:390
  15.7 4.4 %collective-permute-start = (f32[1,20,128]{2,1,0:T(8,128)S(1)}, f32[1,20,128]{2,1,0:T(8,128)S(1)}, u32[]{:S(2)}, u32[]{:S(2)}) collective-permute-start(f32[1,20,128]{2,1,0:T(8,128)S(1)} %bitcast.13), channel_id=1, source_target_pairs={{1,0},{0,1},{3,2},{2,3},{5,4},{4,5},{7,6},{6,7},{9,8},{8,9},{11,10... | collective-permute-start | bytes 30728 | tf_op jit(solution)/shard_map/ppermute | solution.py:390
  20.1 8.4 %collective-permute-start.5 = (f32[4,20,128]{2,1,0:T(8,128)S(1)}, f32[4,20,128]{2,1,0:T(8,128)S(1)}, u32[]{:S(2)}, u32[]{:S(2)}) collective-permute-start(f32[4,20,128]{2,1,0:T(8,128)S(1)} %pad_maximum_fusion.1), channel_id=1, source_target_pairs={{6,0},{7,1},{0,2},{1,3},{2,4},{3,5},{4,6},{5,7},{14,8},{15,9},{8,1... | collective-permute-start | bytes 122888 | tf_op jit(solution)/shard_map/ppermute | solution.py:390
  20.7 7.7 %collective-permute-start.4 = (f32[4,20,128]{2,1,0:T(8,128)S(1)}, f32[4,20,128]{2,1,0:T(8,128)S(1)}, u32[]{:S(2)}, u32[]{:S(2)}) collective-permute-start(f32[4,20,128]{2,1,0:T(8,128)S(1)} %pad_maximum_fusion.1), channel_id=1, source_target_pairs={{4,0},{5,1},{6,2},{7,3},{0,4},{1,5},{2,6},{3,7},{12,8},{13,9},{14,... | collective-permute-start | bytes 122888 | tf_op jit(solution)/shard_map/ppermute | solution.py:390
  23.1 5.3 %collective-permute-start.3 = (f32[4,20,128]{2,1,0:T(8,128)S(1)}, f32[4,20,128]{2,1,0:T(8,128)S(1)}, u32[]{:S(2)}, u32[]{:S(2)}) collective-permute-start(f32[4,20,128]{2,1,0:T(8,128)S(1)} %pad_maximum_fusion.1), channel_id=1, source_target_pairs={{2,0},{3,1},{4,2},{5,3},{6,4},{7,5},{0,6},{1,7},{10,8},{11,9},{12,... | collective-permute-start | bytes 122888 | tf_op jit(solution)/shard_map/ppermute | solution.py:390
  23.1 5.4 %copy-start.1 = (f32[2,128,128]{2,1,0:T(8,128)S(1)}, f32[2,128,128]{2,1,0:T(8,128)}, u32[]{:S(2)}) copy-start(f32[2,128,128]{2,1,0:T(8,128)} %step_ref.9) | copy-start | bytes 393220
  23.1 5.4 %copy-start.2 = (f32[2,128,128]{2,1,0:T(8,128)S(1)}, f32[2,128,128]{2,1,0:T(8,128)}, u32[]{:S(2)}) copy-start(f32[2,128,128]{2,1,0:T(8,128)} %visc_ref.5) | copy-start | bytes 393220
  28.4 0.7 %copy-start.3 = (f32[5,5]{1,0:T(8,128)S(1)}, f32[5,5]{1,0:T(8,128)}, u32[]{:S(2)}) copy-start(f32[5,5]{1,0:T(8,128)} %row_in.1) | copy-start | bytes 304
  28.5 0.7 %copy-start.4 = (f32[5,5]{1,0:T(8,128)S(1)}, f32[5,5]{1,0:T(8,128)}, u32[]{:S(2)}) copy-start(f32[5,5]{1,0:T(8,128)} %cell_in.1) | copy-start | bytes 304
  28.5 0.7 %copy-start.5 = (s32[32]{0:T(128)S(1)}, s32[32]{0:T(128)}, u32[]{:S(2)}) copy-start(s32[32]{0:T(128)} %live_in.3) | copy-start | bytes 388
  28.5 0.7 %copy-start.7 = (s32[64]{0:T(128)S(1)}, s32[64]{0:T(128)}, u32[]{:S(2)}) copy-start(s32[64]{0:T(128)} %partner_ref.3) | copy-start | bytes 772
  39.3 5.1 %copy-start.6 = (f32[16,16]{1,0:T(8,128)S(1)}, f32[16,16]{1,0:T(8,128)}, u32[]{:S(2)}) copy-start(f32[16,16]{1,0:T(8,128)} %constant.2.clone.weights_ref) | copy-start | bytes 3076
  39.3 23.2 %all-to-all-start.1 = ((f32[16,80,128]{2,1,0:T(8,128)}), f32[16,80,128]{2,1,0:T(8,128)S(1)}, u32[]{:S(2)}, u32[]{:S(2)}) async-start(f32[16,80,128]{2,1,0:T(8,128)} %slab.1), calls=%async_computation.1 | async-start | bytes 1310720 | tf_op jit(solution)/shard_map/all_to_all | solution.py:429
  45.2 5.5 %collective-permute-start.8 = (f32[1,40,128]{2,1,0:T(8,128)S(1)}, f32[1,40,128]{2,1,0:T(8,128)S(1)}, u32[]{:S(2)}, u32[]{:S(2)}) collective-permute-start(f32[1,40,128]{2,1,0:T(8,128)S(1)} %bitcast.7), channel_id=1, source_target_pairs={{9,0},{8,1},{11,2},{10,3},{13,4},{12,5},{15,6},{14,7},{1,8},{0,9},... | collective-permute-start | bytes 61448 | tf_op jit(solution)/shard_map/ppermute | solution.py:390
  46.9 5.4 %collective-permute-start.7 = (f32[1,40,128]{2,1,0:T(8,128)S(1)}, f32[1,40,128]{2,1,0:T(8,128)S(1)}, u32[]{:S(2)}, u32[]{:S(2)}) collective-permute-start(f32[1,40,128]{2,1,0:T(8,128)S(1)} %bitcast.8), channel_id=1, source_target_pairs={{8,0},{9,1},{10,2},{11,3},{12,4},{13,5},{14,6},{15,7},{0,8},{1,9},... | collective-permute-start | bytes 61448 | tf_op jit(solution)/shard_map/ppermute | solution.py:390
  47.8 4.6 %collective-permute-start.6 = (f32[1,40,128]{2,1,0:T(8,128)S(1)}, f32[1,40,128]{2,1,0:T(8,128)S(1)}, u32[]{:S(2)}, u32[]{:S(2)}) collective-permute-start(f32[1,40,128]{2,1,0:T(8,128)S(1)} %bitcast.9), channel_id=1, source_target_pairs={{1,0},{0,1},{3,2},{2,3},{5,4},{4,5},{7,6},{6,7},{9,8},{8,9},{11,10... | collective-permute-start | bytes 61448 | tf_op jit(solution)/shard_map/ppermute | solution.py:390
  52.3 8.7 %collective-permute-start.11 = (f32[4,40,128]{2,1,0:T(8,128)S(1)}, f32[4,40,128]{2,1,0:T(8,128)S(1)}, u32[]{:S(2)}, u32[]{:S(2)}) collective-permute-start(f32[4,40,128]{2,1,0:T(8,128)S(1)} %pad_maximum_fusion), channel_id=1, source_target_pairs={{6,0},{7,1},{0,2},{1,3},{2,4},{3,5},{4,6},{5,7},{14,8},{15,9},{8,1... | collective-permute-start | bytes 245768 | tf_op jit(solution)/shard_map/ppermute | solution.py:390
  52.9 8.1 %collective-permute-start.10 = (f32[4,40,128]{2,1,0:T(8,128)S(1)}, f32[4,40,128]{2,1,0:T(8,128)S(1)}, u32[]{:S(2)}, u32[]{:S(2)}) collective-permute-start(f32[4,40,128]{2,1,0:T(8,128)S(1)} %pad_maximum_fusion), channel_id=1, source_target_pairs={{4,0},{5,1},{6,2},{7,3},{0,4},{1,5},{2,6},{3,7},{12,8},{13,9},{14,... | collective-permute-start | bytes 245768 | tf_op jit(solution)/shard_map/ppermute | solution.py:390
  55.3 5.7 %collective-permute-start.9 = (f32[4,40,128]{2,1,0:T(8,128)S(1)}, f32[4,40,128]{2,1,0:T(8,128)S(1)}, u32[]{:S(2)}, u32[]{:S(2)}) collective-permute-start(f32[4,40,128]{2,1,0:T(8,128)S(1)} %pad_maximum_fusion), channel_id=1, source_target_pairs={{2,0},{3,1},{4,2},{5,3},{6,4},{7,5},{0,6},{1,7},{10,8},{11,9},{12,... | collective-permute-start | bytes 245768 | tf_op jit(solution)/shard_map/ppermute | solution.py:390

commit v4 on v3

--- a/solution.py
+++ b/solution.py
@@ -34,6 +34,7 @@
 
 
 HALF = INST // 2
+GROUP = 4
 EVEN = [0.5 * (spectral(m) + spectral(m + HALF)) for m in range(HALF)]
 ODD = [0.5 * (spectral(m) - spectral(m + HALF)) for m in range(HALF)]
 
@@ -302,10 +303,19 @@
             sent_ref[t, rows, :] = total
         return carry
 
-    lax.fori_loop(0, INST, instance, 0, unroll=4)
-    copy = pltpu.make_async_copy(sent_ref, out_ref, written.at[0])
-    copy.start()
-    copy.wait()
+    def sent_copy(g):
+        part = pl.ds(pl.multiple_of(g * GROUP, GROUP), GROUP)
+        return pltpu.make_async_copy(sent_ref.at[part], out_ref.at[part], written.at[g])
+
+    def group(g, carry):
+        for k in range(GROUP):
+            instance(g * GROUP + k, 0)
+        sent_copy(g).start()
+        return carry
+
+    lax.fori_loop(0, INST // GROUP, group, 0)
+    for g in range(INST // GROUP):
+        sent_copy(g).wait()
 
 
 def face_kernel(live_ref, weights_ref, got_ref, half_ref, step_ref, out_ref):
@@ -347,25 +357,33 @@
 
 
 def final_kernel(state_ref, step_ref, mask_ref, spatial_ref, got_ref, new_out, residual_out, new_ref, residual_ref, written):
-    copies = []
-    for b in range(BLOCKS):
-
-        def tile(j, carry):
-            rows = pl.ds(pl.multiple_of(j * SLAB, SLAB), SLAB)
+    span = ROWS // 2
+
+    def out_copies(k):
+        b, rows = k // 2, pl.ds(pl.multiple_of((k % 2) * span, span), span)
+        return [
+            pltpu.make_async_copy(held.at[:, b, rows], out.at[0, :, b, rows], written.at[2 * k + n])
+            for n, (held, out) in enumerate(((new_ref, new_out), (residual_ref, residual_out)))
+        ]
+
+    def part(k, carry):
+        b = k // 2
+        for j in range(PER_BLOCK // 2):
+            slab = k * (PER_BLOCK // 2) + j
+            rows = pl.ds(pl.multiple_of((k % 2) * span + j * SLAB, SLAB), SLAB)
             step, mask = step_ref[b, rows, :], mask_ref[b, rows, :]
             for v in range(VARS):
-                total = mask * got_ref[b * PER_BLOCK + j, v * SLAB : (v + 1) * SLAB, :] + spatial_ref[v, b, rows, :]
+                total = mask * got_ref[slab, v * SLAB : (v + 1) * SLAB, :] + spatial_ref[v, b, rows, :]
                 residual_ref[v, b, rows, :] = total
                 new_ref[v, b, rows, :] = state_ref[0, v, b, rows, :] - step * total
-            return carry
-
-        lax.fori_loop(0, PER_BLOCK, tile, 0, unroll=2)
-        for k, (held, out) in enumerate(((new_ref, new_out), (residual_ref, residual_out))):
-            copy = pltpu.make_async_copy(held.at[:, b], out.at[0, :, b], written.at[2 * b + k])
+        for copy in out_copies(k):
             copy.start()
-            copies.append(copy)
-    for copy in copies:
-        copy.wait()
+        return carry
+
+    lax.fori_loop(0, 2 * BLOCKS, part, 0)
+    for k in range(2 * BLOCKS):
+        for copy in out_copies(k):
+            copy.wait()
 
 
 def call(body, outs, in_specs, scratch=(), name=None, out_specs=None, limit=32, aliases=None):
@@ -422,7 +440,7 @@
             JACOBIAN,
             JACOBIAN,
             pltpu.SemaphoreType.DMA((3,)),
-            pltpu.SemaphoreType.DMA((1,)),
+            pltpu.SemaphoreType.DMA((INST // GROUP,)),
         ],
         name="slab", out_specs=[HBM],
     )(live_rows, row_jacobian, cell_jacobian, slabs, viscosity, local_step)
@@ -437,7 +455,7 @@
     )(live_rows, partner, row_jacobian, viscosity, local_step, ghosts2, spatial)
     new_state, residual = call(
         final_kernel, [whole, whole], [VMEM] * 5,
-        [pltpu.VMEM((VARS, BLOCKS, ROWS, CELLS), jnp.float32)] * 2 + [pltpu.SemaphoreType.DMA((2 * BLOCKS,))],
+        [pltpu.VMEM((VARS, BLOCKS, ROWS, CELLS), jnp.float32)] * 2 + [pltpu.SemaphoreType.DMA((4 * BLOCKS,))],
         name="final", out_specs=[HBM] * 2,
     )(state, local_step, mask, spatial, back)
     return new_state, residual

time: 64.1 us -> 63.9 us (level)
  no operation moved by 1% of the time
where the time goes in v4:
time: 63.9 us; the launch traced here: 63.5 us
  starting transfers between devices  27.7 us (43%)
  waiting for transfers between devices  22.2 us (35%)
  Pallas kernels  11.9 us (19%)
  between operations  0.89 us (1%)
  local copies, waits for them, and re-layouts  0.72 us (1%)
    ppermute x12, waiting for transfers between devices, moved(): return lax.ppermute(array, 'blk', pairs)  18.6 us
    ppermute x12, starting transfers between devices, moved(): return lax.ppermute(array, 'blk', pairs)  12.9 us
    all_to_all x1, starting transfers between devices, per_device(): lax.all_to_all(chunks, 'inst', 0, 0, tiled=True).reshape(INST, SENT, CELLS)  9.73 us
    all_to_all x1, starting transfers between devices, per_device(): back = lax.all_to_all(sent, 'inst', 0, 0, tiled=True)  5.12 us
    pallas_call x1, Pallas kernels, per_device(): call(spatial_kernel, [(VARS, BLOCKS, ROWS, CELLS), (FACES * VARS, CELLS),...  4.55 us
    all_to_all x1, waiting for transfers between devices, per_device(): lax.all_to_all(chunks, 'inst', 0, 0, tiled=True).reshape(INST, SENT, CELLS)  3 us
    pallas_call x1, Pallas kernels, per_device(): call(slab_kernel, [(INST, MAIN, CELLS)], [HBM, HBM, HBM, VMEM, VMEM, VMEM...  2.44 us
    pallas_call x1, Pallas kernels, per_device(): call(pack_kernel, [(INST, SENT // SLAB, SLAB, CELLS), (FACES * VARS, CELL...  2.26 us
  transfers between devices with their start and end apart: 14, of which 8 were waited for; matrix products, arithmetic and copies ran while one was open for 0% of the time, Pallas kernels for 10%

profile of v4, /device:TPU:6, one launch (start us, length us, event | category | flops | bytes accessed | tf_op | source)
XLA Modules:
  0.0 63.5 jit_solution(8352912005121577164)
XLA Ops:
  0.6 2.3 %pack.1 = (f32[16,7,16,128]{3,2,1,0:T(8,128)}, f32[20,128]{1,0:T(8,128)}) custom-call(s32[32]{0:T(128)} %live_in.3, f32[1,5,2,128,128]{4,3,2,1,0:T(8,128)} %state_ref.5), custom_call_target="tpu_custom_call" | custom-call | tf_op jit(solution)/shard_map/pack/pallas_call | solution.py:420
  2.9 9.7 %all-to-all-start = ((f32[16,7,16,128]{3,2,1,0:T(8,128)}), f32[16,7,16,128]{3,2,1,0:T(8,128)S(1)}, u32[]{:S(2)}, u32[]{:S(2)}) async-start(f32[16,7,16,128]{3,2,1,0:T(8,128)} %get-tuple-element.11), calls=%async_computation | async-start | bytes 1835008 | tf_op jit(solution)/shard_map/all_to_all | solution.py:424
  12.7 2.1 %collective-permute-start.2 = (f32[1,20,128]{2,1,0:T(8,128)S(1)}, f32[1,20,128]{2,1,0:T(8,128)S(1)}, u32[]{:S(2)}, u32[]{:S(2)}) collective-permute-start(f32[1,20,128]{2,1,0:T(8,128)S(1)} %bitcast.11), channel_id=1, source_target_pairs={{9,0},{8,1},{11,2},{10,3},{13,4},{12,5},{15,6},{14,7},{1,8},{0,9},... | collective-permute-start | bytes 30728 | tf_op jit(solution)/shard_map/ppermute | solution.py:408
  14.8 0.9 %collective-permute-start.1 = (f32[1,20,128]{2,1,0:T(8,128)S(1)}, f32[1,20,128]{2,1,0:T(8,128)S(1)}, u32[]{:S(2)}, u32[]{:S(2)}) collective-permute-start(f32[1,20,128]{2,1,0:T(8,128)S(1)} %bitcast.12), channel_id=1, source_target_pairs={{8,0},{9,1},{10,2},{11,3},{12,4},{13,5},{14,6},{15,7},{0,8},{1,9},... | collective-permute-start | bytes 30728 | tf_op jit(solution)/shard_map/ppermute | solution.py:408
  16.1 1.4 %collective-permute-done.2 = f32[1,20,128]{2,1,0:T(8,128)S(1)} collective-permute-done((f32[1,20,128]{2,1,0:T(8,128)S(1)}, f32[1,20,128]{2,1,0:T(8,128)S(1)}, u32[]{:S(2)}, u32[]{:S(2)}) %collective-permute-start.2) | collective-permute-done | bytes 10272 | tf_op jit(solution)/shard_map/ppermute | solution.py:408
  17.5 2.6 %collective-permute-done.1 = f32[1,20,128]{2,1,0:T(8,128)S(1)} collective-permute-done((f32[1,20,128]{2,1,0:T(8,128)S(1)}, f32[1,20,128]{2,1,0:T(8,128)S(1)}, u32[]{:S(2)}, u32[]{:S(2)}) %collective-permute-start.1) | collective-permute-done | bytes 10272 | tf_op jit(solution)/shard_map/ppermute | solution.py:408
  20.7 2.4 %collective-permute-start.4 = (f32[4,20,128]{2,1,0:T(8,128)S(1)}, f32[4,20,128]{2,1,0:T(8,128)S(1)}, u32[]{:S(2)}, u32[]{:S(2)}) collective-permute-start(f32[4,20,128]{2,1,0:T(8,128)S(1)} %pad_maximum_fusion.1), channel_id=1, source_target_pairs={{4,0},{5,1},{6,2},{7,3},{0,4},{1,5},{2,6},{3,7},{12,8},{13,9},{14,... | collective-permute-start | bytes 122888 | tf_op jit(solution)/shard_map/ppermute | solution.py:408
  23.2 5.3 %collective-permute-done.3 = f32[4,20,128]{2,1,0:T(8,128)S(1)} collective-permute-done((f32[4,20,128]{2,1,0:T(8,128)S(1)}, f32[4,20,128]{2,1,0:T(8,128)S(1)}, u32[]{:S(2)}, u32[]{:S(2)}) %collective-permute-start.3) | collective-permute-done | bytes 40992 | tf_op jit(solution)/shard_map/ppermute | solution.py:408
  28.5 0.6 copy-done.3
  29.2 4.6 %spatial.1 = (f32[5,2,128,128]{3,2,1,0:T(8,128)S(1)}, f32[20,128]{1,0:T(8,128)S(1)}, f32[2,128,128]{2,1,0:T(8,128)S(1)}) custom-call(s32[32]{0:T(128)S(1)} %copy-done.5, s32[64]{0:T(128)S(1)} %copy-done.7, f32[5,5]{1,0:T(8,128)S(1)} %copy-done.3, f32[5,5]{1,0:T(8,128)S(1)} %copy-done.4, f32[1,5,2,128,128]{4,3,2,1,0:T(8,128)S(1)} %copy-done, ...), custom_call_target="tpu_custom_call" | custom-call | tf_op jit(solution)/shard_map/spatial/pallas_call | solution.py:426
  33.7 3.0 %all-to-all-done = f32[16,7,16,128]{3,2,1,0:T(8,128)S(1)} async-done(((f32[16,7,16,128]{3,2,1,0:T(8,128)}), f32[16,7,16,128]{3,2,1,0:T(8,128)S(1)}, u32[]{:S(2)}, u32[]{:S(2)}) %all-to-all-start) | async-done | bytes 917536 | tf_op jit(solution)/shard_map/all_to_all | solution.py:424
  36.7 2.4 %slab.1 = f32[16,80,128]{2,1,0:T(8,128)} custom-call(s32[32]{0:T(128)S(1)} %copy-done.5, f32[5,5]{1,0:T(8,128)S(1)} %copy-done.3, f32[5,5]{1,0:T(8,128)S(1)} %copy-done.4, f32[16,112,128]{2,1,0:T(8,128)S(1)} %bitcast.5, f32[2,128,128]{2,1,0:T(8,128)S(1)} %copy-done.2, f32[2,128,128]{2,1,0:T(8,128)S(1)} %copy-done.1), custom_call_target="tpu_custom_call" | custom-call | tf_op jit(solution)/shard_map/slab/pallas_call | solution.py:434
  39.2 5.1 %all-to-all-start.1 = ((f32[16,80,128]{2,1,0:T(8,128)}), f32[16,80,128]{2,1,0:T(8,128)S(1)}, u32[]{:S(2)}, u32[]{:S(2)}) async-start(f32[16,80,128]{2,1,0:T(8,128)} %slab.1), calls=%async_computation.1 | async-start | bytes 1310720 | tf_op jit(solution)/shard_map/all_to_all | solution.py:447
  44.3 0.7 %faces.1 = f32[40,128]{1,0:T(8,128)S(1)} custom-call(s32[32]{0:T(128)S(1)} %copy-done.5, f32[16,16]{1,0:T(8,128)S(1)} %copy-done.6, f32[16,112,128]{2,1,0:T(8,128)S(1)} %bitcast.6, f32[20,128]{1,0:T(8,128)S(1)} %get-tuple-element.14.half_ref, f32[2,128,128]{2,1,0:T(8,128)S(1)} %copy-done.1), custom_call_target="tpu_custom_call" | custom-call | tf_op jit(solution)/shard_map/faces/pallas_call | solution.py:449
  45.0 1.7 %collective-permute-start.8 = (f32[1,40,128]{2,1,0:T(8,128)S(1)}, f32[1,40,128]{2,1,0:T(8,128)S(1)}, u32[]{:S(2)}, u32[]{:S(2)}) collective-permute-start(f32[1,40,128]{2,1,0:T(8,128)S(1)} %bitcast.7), channel_id=1, source_target_pairs={{9,0},{8,1},{11,2},{10,3},{13,4},{12,5},{15,6},{14,7},{1,8},{0,9},... | collective-permute-start | bytes 61448 | tf_op jit(solution)/shard_map/ppermute | solution.py:408
  46.8 0.9 %collective-permute-start.7 = (f32[1,40,128]{2,1,0:T(8,128)S(1)}, f32[1,40,128]{2,1,0:T(8,128)S(1)}, u32[]{:S(2)}, u32[]{:S(2)}) collective-permute-start(f32[1,40,128]{2,1,0:T(8,128)S(1)} %bitcast.8), channel_id=1, source_target_pairs={{8,0},{9,1},{10,2},{11,3},{12,4},{13,5},{14,6},{15,7},{0,8},{1,9},... | collective-permute-start | bytes 61448 | tf_op jit(solution)/shard_map/ppermute | solution.py:408
  47.6 0.9 %collective-permute-start.6 = (f32[1,40,128]{2,1,0:T(8,128)S(1)}, f32[1,40,128]{2,1,0:T(8,128)S(1)}, u32[]{:S(2)}, u32[]{:S(2)}) collective-permute-start(f32[1,40,128]{2,1,0:T(8,128)S(1)} %bitcast.9), channel_id=1, source_target_pairs={{1,0},{0,1},{3,2},{2,3},{5,4},{4,5},{7,6},{6,7},{9,8},{8,9},{11,10... | collective-permute-start | bytes 61448 | tf_op jit(solution)/shard_map/ppermute | solution.py:408
  48.5 2.1 %collective-permute-done.8 = f32[1,40,128]{2,1,0:T(8,128)S(1)} collective-permute-done((f32[1,40,128]{2,1,0:T(8,128)S(1)}, f32[1,40,128]{2,1,0:T(8,128)S(1)}, u32[]{:S(2)}, u32[]{:S(2)}) %collective-permute-start.8) | collective-permute-done | bytes 20512 | tf_op jit(solution)/shard_map/ppermute | solution.py:408
  50.6 1.6 %collective-permute-done.7 = f32[1,40,128]{2,1,0:T(8,128)S(1)} collective-permute-done((f32[1,40,128]{2,1,0:T(8,128)S(1)}, f32[1,40,128]{2,1,0:T(8,128)S(1)}, u32[]{:S(2)}, u32[]{:S(2)}) %collective-permute-start.7) | collective-permute-done | bytes 20512 | tf_op jit(solution)/shard_map/ppermute | solution.py:408
  52.7 2.4 %collective-permute-start.10 = (f32[4,40,128]{2,1,0:T(8,128)S(1)}, f32[4,40,128]{2,1,0:T(8,128)S(1)}, u32[]{:S(2)}, u32[]{:S(2)}) collective-permute-start(f32[4,40,128]{2,1,0:T(8,128)S(1)} %pad_maximum_fusion), channel_id=1, source_target_pairs={{4,0},{5,1},{6,2},{7,3},{0,4},{1,5},{2,6},{3,7},{12,8},{13,9},{14,... | collective-permute-start | bytes 245768 | tf_op jit(solution)/shard_map/ppermute | solution.py:408
  55.2 5.6 %collective-permute-done.9 = f32[4,40,128]{2,1,0:T(8,128)S(1)} collective-permute-done((f32[4,40,128]{2,1,0:T(8,128)S(1)}, f32[4,40,128]{2,1,0:T(8,128)S(1)}, u32[]{:S(2)}, u32[]{:S(2)}) %collective-permute-start.9) | collective-permute-done | bytes 81952 | tf_op jit(solution)/shard_map/ppermute | solution.py:408
  60.9 0.8 %ghosts.1.spatial_ref = f32[5,2,128,128]{3,2,1,0:T(8,128)S(1)} custom-call(s32[32]{0:T(128)S(1)} %copy-done.5, s32[64]{0:T(128)S(1)} %copy-done.7, f32[5,5]{1,0:T(8,128)S(1)} %copy-done.3, f32[2,128,128]{2,1,0:T(8,128)S(1)} %copy-done.2, f32[2,128,128]{2,1,0:T(8,128)S(1)} %copy-done.1, ...), custom_call_target="tpu_custom_call", output_to_operand_aliasing={{}: (6, {})} | custom-call | tf_op jit(solution)/shard_map/ghosts/pallas_call | solution.py:453
  61.7 0.6 %all-to-all-done.1.got_ref = f32[16,80,128]{2,1,0:T(8,128)S(1)} async-done(((f32[16,80,128]{2,1,0:T(8,128)}), f32[16,80,128]{2,1,0:T(8,128)S(1)}, u32[]{:S(2)}, u32[]{:S(2)}) %all-to-all-start.1) | async-done | bytes 655392 | tf_op jit(solution)/shard_map/all_to_all | solution.py:447
  62.3 1.2 %final.1 = (f32[1,5,2,128,128]{4,3,2,1,0:T(8,128)}, f32[1,5,2,128,128]{4,3,2,1,0:T(8,128)}) custom-call(f32[1,5,2,128,128]{4,3,2,1,0:T(8,128)S(1)} %copy-done, f32[2,128,128]{2,1,0:T(8,128)S(1)} %copy-done.1, f32[2,128,128]{2,1,0:T(8,128)S(1)} %get-tuple-element.10.mask_ref, f32[5,2,128,128]{3,2,1,0:T(8,128)S(1)} %ghosts.1.spatial_ref, ...), custom_call_target="tpu_custom_call" | custom-call | tf_op jit(solution)/shard_map/final/pallas_call | solution.py:456
  (44 shorter events, 1.6 us)
Async XLA Ops:
  2.9 9.8 %copy-start.8 = (f32[20,128]{1,0:T(8,128)S(1)}, f32[20,128]{1,0:T(8,128)}, u32[]{:S(2)}) copy-start(f32[20,128]{1,0:T(8,128)} %get-tuple-element.9) | copy-start | bytes 30724
  2.9 25.6 %copy-start = (f32[1,5,2,128,128]{4,3,2,1,0:T(8,128)S(1)}, f32[1,5,2,128,128]{4,3,2,1,0:T(8,128)}, u32[]{:S(2)}) copy-start(f32[1,5,2,128,128]{4,3,2,1,0:T(8,128)} %state_ref.5) | copy-start | bytes 1966084
  2.9 33.8 %all-to-all-start = ((f32[16,7,16,128]{3,2,1,0:T(8,128)}), f32[16,7,16,128]{3,2,1,0:T(8,128)S(1)}, u32[]{:S(2)}, u32[]{:S(2)}) async-start(f32[16,7,16,128]{3,2,1,0:T(8,128)} %get-tuple-element.11), calls=%async_computation | async-start | bytes 1835008 | tf_op jit(solution)/shard_map/all_to_all | solution.py:424
  12.7 4.8 %collective-permute-start.2 = (f32[1,20,128]{2,1,0:T(8,128)S(1)}, f32[1,20,128]{2,1,0:T(8,128)S(1)}, u32[]{:S(2)}, u32[]{:S(2)}) collective-permute-start(f32[1,20,128]{2,1,0:T(8,128)S(1)} %bitcast.11), channel_id=1, source_target_pairs={{9,0},{8,1},{11,2},{10,3},{13,4},{12,5},{15,6},{14,7},{1,8},{0,9},... | collective-permute-start | bytes 30728 | tf_op jit(solution)/shard_map/ppermute | solution.py:408
  14.8 5.3 %collective-permute-start.1 = (f32[1,20,128]{2,1,0:T(8,128)S(1)}, f32[1,20,128]{2,1,0:T(8,128)S(1)}, u32[]{:S(2)}, u32[]{:S(2)}) collective-permute-start(f32[1,20,128]{2,1,0:T(8,128)S(1)} %bitcast.12), channel_id=1, source_target_pairs={{8,0},{9,1},{10,2},{11,3},{12,4},{13,5},{14,6},{15,7},{0,8},{1,9},... | collective-permute-start | bytes 30728 | tf_op jit(solution)/shard_map/ppermute | solution.py:408
  15.7 4.4 %collective-permute-start = (f32[1,20,128]{2,1,0:T(8,128)S(1)}, f32[1,20,128]{2,1,0:T(8,128)S(1)}, u32[]{:S(2)}, u32[]{:S(2)}) collective-permute-start(f32[1,20,128]{2,1,0:T(8,128)S(1)} %bitcast.13), channel_id=1, source_target_pairs={{1,0},{0,1},{3,2},{2,3},{5,4},{4,5},{7,6},{6,7},{9,8},{8,9},{11,10... | collective-permute-start | bytes 30728 | tf_op jit(solution)/shard_map/ppermute | solution.py:408
  20.1 8.4 %collective-permute-start.5 = (f32[4,20,128]{2,1,0:T(8,128)S(1)}, f32[4,20,128]{2,1,0:T(8,128)S(1)}, u32[]{:S(2)}, u32[]{:S(2)}) collective-permute-start(f32[4,20,128]{2,1,0:T(8,128)S(1)} %pad_maximum_fusion.1), channel_id=1, source_target_pairs={{6,0},{7,1},{0,2},{1,3},{2,4},{3,5},{4,6},{5,7},{14,8},{15,9},{8,1... | collective-permute-start | bytes 122888 | tf_op jit(solution)/shard_map/ppermute | solution.py:408
  20.7 7.7 %collective-permute-start.4 = (f32[4,20,128]{2,1,0:T(8,128)S(1)}, f32[4,20,128]{2,1,0:T(8,128)S(1)}, u32[]{:S(2)}, u32[]{:S(2)}) collective-permute-start(f32[4,20,128]{2,1,0:T(8,128)S(1)} %pad_maximum_fusion.1), channel_id=1, source_target_pairs={{4,0},{5,1},{6,2},{7,3},{0,4},{1,5},{2,6},{3,7},{12,8},{13,9},{14,... | collective-permute-start | bytes 122888 | tf_op jit(solution)/shard_map/ppermute | solution.py:408
  23.1 5.3 %collective-permute-start.3 = (f32[4,20,128]{2,1,0:T(8,128)S(1)}, f32[4,20,128]{2,1,0:T(8,128)S(1)}, u32[]{:S(2)}, u32[]{:S(2)}) collective-permute-start(f32[4,20,128]{2,1,0:T(8,128)S(1)} %pad_maximum_fusion.1), channel_id=1, source_target_pairs={{2,0},{3,1},{4,2},{5,3},{6,4},{7,5},{0,6},{1,7},{10,8},{11,9},{12,... | collective-permute-start | bytes 122888 | tf_op jit(solution)/shard_map/ppermute | solution.py:408
  23.1 5.4 %copy-start.1 = (f32[2,128,128]{2,1,0:T(8,128)S(1)}, f32[2,128,128]{2,1,0:T(8,128)}, u32[]{:S(2)}) copy-start(f32[2,128,128]{2,1,0:T(8,128)} %step_ref.9) | copy-start | bytes 393220
  23.1 5.4 %copy-start.2 = (f32[2,128,128]{2,1,0:T(8,128)S(1)}, f32[2,128,128]{2,1,0:T(8,128)}, u32[]{:S(2)}) copy-start(f32[2,128,128]{2,1,0:T(8,128)} %visc_ref.5) | copy-start | bytes 393220
  28.4 0.7 %copy-start.3 = (f32[5,5]{1,0:T(8,128)S(1)}, f32[5,5]{1,0:T(8,128)}, u32[]{:S(2)}) copy-start(f32[5,5]{1,0:T(8,128)} %row_in.1) | copy-start | bytes 304
  28.5 0.7 %copy-start.4 = (f32[5,5]{1,0:T(8,128)S(1)}, f32[5,5]{1,0:T(8,128)}, u32[]{:S(2)}) copy-start(f32[5,5]{1,0:T(8,128)} %cell_in.1) | copy-start | bytes 304
  28.5 0.7 %copy-start.5 = (s32[32]{0:T(128)S(1)}, s32[32]{0:T(128)}, u32[]{:S(2)}) copy-start(s32[32]{0:T(128)} %live_in.3) | copy-start | bytes 388
  28.5 0.7 %copy-start.7 = (s32[64]{0:T(128)S(1)}, s32[64]{0:T(128)}, u32[]{:S(2)}) copy-start(s32[64]{0:T(128)} %partner_ref.3) | copy-start | bytes 772
  39.2 5.1 %copy-start.6 = (f32[16,16]{1,0:T(8,128)S(1)}, f32[16,16]{1,0:T(8,128)}, u32[]{:S(2)}) copy-start(f32[16,16]{1,0:T(8,128)} %constant.2.clone.weights_ref) | copy-start | bytes 3076
  39.2 23.2 %all-to-all-start.1 = ((f32[16,80,128]{2,1,0:T(8,128)}), f32[16,80,128]{2,1,0:T(8,128)S(1)}, u32[]{:S(2)}, u32[]{:S(2)}) async-start(f32[16,80,128]{2,1,0:T(8,128)} %slab.1), calls=%async_computation.1 | async-start | bytes 1310720 | tf_op jit(solution)/shard_map/all_to_all | solution.py:447
  45.0 5.5 %collective-permute-start.8 = (f32[1,40,128]{2,1,0:T(8,128)S(1)}, f32[1,40,128]{2,1,0:T(8,128)S(1)}, u32[]{:S(2)}, u32[]{:S(2)}) collective-permute-start(f32[1,40,128]{2,1,0:T(8,128)S(1)} %bitcast.7), channel_id=1, source_target_pairs={{9,0},{8,1},{11,2},{10,3},{13,4},{12,5},{15,6},{14,7},{1,8},{0,9},... | collective-permute-start | bytes 61448 | tf_op jit(solution)/shard_map/ppermute | solution.py:408
  46.8 5.4 %collective-permute-start.7 = (f32[1,40,128]{2,1,0:T(8,128)S(1)}, f32[1,40,128]{2,1,0:T(8,128)S(1)}, u32[]{:S(2)}, u32[]{:S(2)}) collective-permute-start(f32[1,40,128]{2,1,0:T(8,128)S(1)} %bitcast.8), channel_id=1, source_target_pairs={{8,0},{9,1},{10,2},{11,3},{12,4},{13,5},{14,6},{15,7},{0,8},{1,9},... | collective-permute-start | bytes 61448 | tf_op jit(solution)/shard_map/ppermute | solution.py:408
  47.6 4.6 %collective-permute-start.6 = (f32[1,40,128]{2,1,0:T(8,128)S(1)}, f32[1,40,128]{2,1,0:T(8,128)S(1)}, u32[]{:S(2)}, u32[]{:S(2)}) collective-permute-start(f32[1,40,128]{2,1,0:T(8,128)S(1)} %bitcast.9), channel_id=1, source_target_pairs={{1,0},{0,1},{3,2},{2,3},{5,4},{4,5},{7,6},{6,7},{9,8},{8,9},{11,10... | collective-permute-start | bytes 61448 | tf_op jit(solution)/shard_map/ppermute | solution.py:408
  52.2 8.7 %collective-permute-start.11 = (f32[4,40,128]{2,1,0:T(8,128)S(1)}, f32[4,40,128]{2,1,0:T(8,128)S(1)}, u32[]{:S(2)}, u32[]{:S(2)}) collective-permute-start(f32[4,40,128]{2,1,0:T(8,128)S(1)} %pad_maximum_fusion), channel_id=1, source_target_pairs={{6,0},{7,1},{0,2},{1,3},{2,4},{3,5},{4,6},{5,7},{14,8},{15,9},{8,1... | collective-permute-start | bytes 245768 | tf_op jit(solution)/shard_map/ppermute | solution.py:408
  52.7 8.1 %collective-permute-start.10 = (f32[4,40,128]{2,1,0:T(8,128)S(1)}, f32[4,40,128]{2,1,0:T(8,128)S(1)}, u32[]{:S(2)}, u32[]{:S(2)}) collective-permute-start(f32[4,40,128]{2,1,0:T(8,128)S(1)} %pad_maximum_fusion), channel_id=1, source_target_pairs={{4,0},{5,1},{6,2},{7,3},{0,4},{1,5},{2,6},{3,7},{12,8},{13,9},{14,... | collective-permute-start | bytes 245768 | tf_op jit(solution)/shard_map/ppermute | solution.py:408
  55.2 5.7 %collective-permute-start.9 = (f32[4,40,128]{2,1,0:T(8,128)S(1)}, f32[4,40,128]{2,1,0:T(8,128)S(1)}, u32[]{:S(2)}, u32[]{:S(2)}) collective-permute-start(f32[4,40,128]{2,1,0:T(8,128)S(1)} %pad_maximum_fusion), channel_id=1, source_target_pairs={{2,0},{3,1},{4,2},{5,3},{6,4},{7,5},{0,6},{1,7},{10,8},{11,9},{12,... | collective-permute-start | bytes 245768 | tf_op jit(solution)/shard_map/ppermute | solution.py:408

commit v5 on v4

--- a/solution.py
+++ b/solution.py
@@ -34,7 +34,7 @@
 
 
 HALF = INST // 2
-GROUP = 4
+GROUP = 8
 EVEN = [0.5 * (spectral(m) + spectral(m + HALF)) for m in range(HALF)]
 ODD = [0.5 * (spectral(m) - spectral(m + HALF)) for m in range(HALF)]
 
@@ -103,22 +103,25 @@
     return copies
 
 
-def pack_kernel(live_in, state_ref, chunks_ref, faces_ref, live_ref, arrived, ready):
+def pack_kernel(live_in, state_ref, chunks_ref, faces_ref, held_ref, live_ref, arrived, ready):
     first = lax.axis_index("blk") * BLOCKS
     scalars = fetched([live_in], [live_ref], ready)
-    copies = []
-    for i in range(INST):
-        b, low = i // PER_BLOCK, (i % PER_BLOCK) * SLAB
-        copy = pltpu.make_async_copy(
-            state_ref.at[0, :, b, low : low + SLAB, :], chunks_ref.at[i, 0:VARS], arrived.at[i]
-        )
+    places = [(v, b) for v in range(VARS) for b in range(BLOCKS)]
+    copies = [
+        pltpu.make_async_copy(state_ref.at[0, v, b], held_ref.at[v, b], arrived.at[k])
+        for k, (v, b) in enumerate(places)
+    ]
+    for copy in copies:
         copy.start()
-        copies.append(copy)
-    for copy in copies + scalars:
+    for (v, b), copy in zip(places, copies):
         copy.wait()
+        for j in range(PER_BLOCK):
+            chunks_ref[b * PER_BLOCK + j, v] = held_ref[v, b, j * SLAB : (j + 1) * SLAB, :]
+    for copy in scalars:
+        copy.wait()
 
     def row_of(v, b, row):
-        return chunks_ref[b * PER_BLOCK + row // SLAB, v, pl.ds(row % SLAB, 1), :]
+        return held_ref[v, b, pl.ds(row, 1), :]
 
     for b in range(BLOCKS):
         last = live_ref[first + b] - 1
@@ -419,7 +422,13 @@
     whole = state.shape
     chunks, faces = call(
         pack_kernel, [(INST, SENT // SLAB, SLAB, CELLS), (FACES * VARS, CELLS)], [HBM, HBM],
-        [LIVE, pltpu.SemaphoreType.DMA((INST,)), pltpu.SemaphoreType.DMA((1,))], name="pack", limit=60
+        [
+            pltpu.VMEM((VARS, BLOCKS, ROWS, CELLS), jnp.float32),
+            LIVE,
+            pltpu.SemaphoreType.DMA((VARS * BLOCKS,)),
+            pltpu.SemaphoreType.DMA((1,)),
+        ],
+        name="pack", limit=60
     )(live_rows, state)
     slabs = lax.all_to_all(chunks, "inst", 0, 0, tiled=True).reshape(INST, SENT, CELLS)
     ghosts = gathered_over_blocks(faces, ORDER)

time: 63.9 us -> 63.8 us (level)
  no operation moved by 1% of the time
where the time goes in v5:
time: 63.8 us; the launch traced here: 63.4 us
  starting transfers between devices  27.7 us (43%)
  waiting for transfers between devices  22.2 us (35%)
  Pallas kernels  11.8 us (18%)
  between operations  0.89 us (1%)
  local copies, waits for them, and re-layouts  0.72 us (1%)
    ppermute x12, waiting for transfers between devices, moved(): return lax.ppermute(array, 'blk', pairs)  18.6 us
    ppermute x12, starting transfers between devices, moved(): return lax.ppermute(array, 'blk', pairs)  12.9 us
    all_to_all x1, starting transfers between devices, per_device(): lax.all_to_all(chunks, 'inst', 0, 0, tiled=True).reshape(INST, SENT, CELLS)  9.73 us
    all_to_all x1, starting transfers between devices, per_device(): back = lax.all_to_all(sent, 'inst', 0, 0, tiled=True)  5.12 us
    pallas_call x1, Pallas kernels, per_device(): call(spatial_kernel, [(VARS, BLOCKS, ROWS, CELLS), (FACES * VARS, CELLS),...  4.55 us
    all_to_all x1, waiting for transfers between devices, per_device(): lax.all_to_all(chunks, 'inst', 0, 0, tiled=True).reshape(INST, SENT, CELLS)  3 us
    pallas_call x1, Pallas kernels, per_device(): call(slab_kernel, [(INST, MAIN, CELLS)], [HBM, HBM, HBM, VMEM, VMEM, VMEM...  2.36 us
    pallas_call x1, Pallas kernels, per_device(): call(pack_kernel, [(INST, SENT // SLAB, SLAB, CELLS), (FACES * VARS, CELL...  2.24 us
  transfers between devices with their start and end apart: 14, of which 8 were waited for; matrix products, arithmetic and copies ran while one was open for 0% of the time, Pallas kernels for 10%

profile of v5, /device:TPU:6, one launch (start us, length us, event | category | flops | bytes accessed | tf_op | source)
XLA Modules:
  0.0 63.4 jit_solution(6066657101442693379)
XLA Ops:
  0.6 2.2 %pack.1 = (f32[16,7,16,128]{3,2,1,0:T(8,128)}, f32[20,128]{1,0:T(8,128)}) custom-call(s32[32]{0:T(128)} %live_in.3, f32[1,5,2,128,128]{4,3,2,1,0:T(8,128)} %state_ref.5), custom_call_target="tpu_custom_call" | custom-call | tf_op jit(solution)/shard_map/pack/pallas_call | solution.py:423
  2.9 9.7 %all-to-all-start = ((f32[16,7,16,128]{3,2,1,0:T(8,128)}), f32[16,7,16,128]{3,2,1,0:T(8,128)S(1)}, u32[]{:S(2)}, u32[]{:S(2)}) async-start(f32[16,7,16,128]{3,2,1,0:T(8,128)} %get-tuple-element.11), calls=%async_computation | async-start | bytes 1835008 | tf_op jit(solution)/shard_map/all_to_all | solution.py:433
  12.6 2.1 %collective-permute-start.2 = (f32[1,20,128]{2,1,0:T(8,128)S(1)}, f32[1,20,128]{2,1,0:T(8,128)S(1)}, u32[]{:S(2)}, u32[]{:S(2)}) collective-permute-start(f32[1,20,128]{2,1,0:T(8,128)S(1)} %bitcast.11), channel_id=1, source_target_pairs={{9,0},{8,1},{11,2},{10,3},{13,4},{12,5},{15,6},{14,7},{1,8},{0,9},... | collective-permute-start | bytes 30728 | tf_op jit(solution)/shard_map/ppermute | solution.py:411
  14.8 0.9 %collective-permute-start.1 = (f32[1,20,128]{2,1,0:T(8,128)S(1)}, f32[1,20,128]{2,1,0:T(8,128)S(1)}, u32[]{:S(2)}, u32[]{:S(2)}) collective-permute-start(f32[1,20,128]{2,1,0:T(8,128)S(1)} %bitcast.12), channel_id=1, source_target_pairs={{8,0},{9,1},{10,2},{11,3},{12,4},{13,5},{14,6},{15,7},{0,8},{1,9},... | collective-permute-start | bytes 30728 | tf_op jit(solution)/shard_map/ppermute | solution.py:411
  16.1 1.4 %collective-permute-done.2 = f32[1,20,128]{2,1,0:T(8,128)S(1)} collective-permute-done((f32[1,20,128]{2,1,0:T(8,128)S(1)}, f32[1,20,128]{2,1,0:T(8,128)S(1)}, u32[]{:S(2)}, u32[]{:S(2)}) %collective-permute-start.2) | collective-permute-done | bytes 10272 | tf_op jit(solution)/shard_map/ppermute | solution.py:411
  17.5 2.6 %collective-permute-done.1 = f32[1,20,128]{2,1,0:T(8,128)S(1)} collective-permute-done((f32[1,20,128]{2,1,0:T(8,128)S(1)}, f32[1,20,128]{2,1,0:T(8,128)S(1)}, u32[]{:S(2)}, u32[]{:S(2)}) %collective-permute-start.1) | collective-permute-done | bytes 10272 | tf_op jit(solution)/shard_map/ppermute | solution.py:411
  20.7 2.4 %collective-permute-start.4 = (f32[4,20,128]{2,1,0:T(8,128)S(1)}, f32[4,20,128]{2,1,0:T(8,128)S(1)}, u32[]{:S(2)}, u32[]{:S(2)}) collective-permute-start(f32[4,20,128]{2,1,0:T(8,128)S(1)} %pad_maximum_fusion.1), channel_id=1, source_target_pairs={{4,0},{5,1},{6,2},{7,3},{0,4},{1,5},{2,6},{3,7},{12,8},{13,9},{14,... | collective-permute-start | bytes 122888 | tf_op jit(solution)/shard_map/ppermute | solution.py:411
  23.1 5.3 %collective-permute-done.3 = f32[4,20,128]{2,1,0:T(8,128)S(1)} collective-permute-done((f32[4,20,128]{2,1,0:T(8,128)S(1)}, f32[4,20,128]{2,1,0:T(8,128)S(1)}, u32[]{:S(2)}, u32[]{:S(2)}) %collective-permute-start.3) | collective-permute-done | bytes 40992 | tf_op jit(solution)/shard_map/ppermute | solution.py:411
  28.5 0.6 copy-done.3
  29.1 4.6 %spatial.1 = (f32[5,2,128,128]{3,2,1,0:T(8,128)S(1)}, f32[20,128]{1,0:T(8,128)S(1)}, f32[2,128,128]{2,1,0:T(8,128)S(1)}) custom-call(s32[32]{0:T(128)S(1)} %copy-done.5, s32[64]{0:T(128)S(1)} %copy-done.7, f32[5,5]{1,0:T(8,128)S(1)} %copy-done.3, f32[5,5]{1,0:T(8,128)S(1)} %copy-done.4, f32[1,5,2,128,128]{4,3,2,1,0:T(8,128)S(1)} %copy-done, ...), custom_call_target="tpu_custom_call" | custom-call | tf_op jit(solution)/shard_map/spatial/pallas_call | solution.py:435
  33.7 3.0 %all-to-all-done = f32[16,7,16,128]{3,2,1,0:T(8,128)S(1)} async-done(((f32[16,7,16,128]{3,2,1,0:T(8,128)}), f32[16,7,16,128]{3,2,1,0:T(8,128)S(1)}, u32[]{:S(2)}, u32[]{:S(2)}) %all-to-all-start) | async-done | bytes 917536 | tf_op jit(solution)/shard_map/all_to_all | solution.py:433
  36.7 2.4 %slab.1 = f32[16,80,128]{2,1,0:T(8,128)} custom-call(s32[32]{0:T(128)S(1)} %copy-done.5, f32[5,5]{1,0:T(8,128)S(1)} %copy-done.3, f32[5,5]{1,0:T(8,128)S(1)} %copy-done.4, f32[16,112,128]{2,1,0:T(8,128)S(1)} %bitcast.5, f32[2,128,128]{2,1,0:T(8,128)S(1)} %copy-done.2, f32[2,128,128]{2,1,0:T(8,128)S(1)} %copy-done.1), custom_call_target="tpu_custom_call" | custom-call | tf_op jit(solution)/shard_map/slab/pallas_call | solution.py:443
  39.1 5.1 %all-to-all-start.1 = ((f32[16,80,128]{2,1,0:T(8,128)}), f32[16,80,128]{2,1,0:T(8,128)S(1)}, u32[]{:S(2)}, u32[]{:S(2)}) async-start(f32[16,80,128]{2,1,0:T(8,128)} %slab.1), calls=%async_computation.1 | async-start | bytes 1310720 | tf_op jit(solution)/shard_map/all_to_all | solution.py:456
  44.2 0.7 %faces.1 = f32[40,128]{1,0:T(8,128)S(1)} custom-call(s32[32]{0:T(128)S(1)} %copy-done.5, f32[16,16]{1,0:T(8,128)S(1)} %copy-done.6, f32[16,112,128]{2,1,0:T(8,128)S(1)} %bitcast.6, f32[20,128]{1,0:T(8,128)S(1)} %get-tuple-element.14.half_ref, f32[2,128,128]{2,1,0:T(8,128)S(1)} %copy-done.1), custom_call_target="tpu_custom_call" | custom-call | tf_op jit(solution)/shard_map/faces/pallas_call | solution.py:458
  44.9 1.7 %collective-permute-start.8 = (f32[1,40,128]{2,1,0:T(8,128)S(1)}, f32[1,40,128]{2,1,0:T(8,128)S(1)}, u32[]{:S(2)}, u32[]{:S(2)}) collective-permute-start(f32[1,40,128]{2,1,0:T(8,128)S(1)} %bitcast.7), channel_id=1, source_target_pairs={{9,0},{8,1},{11,2},{10,3},{13,4},{12,5},{15,6},{14,7},{1,8},{0,9},... | collective-permute-start | bytes 61448 | tf_op jit(solution)/shard_map/ppermute | solution.py:411
  46.7 0.9 %collective-permute-start.7 = (f32[1,40,128]{2,1,0:T(8,128)S(1)}, f32[1,40,128]{2,1,0:T(8,128)S(1)}, u32[]{:S(2)}, u32[]{:S(2)}) collective-permute-start(f32[1,40,128]{2,1,0:T(8,128)S(1)} %bitcast.8), channel_id=1, source_target_pairs={{8,0},{9,1},{10,2},{11,3},{12,4},{13,5},{14,6},{15,7},{0,8},{1,9},... | collective-permute-start | bytes 61448 | tf_op jit(solution)/shard_map/ppermute | solution.py:411
  47.5 0.9 %collective-permute-start.6 = (f32[1,40,128]{2,1,0:T(8,128)S(1)}, f32[1,40,128]{2,1,0:T(8,128)S(1)}, u32[]{:S(2)}, u32[]{:S(2)}) collective-permute-start(f32[1,40,128]{2,1,0:T(8,128)S(1)} %bitcast.9), channel_id=1, source_target_pairs={{1,0},{0,1},{3,2},{2,3},{5,4},{4,5},{7,6},{6,7},{9,8},{8,9},{11,10... | collective-permute-start | bytes 61448 | tf_op jit(solution)/shard_map/ppermute | solution.py:411
  48.4 2.1 %collective-permute-done.8 = f32[1,40,128]{2,1,0:T(8,128)S(1)} collective-permute-done((f32[1,40,128]{2,1,0:T(8,128)S(1)}, f32[1,40,128]{2,1,0:T(8,128)S(1)}, u32[]{:S(2)}, u32[]{:S(2)}) %collective-permute-start.8) | collective-permute-done | bytes 20512 | tf_op jit(solution)/shard_map/ppermute | solution.py:411
  50.5 1.6 %collective-permute-done.7 = f32[1,40,128]{2,1,0:T(8,128)S(1)} collective-permute-done((f32[1,40,128]{2,1,0:T(8,128)S(1)}, f32[1,40,128]{2,1,0:T(8,128)S(1)}, u32[]{:S(2)}, u32[]{:S(2)}) %collective-permute-start.7) | collective-permute-done | bytes 20512 | tf_op jit(solution)/shard_map/ppermute | solution.py:411
  52.6 2.4 %collective-permute-start.10 = (f32[4,40,128]{2,1,0:T(8,128)S(1)}, f32[4,40,128]{2,1,0:T(8,128)S(1)}, u32[]{:S(2)}, u32[]{:S(2)}) collective-permute-start(f32[4,40,128]{2,1,0:T(8,128)S(1)} %pad_maximum_fusion), channel_id=1, source_target_pairs={{4,0},{5,1},{6,2},{7,3},{0,4},{1,5},{2,6},{3,7},{12,8},{13,9},{14,... | collective-permute-start | bytes 245768 | tf_op jit(solution)/shard_map/ppermute | solution.py:411
  55.1 5.6 %collective-permute-done.9 = f32[4,40,128]{2,1,0:T(8,128)S(1)} collective-permute-done((f32[4,40,128]{2,1,0:T(8,128)S(1)}, f32[4,40,128]{2,1,0:T(8,128)S(1)}, u32[]{:S(2)}, u32[]{:S(2)}) %collective-permute-start.9) | collective-permute-done | bytes 81952 | tf_op jit(solution)/shard_map/ppermute | solution.py:411
  60.8 0.8 %ghosts.1.spatial_ref = f32[5,2,128,128]{3,2,1,0:T(8,128)S(1)} custom-call(s32[32]{0:T(128)S(1)} %copy-done.5, s32[64]{0:T(128)S(1)} %copy-done.7, f32[5,5]{1,0:T(8,128)S(1)} %copy-done.3, f32[2,128,128]{2,1,0:T(8,128)S(1)} %copy-done.2, f32[2,128,128]{2,1,0:T(8,128)S(1)} %copy-done.1, ...), custom_call_target="tpu_custom_call", output_to_operand_aliasing={{}: (6, {})} | custom-call | tf_op jit(solution)/shard_map/ghosts/pallas_call | solution.py:462
  61.6 0.6 %all-to-all-done.1.got_ref = f32[16,80,128]{2,1,0:T(8,128)S(1)} async-done(((f32[16,80,128]{2,1,0:T(8,128)}), f32[16,80,128]{2,1,0:T(8,128)S(1)}, u32[]{:S(2)}, u32[]{:S(2)}) %all-to-all-start.1) | async-done | bytes 655392 | tf_op jit(solution)/shard_map/all_to_all | solution.py:456
  62.2 1.2 %final.1 = (f32[1,5,2,128,128]{4,3,2,1,0:T(8,128)}, f32[1,5,2,128,128]{4,3,2,1,0:T(8,128)}) custom-call(f32[1,5,2,128,128]{4,3,2,1,0:T(8,128)S(1)} %copy-done, f32[2,128,128]{2,1,0:T(8,128)S(1)} %copy-done.1, f32[2,128,128]{2,1,0:T(8,128)S(1)} %get-tuple-element.10.mask_ref, f32[5,2,128,128]{3,2,1,0:T(8,128)S(1)} %ghosts.1.spatial_ref, ...), custom_call_target="tpu_custom_call" | custom-call | tf_op jit(solution)/shard_map/final/pallas_call | solution.py:465
  (44 shorter events, 1.6 us)
Async XLA Ops:
  2.9 9.8 %copy-start.8 = (f32[20,128]{1,0:T(8,128)S(1)}, f32[20,128]{1,0:T(8,128)}, u32[]{:S(2)}) copy-start(f32[20,128]{1,0:T(8,128)} %get-tuple-element.9) | copy-start | bytes 30724
  2.9 25.6 %copy-start = (f32[1,5,2,128,128]{4,3,2,1,0:T(8,128)S(1)}, f32[1,5,2,128,128]{4,3,2,1,0:T(8,128)}, u32[]{:S(2)}) copy-start(f32[1,5,2,128,128]{4,3,2,1,0:T(8,128)} %state_ref.5) | copy-start | bytes 1966084
  2.9 33.8 %all-to-all-start = ((f32[16,7,16,128]{3,2,1,0:T(8,128)}), f32[16,7,16,128]{3,2,1,0:T(8,128)S(1)}, u32[]{:S(2)}, u32[]{:S(2)}) async-start(f32[16,7,16,128]{3,2,1,0:T(8,128)} %get-tuple-element.11), calls=%async_computation | async-start | bytes 1835008 | tf_op jit(solution)/shard_map/all_to_all | solution.py:433
  12.6 4.8 %collective-permute-start.2 = (f32[1,20,128]{2,1,0:T(8,128)S(1)}, f32[1,20,128]{2,1,0:T(8,128)S(1)}, u32[]{:S(2)}, u32[]{:S(2)}) collective-permute-start(f32[1,20,128]{2,1,0:T(8,128)S(1)} %bitcast.11), channel_id=1, source_target_pairs={{9,0},{8,1},{11,2},{10,3},{13,4},{12,5},{15,6},{14,7},{1,8},{0,9},... | collective-permute-start | bytes 30728 | tf_op jit(solution)/shard_map/ppermute | solution.py:411
  14.8 5.3 %collective-permute-start.1 = (f32[1,20,128]{2,1,0:T(8,128)S(1)}, f32[1,20,128]{2,1,0:T(8,128)S(1)}, u32[]{:S(2)}, u32[]{:S(2)}) collective-permute-start(f32[1,20,128]{2,1,0:T(8,128)S(1)} %bitcast.12), channel_id=1, source_target_pairs={{8,0},{9,1},{10,2},{11,3},{12,4},{13,5},{14,6},{15,7},{0,8},{1,9},... | collective-permute-start | bytes 30728 | tf_op jit(solution)/shard_map/ppermute | solution.py:411
  15.7 4.4 %collective-permute-start = (f32[1,20,128]{2,1,0:T(8,128)S(1)}, f32[1,20,128]{2,1,0:T(8,128)S(1)}, u32[]{:S(2)}, u32[]{:S(2)}) collective-permute-start(f32[1,20,128]{2,1,0:T(8,128)S(1)} %bitcast.13), channel_id=1, source_target_pairs={{1,0},{0,1},{3,2},{2,3},{5,4},{4,5},{7,6},{6,7},{9,8},{8,9},{11,10... | collective-permute-start | bytes 30728 | tf_op jit(solution)/shard_map/ppermute | solution.py:411
  20.1 8.4 %collective-permute-start.5 = (f32[4,20,128]{2,1,0:T(8,128)S(1)}, f32[4,20,128]{2,1,0:T(8,128)S(1)}, u32[]{:S(2)}, u32[]{:S(2)}) collective-permute-start(f32[4,20,128]{2,1,0:T(8,128)S(1)} %pad_maximum_fusion.1), channel_id=1, source_target_pairs={{6,0},{7,1},{0,2},{1,3},{2,4},{3,5},{4,6},{5,7},{14,8},{15,9},{8,1... | collective-permute-start | bytes 122888 | tf_op jit(solution)/shard_map/ppermute | solution.py:411
  20.7 7.7 %collective-permute-start.4 = (f32[4,20,128]{2,1,0:T(8,128)S(1)}, f32[4,20,128]{2,1,0:T(8,128)S(1)}, u32[]{:S(2)}, u32[]{:S(2)}) collective-permute-start(f32[4,20,128]{2,1,0:T(8,128)S(1)} %pad_maximum_fusion.1), channel_id=1, source_target_pairs={{4,0},{5,1},{6,2},{7,3},{0,4},{1,5},{2,6},{3,7},{12,8},{13,9},{14,... | collective-permute-start | bytes 122888 | tf_op jit(solution)/shard_map/ppermute | solution.py:411
  23.1 5.3 %collective-permute-start.3 = (f32[4,20,128]{2,1,0:T(8,128)S(1)}, f32[4,20,128]{2,1,0:T(8,128)S(1)}, u32[]{:S(2)}, u32[]{:S(2)}) collective-permute-start(f32[4,20,128]{2,1,0:T(8,128)S(1)} %pad_maximum_fusion.1), channel_id=1, source_target_pairs={{2,0},{3,1},{4,2},{5,3},{6,4},{7,5},{0,6},{1,7},{10,8},{11,9},{12,... | collective-permute-start | bytes 122888 | tf_op jit(solution)/shard_map/ppermute | solution.py:411
  23.1 5.4 %copy-start.1 = (f32[2,128,128]{2,1,0:T(8,128)S(1)}, f32[2,128,128]{2,1,0:T(8,128)}, u32[]{:S(2)}) copy-start(f32[2,128,128]{2,1,0:T(8,128)} %step_ref.9) | copy-start | bytes 393220
  23.1 5.4 %copy-start.2 = (f32[2,128,128]{2,1,0:T(8,128)S(1)}, f32[2,128,128]{2,1,0:T(8,128)}, u32[]{:S(2)}) copy-start(f32[2,128,128]{2,1,0:T(8,128)} %visc_ref.5) | copy-start | bytes 393220
  28.4 0.7 %copy-start.3 = (f32[5,5]{1,0:T(8,128)S(1)}, f32[5,5]{1,0:T(8,128)}, u32[]{:S(2)}) copy-start(f32[5,5]{1,0:T(8,128)} %row_in.1) | copy-start | bytes 304
  28.4 0.7 %copy-start.4 = (f32[5,5]{1,0:T(8,128)S(1)}, f32[5,5]{1,0:T(8,128)}, u32[]{:S(2)}) copy-start(f32[5,5]{1,0:T(8,128)} %cell_in.1) | copy-start | bytes 304
  28.4 0.7 %copy-start.5 = (s32[32]{0:T(128)S(1)}, s32[32]{0:T(128)}, u32[]{:S(2)}) copy-start(s32[32]{0:T(128)} %live_in.3) | copy-start | bytes 388
  28.5 0.7 %copy-start.7 = (s32[64]{0:T(128)S(1)}, s32[64]{0:T(128)}, u32[]{:S(2)}) copy-start(s32[64]{0:T(128)} %partner_ref.3) | copy-start | bytes 772
  39.1 5.1 %copy-start.6 = (f32[16,16]{1,0:T(8,128)S(1)}, f32[16,16]{1,0:T(8,128)}, u32[]{:S(2)}) copy-start(f32[16,16]{1,0:T(8,128)} %constant.2.clone.weights_ref) | copy-start | bytes 3076
  39.1 23.2 %all-to-all-start.1 = ((f32[16,80,128]{2,1,0:T(8,128)}), f32[16,80,128]{2,1,0:T(8,128)S(1)}, u32[]{:S(2)}, u32[]{:S(2)}) async-start(f32[16,80,128]{2,1,0:T(8,128)} %slab.1), calls=%async_computation.1 | async-start | bytes 1310720 | tf_op jit(solution)/shard_map/all_to_all | solution.py:456
  44.9 5.5 %collective-permute-start.8 = (f32[1,40,128]{2,1,0:T(8,128)S(1)}, f32[1,40,128]{2,1,0:T(8,128)S(1)}, u32[]{:S(2)}, u32[]{:S(2)}) collective-permute-start(f32[1,40,128]{2,1,0:T(8,128)S(1)} %bitcast.7), channel_id=1, source_target_pairs={{9,0},{8,1},{11,2},{10,3},{13,4},{12,5},{15,6},{14,7},{1,8},{0,9},... | collective-permute-start | bytes 61448 | tf_op jit(solution)/shard_map/ppermute | solution.py:411
  46.7 5.4 %collective-permute-start.7 = (f32[1,40,128]{2,1,0:T(8,128)S(1)}, f32[1,40,128]{2,1,0:T(8,128)S(1)}, u32[]{:S(2)}, u32[]{:S(2)}) collective-permute-start(f32[1,40,128]{2,1,0:T(8,128)S(1)} %bitcast.8), channel_id=1, source_target_pairs={{8,0},{9,1},{10,2},{11,3},{12,4},{13,5},{14,6},{15,7},{0,8},{1,9},... | collective-permute-start | bytes 61448 | tf_op jit(solution)/shard_map/ppermute | solution.py:411
  47.5 4.6 %collective-permute-start.6 = (f32[1,40,128]{2,1,0:T(8,128)S(1)}, f32[1,40,128]{2,1,0:T(8,128)S(1)}, u32[]{:S(2)}, u32[]{:S(2)}) collective-permute-start(f32[1,40,128]{2,1,0:T(8,128)S(1)} %bitcast.9), channel_id=1, source_target_pairs={{1,0},{0,1},{3,2},{2,3},{5,4},{4,5},{7,6},{6,7},{9,8},{8,9},{11,10... | collective-permute-start | bytes 61448 | tf_op jit(solution)/shard_map/ppermute | solution.py:411
  52.1 8.7 %collective-permute-start.11 = (f32[4,40,128]{2,1,0:T(8,128)S(1)}, f32[4,40,128]{2,1,0:T(8,128)S(1)}, u32[]{:S(2)}, u32[]{:S(2)}) collective-permute-start(f32[4,40,128]{2,1,0:T(8,128)S(1)} %pad_maximum_fusion), channel_id=1, source_target_pairs={{6,0},{7,1},{0,2},{1,3},{2,4},{3,5},{4,6},{5,7},{14,8},{15,9},{8,1... | collective-permute-start | bytes 245768 | tf_op jit(solution)/shard_map/ppermute | solution.py:411
  52.6 8.1 %collective-permute-start.10 = (f32[4,40,128]{2,1,0:T(8,128)S(1)}, f32[4,40,128]{2,1,0:T(8,128)S(1)}, u32[]{:S(2)}, u32[]{:S(2)}) collective-permute-start(f32[4,40,128]{2,1,0:T(8,128)S(1)} %pad_maximum_fusion), channel_id=1, source_target_pairs={{4,0},{5,1},{6,2},{7,3},{0,4},{1,5},{2,6},{3,7},{12,8},{13,9},{14,... | collective-permute-start | bytes 245768 | tf_op jit(solution)/shard_map/ppermute | solution.py:411
  55.1 5.7 %collective-permute-start.9 = (f32[4,40,128]{2,1,0:T(8,128)S(1)}, f32[4,40,128]{2,1,0:T(8,128)S(1)}, u32[]{:S(2)}, u32[]{:S(2)}) collective-permute-start(f32[4,40,128]{2,1,0:T(8,128)S(1)} %pad_maximum_fusion), channel_id=1, source_target_pairs={{2,0},{3,1},{4,2},{5,3},{6,4},{7,5},{0,6},{1,7},{10,8},{11,9},{12,... | collective-permute-start | bytes 245768 | tf_op jit(solution)/shard_map/ppermute | solution.py:411

commit v6 on v5

--- a/solution.py
+++ b/solution.py
@@ -3,6 +3,7 @@
 
 import jax
 import jax.numpy as jnp
+import numpy as np
 from jax import lax
 from jax.experimental import pallas as pl
 from jax.experimental.pallas import tpu as pltpu
@@ -321,13 +322,16 @@
         sent_copy(g).wait()
 
 
-def face_kernel(live_ref, weights_ref, got_ref, half_ref, step_ref, out_ref):
+def face_kernel(live_in, weights_ref, got_ref, half_ref, step_ref, out_ref, live_ref, ready):
+    scalars = fetched([live_in], [live_ref], ready)
     first = lax.axis_index("blk") * BLOCKS
     me = lax.axis_index("inst")
     total = jnp.zeros((FACES * VARS, CELLS), jnp.float32)
     for s in range(INST):
-        total = total + weights_ref[me, s] * got_ref[s, FACE : FACE + FACES * VARS, :]
+        total = total + weights_ref[me, s : s + 1, :] * got_ref[s, FACE : FACE + FACES * VARS, :]
     out_ref[FACES * VARS :, :] = total
+    for copy in scalars:
+        copy.wait()
     for b in range(BLOCKS):
         for side in range(2):
             row = (live_ref[first + b] - 1) if side else 0
@@ -454,9 +458,11 @@
         name="slab", out_specs=[HBM],
     )(live_rows, row_jacobian, cell_jacobian, slabs, viscosity, local_step)
     back = lax.all_to_all(sent, "inst", 0, 0, tiled=True)
-    weights = jnp.array([[spectral(t - s) for s in range(INST)] for t in range(INST)], jnp.float32)
+    table = np.array([[spectral(t - s) for s in range(INST)] for t in range(INST)], np.float32)
+    weights = jnp.asarray(np.repeat(table[:, :, None], CELLS, 2))
     (faces2,) = call(
-        face_kernel, [(2 * FACES * VARS, CELLS)], [SMEM, SMEM, VMEM, VMEM, VMEM], name="faces"
+        face_kernel, [(2 * FACES * VARS, CELLS)], [HBM, VMEM, VMEM, VMEM, VMEM],
+        [LIVE, pltpu.SemaphoreType.DMA((1,))], name="faces"
     )(live_rows, weights, slabs, half_faces, local_step)
     ghosts2 = gathered_over_blocks(faces2, ORDER2)
     (spatial,) = call(

time: 63.8 us -> 63.9 us (level)
  transfers between devices with their start and end apart: 14 -> 14, of which waited for: 8 -> 8; matrix products, arithmetic and copies ran while one was open for 0% -> 0% of each run, Pallas kernels for 10% -> 9%
where the time goes in v6:
time: 63.9 us; the launch traced here: 63.5 us
  starting transfers between devices  27.8 us (44%)
  waiting for transfers between devices  22.4 us (35%)
  Pallas kernels  11.7 us (18%)
  between operations  0.89 us (1%)
  local copies, waits for them, and re-layouts  0.72 us (1%)
    ppermute x12, waiting for transfers between devices, moved(): return lax.ppermute(array, 'blk', pairs)  18.6 us
    ppermute x12, starting transfers between devices, moved(): return lax.ppermute(array, 'blk', pairs)  12.9 us
    all_to_all x1, starting transfers between devices, per_device(): lax.all_to_all(chunks, 'inst', 0, 0, tiled=True).reshape(INST, SENT, CELLS)  9.73 us
    all_to_all x1, starting transfers between devices, per_device(): back = lax.all_to_all(sent, 'inst', 0, 0, tiled=True)  5.26 us
    pallas_call x1, Pallas kernels, per_device(): call(spatial_kernel, [(VARS, BLOCKS, ROWS, CELLS), (FACES * VARS, CELLS),...  4.55 us
    all_to_all x1, waiting for transfers between devices, per_device(): lax.all_to_all(chunks, 'inst', 0, 0, tiled=True).reshape(INST, SENT, CELLS)  3 us
    pallas_call x1, Pallas kernels, per_device(): call(slab_kernel, [(INST, MAIN, CELLS)], [HBM, HBM, HBM, VMEM, VMEM, VMEM...  2.36 us
    pallas_call x1, Pallas kernels, per_device(): call(pack_kernel, [(INST, SENT // SLAB, SLAB, CELLS), (FACES * VARS, CELL...  2.24 us
  transfers between devices with their start and end apart: 14, of which 8 were waited for; matrix products, arithmetic and copies ran while one was open for 0% of the time, Pallas kernels for 9%

profile of v6, /device:TPU:6, one launch (start us, length us, event | category | flops | bytes accessed | tf_op | source)
XLA Modules:
  0.0 63.5 jit_solution(13527913667285963572)
XLA Ops:
  0.6 2.2 %pack.1 = (f32[16,7,16,128]{3,2,1,0:T(8,128)}, f32[20,128]{1,0:T(8,128)}) custom-call(s32[32]{0:T(128)} %live_in.5, f32[1,5,2,128,128]{4,3,2,1,0:T(8,128)} %state_ref.5), custom_call_target="tpu_custom_call" | custom-call | tf_op jit(solution)/shard_map/pack/pallas_call | solution.py:427
  2.9 9.7 %all-to-all-start = ((f32[16,7,16,128]{3,2,1,0:T(8,128)}), f32[16,7,16,128]{3,2,1,0:T(8,128)S(1)}, u32[]{:S(2)}, u32[]{:S(2)}) async-start(f32[16,7,16,128]{3,2,1,0:T(8,128)} %get-tuple-element.11), calls=%async_computation | async-start | bytes 1835008 | tf_op jit(solution)/shard_map/all_to_all | solution.py:437
  12.6 2.1 %collective-permute-start.2 = (f32[1,20,128]{2,1,0:T(8,128)S(1)}, f32[1,20,128]{2,1,0:T(8,128)S(1)}, u32[]{:S(2)}, u32[]{:S(2)}) collective-permute-start(f32[1,20,128]{2,1,0:T(8,128)S(1)} %bitcast.11), channel_id=1, source_target_pairs={{9,0},{8,1},{11,2},{10,3},{13,4},{12,5},{15,6},{14,7},{1,8},{0,9},... | collective-permute-start | bytes 30728 | tf_op jit(solution)/shard_map/ppermute | solution.py:415
  14.8 0.9 %collective-permute-start.1 = (f32[1,20,128]{2,1,0:T(8,128)S(1)}, f32[1,20,128]{2,1,0:T(8,128)S(1)}, u32[]{:S(2)}, u32[]{:S(2)}) collective-permute-start(f32[1,20,128]{2,1,0:T(8,128)S(1)} %bitcast.12), channel_id=1, source_target_pairs={{8,0},{9,1},{10,2},{11,3},{12,4},{13,5},{14,6},{15,7},{0,8},{1,9},... | collective-permute-start | bytes 30728 | tf_op jit(solution)/shard_map/ppermute | solution.py:415
  16.1 1.4 %collective-permute-done.2 = f32[1,20,128]{2,1,0:T(8,128)S(1)} collective-permute-done((f32[1,20,128]{2,1,0:T(8,128)S(1)}, f32[1,20,128]{2,1,0:T(8,128)S(1)}, u32[]{:S(2)}, u32[]{:S(2)}) %collective-permute-start.2) | collective-permute-done | bytes 10272 | tf_op jit(solution)/shard_map/ppermute | solution.py:415
  17.5 2.6 %collective-permute-done.1 = f32[1,20,128]{2,1,0:T(8,128)S(1)} collective-permute-done((f32[1,20,128]{2,1,0:T(8,128)S(1)}, f32[1,20,128]{2,1,0:T(8,128)S(1)}, u32[]{:S(2)}, u32[]{:S(2)}) %collective-permute-start.1) | collective-permute-done | bytes 10272 | tf_op jit(solution)/shard_map/ppermute | solution.py:415
  20.7 2.4 %collective-permute-start.4 = (f32[4,20,128]{2,1,0:T(8,128)S(1)}, f32[4,20,128]{2,1,0:T(8,128)S(1)}, u32[]{:S(2)}, u32[]{:S(2)}) collective-permute-start(f32[4,20,128]{2,1,0:T(8,128)S(1)} %pad_maximum_fusion.1), channel_id=1, source_target_pairs={{4,0},{5,1},{6,2},{7,3},{0,4},{1,5},{2,6},{3,7},{12,8},{13,9},{14,... | collective-permute-start | bytes 122888 | tf_op jit(solution)/shard_map/ppermute | solution.py:415
  23.1 5.3 %collective-permute-done.3 = f32[4,20,128]{2,1,0:T(8,128)S(1)} collective-permute-done((f32[4,20,128]{2,1,0:T(8,128)S(1)}, f32[4,20,128]{2,1,0:T(8,128)S(1)}, u32[]{:S(2)}, u32[]{:S(2)}) %collective-permute-start.3) | collective-permute-done | bytes 40992 | tf_op jit(solution)/shard_map/ppermute | solution.py:415
  28.5 0.6 copy-done.4
  29.1 4.6 %spatial.1 = (f32[5,2,128,128]{3,2,1,0:T(8,128)S(1)}, f32[20,128]{1,0:T(8,128)S(1)}, f32[2,128,128]{2,1,0:T(8,128)S(1)}) custom-call(s32[32]{0:T(128)S(1)} %copy-done.6, s32[64]{0:T(128)S(1)} %copy-done.7, f32[5,5]{1,0:T(8,128)S(1)} %copy-done.4, f32[5,5]{1,0:T(8,128)S(1)} %copy-done.5, f32[1,5,2,128,128]{4,3,2,1,0:T(8,128)S(1)} %copy-done, ...), custom_call_target="tpu_custom_call" | custom-call | tf_op jit(solution)/shard_map/spatial/pallas_call | solution.py:439
  33.7 3.0 %all-to-all-done = f32[16,7,16,128]{3,2,1,0:T(8,128)S(1)} async-done(((f32[16,7,16,128]{3,2,1,0:T(8,128)}), f32[16,7,16,128]{3,2,1,0:T(8,128)S(1)}, u32[]{:S(2)}, u32[]{:S(2)}) %all-to-all-start) | async-done | bytes 917536 | tf_op jit(solution)/shard_map/all_to_all | solution.py:437
  36.7 2.4 %slab.1 = f32[16,80,128]{2,1,0:T(8,128)} custom-call(s32[32]{0:T(128)S(1)} %copy-done.6, f32[5,5]{1,0:T(8,128)S(1)} %copy-done.4, f32[5,5]{1,0:T(8,128)S(1)} %copy-done.5, f32[16,112,128]{2,1,0:T(8,128)S(1)} %bitcast.5, f32[2,128,128]{2,1,0:T(8,128)S(1)} %copy-done.2, f32[2,128,128]{2,1,0:T(8,128)S(1)} %copy-done.1), custom_call_target="tpu_custom_call" | custom-call | tf_op jit(solution)/shard_map/slab/pallas_call | solution.py:447
  39.1 5.3 %all-to-all-start.1 = ((f32[16,80,128]{2,1,0:T(8,128)}), f32[16,80,128]{2,1,0:T(8,128)S(1)}, u32[]{:S(2)}, u32[]{:S(2)}) async-start(f32[16,80,128]{2,1,0:T(8,128)} %slab.1), calls=%async_computation.1 | async-start | bytes 1310720 | tf_op jit(solution)/shard_map/all_to_all | solution.py:460
  44.4 0.6 faces.1
  44.9 1.7 %collective-permute-start.8 = (f32[1,40,128]{2,1,0:T(8,128)S(1)}, f32[1,40,128]{2,1,0:T(8,128)S(1)}, u32[]{:S(2)}, u32[]{:S(2)}) collective-permute-start(f32[1,40,128]{2,1,0:T(8,128)S(1)} %bitcast.7), channel_id=1, source_target_pairs={{9,0},{8,1},{11,2},{10,3},{13,4},{12,5},{15,6},{14,7},{1,8},{0,9},... | collective-permute-start | bytes 61448 | tf_op jit(solution)/shard_map/ppermute | solution.py:415
  46.6 0.9 %collective-permute-start.7 = (f32[1,40,128]{2,1,0:T(8,128)S(1)}, f32[1,40,128]{2,1,0:T(8,128)S(1)}, u32[]{:S(2)}, u32[]{:S(2)}) collective-permute-start(f32[1,40,128]{2,1,0:T(8,128)S(1)} %bitcast.8), channel_id=1, source_target_pairs={{8,0},{9,1},{10,2},{11,3},{12,4},{13,5},{14,6},{15,7},{0,8},{1,9},... | collective-permute-start | bytes 61448 | tf_op jit(solution)/shard_map/ppermute | solution.py:415
  47.5 0.9 %collective-permute-start.6 = (f32[1,40,128]{2,1,0:T(8,128)S(1)}, f32[1,40,128]{2,1,0:T(8,128)S(1)}, u32[]{:S(2)}, u32[]{:S(2)}) collective-permute-start(f32[1,40,128]{2,1,0:T(8,128)S(1)} %bitcast.9), channel_id=1, source_target_pairs={{1,0},{0,1},{3,2},{2,3},{5,4},{4,5},{7,6},{6,7},{9,8},{8,9},{11,10... | collective-permute-start | bytes 61448 | tf_op jit(solution)/shard_map/ppermute | solution.py:415
  48.4 1.8 %collective-permute-done.8 = f32[1,40,128]{2,1,0:T(8,128)S(1)} collective-permute-done((f32[1,40,128]{2,1,0:T(8,128)S(1)}, f32[1,40,128]{2,1,0:T(8,128)S(1)}, u32[]{:S(2)}, u32[]{:S(2)}) %collective-permute-start.8) | collective-permute-done | bytes 20512 | tf_op jit(solution)/shard_map/ppermute | solution.py:415
  50.1 1.9 %collective-permute-done.7 = f32[1,40,128]{2,1,0:T(8,128)S(1)} collective-permute-done((f32[1,40,128]{2,1,0:T(8,128)S(1)}, f32[1,40,128]{2,1,0:T(8,128)S(1)}, u32[]{:S(2)}, u32[]{:S(2)}) %collective-permute-start.7) | collective-permute-done | bytes 20512 | tf_op jit(solution)/shard_map/ppermute | solution.py:415
  52.6 2.4 %collective-permute-start.10 = (f32[4,40,128]{2,1,0:T(8,128)S(1)}, f32[4,40,128]{2,1,0:T(8,128)S(1)}, u32[]{:S(2)}, u32[]{:S(2)}) collective-permute-start(f32[4,40,128]{2,1,0:T(8,128)S(1)} %pad_maximum_fusion), channel_id=1, source_target_pairs={{4,0},{5,1},{6,2},{7,3},{0,4},{1,5},{2,6},{3,7},{12,8},{13,9},{14,... | collective-permute-start | bytes 245768 | tf_op jit(solution)/shard_map/ppermute | solution.py:415
  55.1 5.6 %collective-permute-done.9 = f32[4,40,128]{2,1,0:T(8,128)S(1)} collective-permute-done((f32[4,40,128]{2,1,0:T(8,128)S(1)}, f32[4,40,128]{2,1,0:T(8,128)S(1)}, u32[]{:S(2)}, u32[]{:S(2)}) %collective-permute-start.9) | collective-permute-done | bytes 81952 | tf_op jit(solution)/shard_map/ppermute | solution.py:415
  60.8 0.8 %ghosts.1.spatial_ref = f32[5,2,128,128]{3,2,1,0:T(8,128)S(1)} custom-call(s32[32]{0:T(128)S(1)} %copy-done.6, s32[64]{0:T(128)S(1)} %copy-done.7, f32[5,5]{1,0:T(8,128)S(1)} %copy-done.4, f32[2,128,128]{2,1,0:T(8,128)S(1)} %copy-done.2, f32[2,128,128]{2,1,0:T(8,128)S(1)} %copy-done.1, ...), custom_call_target="tpu_custom_call", output_to_operand_aliasing={{}: (6, {})} | custom-call | tf_op jit(solution)/shard_map/ghosts/pallas_call | solution.py:468
  61.6 0.8 %all-to-all-done.1.got_ref = f32[16,80,128]{2,1,0:T(8,128)S(1)} async-done(((f32[16,80,128]{2,1,0:T(8,128)}), f32[16,80,128]{2,1,0:T(8,128)S(1)}, u32[]{:S(2)}, u32[]{:S(2)}) %all-to-all-start.1) | async-done | bytes 655392 | tf_op jit(solution)/shard_map/all_to_all | solution.py:460
  62.4 1.2 %final.1 = (f32[1,5,2,128,128]{4,3,2,1,0:T(8,128)}, f32[1,5,2,128,128]{4,3,2,1,0:T(8,128)}) custom-call(f32[1,5,2,128,128]{4,3,2,1,0:T(8,128)S(1)} %copy-done, f32[2,128,128]{2,1,0:T(8,128)S(1)} %copy-done.1, f32[2,128,128]{2,1,0:T(8,128)S(1)} %get-tuple-element.10.mask_ref, f32[5,2,128,128]{3,2,1,0:T(8,128)S(1)} %ghosts.1.spatial_ref, ...), custom_call_target="tpu_custom_call" | custom-call | tf_op jit(solution)/shard_map/final/pallas_call | solution.py:471
  (44 shorter events, 1.6 us)
Async XLA Ops:
  2.9 9.8 %copy-start.8 = (f32[20,128]{1,0:T(8,128)S(1)}, f32[20,128]{1,0:T(8,128)}, u32[]{:S(2)}) copy-start(f32[20,128]{1,0:T(8,128)} %get-tuple-element.9) | copy-start | bytes 30724
  2.9 25.6 %copy-start = (f32[1,5,2,128,128]{4,3,2,1,0:T(8,128)S(1)}, f32[1,5,2,128,128]{4,3,2,1,0:T(8,128)}, u32[]{:S(2)}) copy-start(f32[1,5,2,128,128]{4,3,2,1,0:T(8,128)} %state_ref.5) | copy-start | bytes 1966084
  2.9 33.8 %all-to-all-start = ((f32[16,7,16,128]{3,2,1,0:T(8,128)}), f32[16,7,16,128]{3,2,1,0:T(8,128)S(1)}, u32[]{:S(2)}, u32[]{:S(2)}) async-start(f32[16,7,16,128]{3,2,1,0:T(8,128)} %get-tuple-element.11), calls=%async_computation | async-start | bytes 1835008 | tf_op jit(solution)/shard_map/all_to_all | solution.py:437
  12.6 4.8 %collective-permute-start.2 = (f32[1,20,128]{2,1,0:T(8,128)S(1)}, f32[1,20,128]{2,1,0:T(8,128)S(1)}, u32[]{:S(2)}, u32[]{:S(2)}) collective-permute-start(f32[1,20,128]{2,1,0:T(8,128)S(1)} %bitcast.11), channel_id=1, source_target_pairs={{9,0},{8,1},{11,2},{10,3},{13,4},{12,5},{15,6},{14,7},{1,8},{0,9},... | collective-permute-start | bytes 30728 | tf_op jit(solution)/shard_map/ppermute | solution.py:415
  14.8 5.3 %collective-permute-start.1 = (f32[1,20,128]{2,1,0:T(8,128)S(1)}, f32[1,20,128]{2,1,0:T(8,128)S(1)}, u32[]{:S(2)}, u32[]{:S(2)}) collective-permute-start(f32[1,20,128]{2,1,0:T(8,128)S(1)} %bitcast.12), channel_id=1, source_target_pairs={{8,0},{9,1},{10,2},{11,3},{12,4},{13,5},{14,6},{15,7},{0,8},{1,9},... | collective-permute-start | bytes 30728 | tf_op jit(solution)/shard_map/ppermute | solution.py:415
  15.7 4.4 %collective-permute-start = (f32[1,20,128]{2,1,0:T(8,128)S(1)}, f32[1,20,128]{2,1,0:T(8,128)S(1)}, u32[]{:S(2)}, u32[]{:S(2)}) collective-permute-start(f32[1,20,128]{2,1,0:T(8,128)S(1)} %bitcast.13), channel_id=1, source_target_pairs={{1,0},{0,1},{3,2},{2,3},{5,4},{4,5},{7,6},{6,7},{9,8},{8,9},{11,10... | collective-permute-start | bytes 30728 | tf_op jit(solution)/shard_map/ppermute | solution.py:415
  20.1 8.4 %collective-permute-start.5 = (f32[4,20,128]{2,1,0:T(8,128)S(1)}, f32[4,20,128]{2,1,0:T(8,128)S(1)}, u32[]{:S(2)}, u32[]{:S(2)}) collective-permute-start(f32[4,20,128]{2,1,0:T(8,128)S(1)} %pad_maximum_fusion.1), channel_id=1, source_target_pairs={{6,0},{7,1},{0,2},{1,3},{2,4},{3,5},{4,6},{5,7},{14,8},{15,9},{8,1... | collective-permute-start | bytes 122888 | tf_op jit(solution)/shard_map/ppermute | solution.py:415
  20.7 7.7 %collective-permute-start.4 = (f32[4,20,128]{2,1,0:T(8,128)S(1)}, f32[4,20,128]{2,1,0:T(8,128)S(1)}, u32[]{:S(2)}, u32[]{:S(2)}) collective-permute-start(f32[4,20,128]{2,1,0:T(8,128)S(1)} %pad_maximum_fusion.1), channel_id=1, source_target_pairs={{4,0},{5,1},{6,2},{7,3},{0,4},{1,5},{2,6},{3,7},{12,8},{13,9},{14,... | collective-permute-start | bytes 122888 | tf_op jit(solution)/shard_map/ppermute | solution.py:415
  23.1 5.3 %collective-permute-start.3 = (f32[4,20,128]{2,1,0:T(8,128)S(1)}, f32[4,20,128]{2,1,0:T(8,128)S(1)}, u32[]{:S(2)}, u32[]{:S(2)}) collective-permute-start(f32[4,20,128]{2,1,0:T(8,128)S(1)} %pad_maximum_fusion.1), channel_id=1, source_target_pairs={{2,0},{3,1},{4,2},{5,3},{6,4},{7,5},{0,6},{1,7},{10,8},{11,9},{12,... | collective-permute-start | bytes 122888 | tf_op jit(solution)/shard_map/ppermute | solution.py:415
  23.1 5.4 %copy-start.1 = (f32[2,128,128]{2,1,0:T(8,128)S(1)}, f32[2,128,128]{2,1,0:T(8,128)}, u32[]{:S(2)}) copy-start(f32[2,128,128]{2,1,0:T(8,128)} %step_ref.9) | copy-start | bytes 393220
  23.1 5.4 %copy-start.2 = (f32[2,128,128]{2,1,0:T(8,128)S(1)}, f32[2,128,128]{2,1,0:T(8,128)}, u32[]{:S(2)}) copy-start(f32[2,128,128]{2,1,0:T(8,128)} %visc_ref.5) | copy-start | bytes 393220
  28.4 0.7 %copy-start.4 = (f32[5,5]{1,0:T(8,128)S(1)}, f32[5,5]{1,0:T(8,128)}, u32[]{:S(2)}) copy-start(f32[5,5]{1,0:T(8,128)} %row_in.1) | copy-start | bytes 304
  28.4 0.7 %copy-start.5 = (f32[5,5]{1,0:T(8,128)S(1)}, f32[5,5]{1,0:T(8,128)}, u32[]{:S(2)}) copy-start(f32[5,5]{1,0:T(8,128)} %cell_in.1) | copy-start | bytes 304
  28.4 0.7 %copy-start.6 = (s32[32]{0:T(128)S(1)}, s32[32]{0:T(128)}, u32[]{:S(2)}) copy-start(s32[32]{0:T(128)} %live_in.5) | copy-start | bytes 388
  28.5 0.7 %copy-start.7 = (s32[64]{0:T(128)S(1)}, s32[64]{0:T(128)}, u32[]{:S(2)}) copy-start(s32[64]{0:T(128)} %partner_ref.3) | copy-start | bytes 772
  39.1 5.3 %copy-start.3 = (f32[16,16,128]{2,1,0:T(8,128)S(1)}, f32[16,16,128]{2,1,0:T(8,128)}, u32[]{:S(2)}) copy-start(f32[16,16,128]{2,1,0:T(8,128)} %constant.2.clone.weights_ref) | copy-start | bytes 393220
  39.1 23.3 %all-to-all-start.1 = ((f32[16,80,128]{2,1,0:T(8,128)}), f32[16,80,128]{2,1,0:T(8,128)S(1)}, u32[]{:S(2)}, u32[]{:S(2)}) async-start(f32[16,80,128]{2,1,0:T(8,128)} %slab.1), calls=%async_computation.1 | async-start | bytes 1310720 | tf_op jit(solution)/shard_map/all_to_all | solution.py:460
  44.9 5.2 %collective-permute-start.8 = (f32[1,40,128]{2,1,0:T(8,128)S(1)}, f32[1,40,128]{2,1,0:T(8,128)S(1)}, u32[]{:S(2)}, u32[]{:S(2)}) collective-permute-start(f32[1,40,128]{2,1,0:T(8,128)S(1)} %bitcast.7), channel_id=1, source_target_pairs={{9,0},{8,1},{11,2},{10,3},{13,4},{12,5},{15,6},{14,7},{1,8},{0,9},... | collective-permute-start | bytes 61448 | tf_op jit(solution)/shard_map/ppermute | solution.py:415
  46.6 5.4 %collective-permute-start.7 = (f32[1,40,128]{2,1,0:T(8,128)S(1)}, f32[1,40,128]{2,1,0:T(8,128)S(1)}, u32[]{:S(2)}, u32[]{:S(2)}) collective-permute-start(f32[1,40,128]{2,1,0:T(8,128)S(1)} %bitcast.8), channel_id=1, source_target_pairs={{8,0},{9,1},{10,2},{11,3},{12,4},{13,5},{14,6},{15,7},{0,8},{1,9},... | collective-permute-start | bytes 61448 | tf_op jit(solution)/shard_map/ppermute | solution.py:415
  47.5 4.6 %collective-permute-start.6 = (f32[1,40,128]{2,1,0:T(8,128)S(1)}, f32[1,40,128]{2,1,0:T(8,128)S(1)}, u32[]{:S(2)}, u32[]{:S(2)}) collective-permute-start(f32[1,40,128]{2,1,0:T(8,128)S(1)} %bitcast.9), channel_id=1, source_target_pairs={{1,0},{0,1},{3,2},{2,3},{5,4},{4,5},{7,6},{6,7},{9,8},{8,9},{11,10... | collective-permute-start | bytes 61448 | tf_op jit(solution)/shard_map/ppermute | solution.py:415
  52.1 8.7 %collective-permute-start.11 = (f32[4,40,128]{2,1,0:T(8,128)S(1)}, f32[4,40,128]{2,1,0:T(8,128)S(1)}, u32[]{:S(2)}, u32[]{:S(2)}) collective-permute-start(f32[4,40,128]{2,1,0:T(8,128)S(1)} %pad_maximum_fusion), channel_id=1, source_target_pairs={{6,0},{7,1},{0,2},{1,3},{2,4},{3,5},{4,6},{5,7},{14,8},{15,9},{8,1... | collective-permute-start | bytes 245768 | tf_op jit(solution)/shard_map/ppermute | solution.py:415
  52.6 8.1 %collective-permute-start.10 = (f32[4,40,128]{2,1,0:T(8,128)S(1)}, f32[4,40,128]{2,1,0:T(8,128)S(1)}, u32[]{:S(2)}, u32[]{:S(2)}) collective-permute-start(f32[4,40,128]{2,1,0:T(8,128)S(1)} %pad_maximum_fusion), channel_id=1, source_target_pairs={{4,0},{5,1},{6,2},{7,3},{0,4},{1,5},{2,6},{3,7},{12,8},{13,9},{14,... | collective-permute-start | bytes 245768 | tf_op jit(solution)/shard_map/ppermute | solution.py:415
  55.0 5.7 %collective-permute-start.9 = (f32[4,40,128]{2,1,0:T(8,128)S(1)}, f32[4,40,128]{2,1,0:T(8,128)S(1)}, u32[]{:S(2)}, u32[]{:S(2)}) collective-permute-start(f32[4,40,128]{2,1,0:T(8,128)S(1)} %pad_maximum_fusion), channel_id=1, source_target_pairs={{2,0},{3,1},{4,2},{5,3},{6,4},{7,5},{0,6},{1,7},{10,8},{11,9},{12,... | collective-permute-start | bytes 245768 | tf_op jit(solution)/shard_map/ppermute | solution.py:415
